TPU v7x, 32 devices: a whole 2x2x4 slice. The times are simulated.
32 devices in a mesh: rep: 4 (over z), shard: 8 (over y, x, core).
Axes of the slice: x: 2, y: 2, z: 4, core: 2. Of those that a mesh axis runs over, the one named last changes fastest.
Arguments:
- query_tokens: bfloat16 [128, 32, 768], P(('rep', 'shard')), may hold values from -6 to 6
- passage_tokens: bfloat16 [32, 256, 768], P(('rep', 'shard')), may hold values from -6 to 6
- query_cot: bfloat16 [128, 32, 768], P(('rep', 'shard')), may hold values from -4 to 4
- passage_cot: bfloat16 [32, 256, 768], P(('rep', 'shard')), may hold values from -4 to 4
- bucket_counts: int32 [32], replicated, may hold values from 0 to 1, as said below
- positives: int32 [128], P(('rep', 'shard')), may hold values from 0 to 127, as said below
- qkv_weight: bfloat16 [2, 768, 2304], P(None, 'shard'), may hold values from -0.21875 to 0.21875
- qv_bias: bfloat16 [2, 1536], P(None, 'shard'), may hold values from -3 to 3
- out_weight: bfloat16 [2, 768, 768], P(None, 'shard'), may hold values from -1.75 to 1.75
- out_bias: bfloat16 [2, 768], P(None, 'shard'), may hold values from -2 to 2
- up_weight: bfloat16 [2, 768, 3072], P(None, 'shard'), may hold values from -0.21875 to 0.21875
- up_bias: bfloat16 [2, 3072], P(None, 'shard'), may hold values from -2 to 2
- down_weight: bfloat16 [2, 3072, 768], P(None, 'shard'), may hold values from -0.109375 to 0.109375
- down_bias: bfloat16 [2, 768], P(None, 'shard'), may hold values from -2 to 2
- norm_gains: bfloat16 [2, 2, 768], P(None, None, 'shard'), may hold values from 0.5 to 1.5
- norm_shifts: bfloat16 [2, 2, 768], P(None, None, 'shard'), may hold values from -2 to 2
Outputs:
- loss: float32 [], replicated
- query_out: bfloat16 [128, 32, 768], P(('rep', 'shard'))
- passage_out: bfloat16 [32, 256, 768], P(('rep', 'shard'))
- query_grad: bfloat16 [128, 32, 768], P(('rep', 'shard'))
- passage_grad: bfloat16 [32, 256, 768], P(('rep', 'shard'))
- qkv_weight_grad: float32 [2, 768, 2304], P(None, 'shard')
- qv_bias_grad: float32 [2, 1536], P(None, 'shard')
- out_weight_grad: float32 [2, 768, 768], P(None, 'shard')
- out_bias_grad: float32 [2, 768], P(None, 'shard')
- up_weight_grad: float32 [2, 768, 3072], P(None, 'shard')
- up_bias_grad: float32 [2, 3072], P(None, 'shard')
- down_weight_grad: float32 [2, 3072, 768], P(None, 'shard')
- down_bias_grad: float32 [2, 768], P(None, 'shard')
- norm_gains_grad: float32 [2, 2, 768], P(None, None, 'shard')
- norm_shifts_grad: float32 [2, 2, 768], P(None, None, 'shard')
Inputs may be any that keep to these rules, and one draw needn't show every extreme that they name: `bucket_counts`: each device's number of long-passage blocks (its first blocks); some device has 1 and some has 0; the last device has fewer than 1. `positives`: a valid slot d * 4 + b * 4 + s: s is 0 where block b of device d holds one long passage; the last query's positive is the last slot.
All inputs are finite; a program needn't handle non-finite values.
Results may differ from a plain program's by a relative error of at most 0.015.
Values may be sent and summed in bfloat16 or wider, within the bound.
A program may use at most 192 MiB of HBM per device.

v0:
```python
import math

import jax
import jax.numpy as jnp
from jax import lax
from jax.sharding import PartitionSpec as P

HD = 64
SHORT = 64


LN_EPS = 1e-05
NEG_FILL = -1e30
INV_ROOT_TWO = 0.7071067811865476
INV_ROOT_TWO_PI = 0.3989422804014327


def for_sending(array):
    return jax.tree.map(lambda a: a.astype(jnp.bfloat16) if a.dtype == jnp.float32 else a, array)


def pick_tower(stacks, tower_index):
    qkv_w, qv_b, out_w, out_b, up_w, up_b, down_w, down_b, gains, shifts = stacks
    return (
        qkv_w[tower_index],
        qv_b[tower_index],
        out_w[tower_index],
        out_b[tower_index],
        up_w[tower_index],
        up_b[tower_index],
        down_w[tower_index],
        down_b[tower_index],
        gains[tower_index].T,
        shifts[tower_index].T,
    )


def fetch_layer(stacks, tower_index):
    return lax.all_gather(for_sending(pick_tower(stacks, tower_index)), "shard", axis=0, tiled=True)


def fetch_again(stacks, tower_index):
    return lax.all_gather(for_sending(pick_tower(stacks, tower_index)), "shard", axis=0, tiled=True)


def normalize(hidden):
    row_mean = jnp.mean(hidden, axis=-1, keepdims=True)
    centred = hidden - row_mean
    inv_std = lax.rsqrt(jnp.mean(centred * centred, axis=-1, keepdims=True) + LN_EPS)
    return (centred * inv_std, inv_std)


def norm_back(grad_in, normed, inv_std):
    return inv_std * (
        grad_in
        - jnp.mean(grad_in, axis=-1, keepdims=True)
        - normed * jnp.mean(grad_in * normed, axis=-1, keepdims=True)
    )


def block_mask(long_flags, length, short_len):
    row_part = lax.broadcasted_iota(jnp.int32, (length, length), 0) // short_len
    col_part = lax.broadcasted_iota(jnp.int32, (length, length), 1) // short_len
    return long_flags[:, None, None] | (row_part == col_part)[None]


def head_scores(head_query, head_key, attn_mask):
    raw_scores = jnp.einsum(
        "slhd,smhd->shlm", head_query, head_key, preferred_element_type=jnp.float32
    ) * (1.0 / math.sqrt(HD))
    return jnp.where(attn_mask[:, None], raw_scores, NEG_FILL)


def layer_forward(tokens, weights, attn_mask):
    qkv_w, qv_b, out_w, out_b, up_w, up_b, down_w, down_b, gains, shifts = weights
    seq_count, length, model_width = tokens.shape
    head_count = model_width // HD
    token_rows = tokens.reshape(seq_count * length, model_width)
    qv_float = qv_b.astype(jnp.float32)
    qkv_bias = jnp.concatenate(
        [qv_float[:model_width], jnp.zeros((model_width,), jnp.float32), qv_float[model_width:]]
    )
    qkv_low = (jnp.dot(token_rows, qkv_w, preferred_element_type=jnp.float32) + qkv_bias).astype(
        jnp.bfloat16
    )
    head_split = qkv_low.reshape(seq_count, length, 3, head_count, HD)
    scores = head_scores(head_split[:, :, 0], head_split[:, :, 1], attn_mask)
    row_max = jnp.max(scores, axis=-1, keepdims=True)
    exp_scores = jnp.exp(scores - row_max)
    row_total = jnp.sum(exp_scores, axis=-1, keepdims=True)
    attn_probs = (exp_scores / row_total).astype(jnp.bfloat16)
    log_total = row_max + jnp.log(row_total)
    attn_mixed = jnp.einsum(
        "shlm,smhd->slhd", attn_probs, head_split[:, :, 2], preferred_element_type=jnp.float32
    )
    attn_low = attn_mixed.reshape(seq_count * length, model_width).astype(jnp.bfloat16)
    first_sum = (
        token_rows.astype(jnp.float32)
        + jnp.dot(attn_low, out_w, preferred_element_type=jnp.float32)
        + out_b.astype(jnp.float32)
    )
    normed_one, inv_one = normalize(first_sum)
    gain_float = gains.astype(jnp.float32)
    shift_float = shifts.astype(jnp.float32)
    middle = normed_one * gain_float[:, 0] + shift_float[:, 0]
    middle_low = middle.astype(jnp.bfloat16)
    pre_act = jnp.dot(middle_low, up_w, preferred_element_type=jnp.float32) + up_b.astype(
        jnp.float32
    )
    act_low = jax.nn.gelu(pre_act, approximate=False).astype(jnp.bfloat16)
    second = (
        middle
        + jnp.dot(act_low, down_w, preferred_element_type=jnp.float32)
        + down_b.astype(jnp.float32)
    )
    normed_two, inv_two = normalize(second)
    result = normed_two * gain_float[:, 1] + shift_float[:, 1]
    kept = (
        token_rows,
        qkv_low,
        log_total,
        attn_low,
        normed_one,
        inv_one,
        middle_low,
        pre_act,
        act_low,
        normed_two,
        inv_two,
    )
    return (result, kept)


def layer_backward(grad_out, weights, kept, attn_mask):
    qkv_w, qv_b, out_w, out_b, up_w, up_b, down_w, down_b, gains, shifts = weights
    (
        token_rows,
        qkv_low,
        log_total,
        attn_low,
        normed_one,
        inv_one,
        middle_low,
        pre_act,
        act_low,
        normed_two,
        inv_two,
    ) = kept
    seq_count = attn_mask.shape[0]
    model_width = token_rows.shape[1]
    length = token_rows.shape[0] // seq_count
    head_count = model_width // HD
    gain_float = gains.astype(jnp.float32)
    gain_two = jnp.sum(grad_out * normed_two, axis=0)
    shift_two = jnp.sum(grad_out, axis=0)
    d_second = norm_back(grad_out * gain_float[:, 1], normed_two, inv_two)
    d_ffn = d_second.astype(jnp.bfloat16)
    d_down_w = jnp.dot(act_low.T, d_ffn, preferred_element_type=jnp.float32)
    d_down_b = jnp.sum(d_ffn.astype(jnp.float32), axis=0)
    d_act = jnp.dot(d_ffn, down_w.T, preferred_element_type=jnp.float32)
    gelu_slope = (
        0.5 * (1.0 + lax.erf(pre_act * INV_ROOT_TWO))
        + pre_act * jnp.exp(-0.5 * pre_act * pre_act) * INV_ROOT_TWO_PI
    )
    d_pre = (d_act * gelu_slope).astype(jnp.bfloat16)
    d_up_w = jnp.dot(middle_low.T, d_pre, preferred_element_type=jnp.float32)
    d_up_b = jnp.sum(d_pre.astype(jnp.float32), axis=0)
    d_middle = d_second + jnp.dot(d_pre, up_w.T, preferred_element_type=jnp.float32)
    gain_one = jnp.sum(d_middle * normed_one, axis=0)
    shift_one = jnp.sum(d_middle, axis=0)
    d_first = norm_back(d_middle * gain_float[:, 0], normed_one, inv_one)
    d_attn_out = d_first.astype(jnp.bfloat16)
    d_out_w = jnp.dot(attn_low.T, d_attn_out, preferred_element_type=jnp.float32)
    d_out_b = jnp.sum(d_attn_out.astype(jnp.float32), axis=0)
    d_mixed = (
        jnp.dot(d_attn_out, out_w.T, preferred_element_type=jnp.float32)
        .astype(jnp.bfloat16)
        .reshape(seq_count, length, head_count, HD)
    )
    head_split = qkv_low.reshape(seq_count, length, 3, head_count, HD)
    head_query = head_split[:, :, 0]
    head_key = head_split[:, :, 1]
    head_value = head_split[:, :, 2]
    attn_probs = jnp.exp(head_scores(head_query, head_key, attn_mask) - log_total)
    d_probs = jnp.einsum("slhd,smhd->shlm", d_mixed, head_value, preferred_element_type=jnp.float32)
    d_value = jnp.einsum(
        "shlm,slhd->smhd",
        attn_probs.astype(jnp.bfloat16),
        d_mixed,
        preferred_element_type=jnp.float32,
    )
    d_scores = (
        attn_probs * (d_probs - jnp.sum(d_probs * attn_probs, axis=-1, keepdims=True))
    ).astype(jnp.bfloat16)
    d_query = jnp.einsum(
        "shlm,smhd->slhd", d_scores, head_key, preferred_element_type=jnp.float32
    ) * (1.0 / math.sqrt(HD))
    d_key = jnp.einsum(
        "shlm,slhd->smhd", d_scores, head_query, preferred_element_type=jnp.float32
    ) * (1.0 / math.sqrt(HD))
    d_qkv = (
        jnp.stack([d_query, d_key, d_value], axis=2)
        .reshape(seq_count * length, 3 * model_width)
        .astype(jnp.bfloat16)
    )
    d_qkv_w = jnp.dot(token_rows.T, d_qkv, preferred_element_type=jnp.float32)
    column_sums = jnp.sum(d_qkv.astype(jnp.float32), axis=0)
    d_qv_b = jnp.concatenate([column_sums[:model_width], column_sums[2 * model_width :]])
    d_tokens = d_first + jnp.dot(d_qkv, qkv_w.T, preferred_element_type=jnp.float32)
    layer_grads = (
        d_qkv_w,
        d_qv_b,
        d_out_w,
        d_out_b,
        d_up_w,
        d_up_b,
        d_down_w,
        d_down_b,
        jnp.stack([gain_one, gain_two], axis=1),
        jnp.stack([shift_one, shift_two], axis=1),
    )
    return (d_tokens, layer_grads)


def reduce_layer(layer_grads):
    owned_grads = (
        lax.psum_scatter(layer_grads[0], "shard", scatter_dimension=0, tiled=True),
        lax.psum_scatter(layer_grads[1], "shard", scatter_dimension=0, tiled=True),
        lax.psum_scatter(layer_grads[2], "shard", scatter_dimension=0, tiled=True),
        lax.psum_scatter(layer_grads[3], "shard", scatter_dimension=0, tiled=True),
        lax.psum_scatter(layer_grads[4], "shard", scatter_dimension=0, tiled=True),
        lax.psum_scatter(layer_grads[5], "shard", scatter_dimension=0, tiled=True),
        lax.psum_scatter(layer_grads[6], "shard", scatter_dimension=0, tiled=True),
        lax.psum_scatter(layer_grads[7], "shard", scatter_dimension=0, tiled=True),
        lax.psum_scatter(layer_grads[8], "shard", scatter_dimension=0, tiled=True),
        lax.psum_scatter(layer_grads[9], "shard", scatter_dimension=0, tiled=True),
    )
    quarter = (
        lax.psum_scatter(
            owned_grads[0].astype(jnp.bfloat16), "rep", scatter_dimension=0, tiled=True
        ).astype(jnp.float32),
        lax.psum_scatter(
            owned_grads[1].astype(jnp.bfloat16), "rep", scatter_dimension=0, tiled=True
        ).astype(jnp.float32),
        lax.psum_scatter(
            owned_grads[2].astype(jnp.bfloat16), "rep", scatter_dimension=0, tiled=True
        ).astype(jnp.float32),
        lax.psum_scatter(
            owned_grads[3].astype(jnp.bfloat16), "rep", scatter_dimension=0, tiled=True
        ).astype(jnp.float32),
        lax.psum_scatter(
            owned_grads[4].astype(jnp.bfloat16), "rep", scatter_dimension=0, tiled=True
        ).astype(jnp.float32),
        lax.psum_scatter(
            owned_grads[5].astype(jnp.bfloat16), "rep", scatter_dimension=0, tiled=True
        ).astype(jnp.float32),
        lax.psum_scatter(
            owned_grads[6].astype(jnp.bfloat16), "rep", scatter_dimension=0, tiled=True
        ).astype(jnp.float32),
        lax.psum_scatter(
            owned_grads[7].astype(jnp.bfloat16), "rep", scatter_dimension=0, tiled=True
        ).astype(jnp.float32),
        lax.psum_scatter(
            owned_grads[8].astype(jnp.bfloat16), "rep", scatter_dimension=0, tiled=True
        ).astype(jnp.float32),
        lax.psum_scatter(
            owned_grads[9].astype(jnp.bfloat16), "rep", scatter_dimension=0, tiled=True
        ).astype(jnp.float32),
    )
    return (
        lax.all_gather(quarter[0].astype(jnp.bfloat16), "rep", axis=0, tiled=True).astype(
            jnp.float32
        ),
        lax.all_gather(quarter[1].astype(jnp.bfloat16), "rep", axis=0, tiled=True).astype(
            jnp.float32
        ),
        lax.all_gather(quarter[2].astype(jnp.bfloat16), "rep", axis=0, tiled=True).astype(
            jnp.float32
        ),
        lax.all_gather(quarter[3].astype(jnp.bfloat16), "rep", axis=0, tiled=True).astype(
            jnp.float32
        ),
        lax.all_gather(quarter[4].astype(jnp.bfloat16), "rep", axis=0, tiled=True).astype(
            jnp.float32
        ),
        lax.all_gather(quarter[5].astype(jnp.bfloat16), "rep", axis=0, tiled=True).astype(
            jnp.float32
        ),
        lax.all_gather(quarter[6].astype(jnp.bfloat16), "rep", axis=0, tiled=True).astype(
            jnp.float32
        ),
        lax.all_gather(quarter[7].astype(jnp.bfloat16), "rep", axis=0, tiled=True).astype(
            jnp.float32
        ),
        lax.all_gather(quarter[8].astype(jnp.bfloat16), "rep", axis=0, tiled=True).astype(
            jnp.float32
        ),
        lax.all_gather(quarter[9].astype(jnp.bfloat16), "rep", axis=0, tiled=True).astype(
            jnp.float32
        ),
    )


def local(
    query_tokens,
    passage_tokens,
    query_cot,
    passage_cot,
    bucket_counts,
    positives,
    qkv_weight,
    qv_bias,
    out_weight,
    out_bias,
    up_weight,
    up_bias,
    down_weight,
    down_bias,
    norm_gains,
    norm_shifts,
):
    stacks = (
        qkv_weight,
        qv_bias,
        out_weight,
        out_bias,
        up_weight,
        up_bias,
        down_weight,
        down_bias,
        norm_gains,
        norm_shifts,
    )
    blocks, long_len, model_width = passage_tokens.shape
    query_count, query_len, unused_width = query_tokens.shape
    subs_count = long_len // SHORT
    slot_count = blocks * subs_count
    my_index = lax.axis_index(("rep", "shard"))
    own_count = lax.dynamic_index_in_dim(bucket_counts, my_index, 0, keepdims=False)
    passage_mask = block_mask(lax.iota(jnp.int32, blocks) < own_count, long_len, SHORT)
    query_mask = block_mask(jnp.ones((query_count,), dtype=bool), query_len, query_len)
    query_weights = fetch_layer(stacks, 0)
    query_result, query_kept = layer_forward(query_tokens, query_weights, query_mask)
    passage_weights = fetch_layer(stacks, 1)
    passage_result, passage_kept = layer_forward(passage_tokens, passage_weights, passage_mask)
    query_cls = query_result.reshape(query_count, query_len, model_width)[:, 0].astype(jnp.bfloat16)
    passage_cls = (
        passage_result.reshape(blocks, subs_count, SHORT, model_width)[:, :, 0]
        .reshape(slot_count, model_width)
        .astype(jnp.bfloat16)
    )
    every_cls = lax.all_gather(passage_cls, ("rep", "shard"), axis=0, tiled=True)
    cand_count = every_cls.shape[0]
    device_count = bucket_counts.shape[0]
    score_scale = 2.0 / math.sqrt(model_width)
    logits = jnp.dot(query_cls, every_cls.T, preferred_element_type=jnp.float32) * score_scale
    slot_ids = lax.iota(jnp.int32, cand_count)
    owner_index = slot_ids // slot_count
    owner_counts = jnp.sum(
        jnp.where(
            owner_index[:, None] == lax.iota(jnp.int32, device_count)[None], bucket_counts[None], 0
        ),
        axis=1,
    )
    slot_valid = (slot_ids % slot_count // subs_count >= owner_counts) | (
        slot_ids % subs_count == 0
    )
    masked = jnp.where(slot_valid[None], logits, NEG_FILL)
    row_max = jnp.max(masked, axis=1, keepdims=True)
    exp_scores = jnp.exp(masked - row_max)
    row_total = jnp.sum(exp_scores, axis=1, keepdims=True)
    log_total = row_max[:, 0] + jnp.log(row_total[:, 0])
    hit_mask = slot_ids[None] == positives[:, None]
    picked = jnp.sum(jnp.where(hit_mask, masked, 0.0), axis=1)
    local_loss = jnp.sum(log_total - picked)
    d_logits = (exp_scores / row_total - hit_mask.astype(jnp.float32)).astype(jnp.bfloat16)
    d_query_cls = jnp.dot(d_logits, every_cls, preferred_element_type=jnp.float32) * score_scale
    d_cands = (
        lax.dot_general(
            d_logits, query_cls, (((0,), (0,)), ((), ())), preferred_element_type=jnp.float32
        )
        * score_scale
    )
    d_passage_cls = lax.psum_scatter(d_cands, ("rep", "shard"), scatter_dimension=0, tiled=True)
    loss_sum = lax.psum(local_loss, ("rep", "shard"))
    loss = loss_sum / (query_count * lax.axis_size(("rep", "shard")))
    query_dout = (
        query_cot.astype(jnp.float32)
        .at[:, 0]
        .add(d_query_cls)
        .reshape(query_count * query_len, model_width)
    )
    passage_dout = (
        passage_cot.astype(jnp.float32)
        .reshape(blocks, subs_count, SHORT, model_width)
        .at[:, :, 0]
        .add(d_passage_cls.reshape(blocks, subs_count, model_width))
        .reshape(blocks * long_len, model_width)
    )
    passage_back = fetch_again(stacks, 1)
    passage_dx, passage_grads = layer_backward(
        passage_dout, passage_back, passage_kept, passage_mask
    )
    passage_owned = reduce_layer(passage_grads)
    query_back = fetch_again(stacks, 0)
    query_dx, query_grads = layer_backward(query_dout, query_back, query_kept, query_mask)
    query_owned = reduce_layer(query_grads)
    stacked = [
        jnp.stack([first_g, second_g]) for first_g, second_g in zip(query_owned, passage_owned)
    ]
    gains_grad = jnp.swapaxes(stacked[8], 1, 2)
    shifts_grad = jnp.swapaxes(stacked[9], 1, 2)
    return (
        loss,
        query_result.reshape(query_count, query_len, model_width).astype(jnp.bfloat16),
        passage_result.reshape(blocks, long_len, model_width).astype(jnp.bfloat16),
        query_dx.reshape(query_count, query_len, model_width).astype(jnp.bfloat16),
        passage_dx.reshape(blocks, long_len, model_width).astype(jnp.bfloat16),
        stacked[0],
        stacked[1],
        stacked[2],
        stacked[3],
        stacked[4],
        stacked[5],
        stacked[6],
        stacked[7],
        gains_grad,
        shifts_grad,
    )


def solution(mesh):
    in_specs = (
        P(("rep", "shard"), None, None),
        P(("rep", "shard"), None, None),
        P(("rep", "shard"), None, None),
        P(("rep", "shard"), None, None),
        P(),
        P(("rep", "shard")),
        P(None, "shard", None),
        P(None, "shard"),
        P(None, "shard", None),
        P(None, "shard"),
        P(None, "shard", None),
        P(None, "shard"),
        P(None, "shard", None),
        P(None, "shard"),
        P(None, None, "shard"),
        P(None, None, "shard"),
    )
    out_specs = (
        P(),
        P(("rep", "shard"), None, None),
        P(("rep", "shard"), None, None),
        P(("rep", "shard"), None, None),
        P(("rep", "shard"), None, None),
        P(None, "shard", None),
        P(None, "shard"),
        P(None, "shard", None),
        P(None, "shard"),
        P(None, "shard", None),
        P(None, "shard"),
        P(None, "shard", None),
        P(None, "shard"),
        P(None, None, "shard"),
        P(None, None, "shard"),
    )
    return jax.shard_map(local, mesh=mesh, in_specs=in_specs, out_specs=out_specs, check_vma=False)
```

profile of v0, /device:TPU:0, one launch (start us, length us, event | category | flops | bytes accessed | tf_op | source)
XLA Modules:
  0.0 1370.3 jit_solution(17072326907275681100)
XLA Ops:
  19.1 26.0 %all-reduce.36 = (bf16[1536]{0:T(1024)(128)(2,1)S(1)}, bf16[1536]{0:T(1024)(128)(2,1)S(1)}, bf16[768]{0:T(1024)(128)(2,1)S(1)}, bf16[768]{0:T(1024)(128)(2,1)S(1...) all-reduce(bf16[1536]{0:T(1024)(128)(2,1)S(1)} %dynamic-update-slic, ...), channel_id=3, replica_groups=mesh['rep'=4,'shard'=8] {'shard'}, use_global_device_ids=true, to_apply=%add | all-reduce | flops 6144 | bytes 24576
  45.7 7.9 all-gather.13
  54.9 8.7 all-gather.20
  63.8 7.8 all-gather.19
  72.2 8.9 all-gather.5
  81.7 7.7 all-gather.18
  90.2 8.7 all-gather.17
  123.7 11.5 all-gather.44.cloned.1.call-done
  139.5 36.9 %all-gather.46.cloned.1.call-done = bf16[1,768,3072]{2,1,0:T(8,128)(2,1)} async-done(((bf16[1,96,3072]{2,1,0:T(8,128)(2,1)}), bf16[1,768,3072]{2,1,0:T(8,128)(2,1)}) %all-gather.46.cloned.1.call-update) | async-done | bytes 4718608 | tf_op jit(solution)/shard_map/all_gather | solution.py:39
  176.5 11.2 fusion.44
  187.7 30.0 %all-gather.48.cloned.1.call-done = bf16[1,3072,768]{2,1,0:T(8,128)(2,1)} async-done(((bf16[1,384,768]{2,1,0:T(8,128)(2,1)}), bf16[1,3072,768]{2,1,0:T(8,128)(2,1)}) %all-gather.48.cloned.1.call-update) | async-done | bytes 4718608 | tf_op jit(solution)/shard_map/all_gather | solution.py:39
  223.4 45.2 %all-gather.16 = bf16[1,128,1,768]{3,2,0,1:T(2,128)(2,1)} all-gather(bf16[1,4,1,768]{3,2,0,1:T(2,128)(2,1)S(1)} %slice.288), channel_id=18, replica_groups=mesh['rep'=4,'shard'=8] {'rep','shard'}, dimensions={1}, use_global_device_ids=true | all-gather | bytes 202752 | tf_op jit(solution)/shard_map/all_gather | solution.py:352
  268.7 8.2 fusion.60
  276.8 25.6 %all-gather.40.cloned.1.call-done = bf16[1,3072,768]{2,1,0:T(8,128)(2,1)} async-done(((bf16[1,384,768]{2,1,0:T(8,128)(2,1)}), bf16[1,3072,768]{2,1,0:T(8,128)(2,1)}) %all-gather.40.cloned.1.call-update) | async-done | bytes 4718608 | tf_op jit(solution)/shard_map/all_gather | solution.py:39
  319.5 5.3 convert_reduce_fusion.3
  334.7 121.8 %all-reduce.41.cloned.1.call-done = f32[128,768]{1,0:T(8,128)} async-done(((f32[128,768]{1,0:T(8,128)}), f32[128,768]{1,0:T(8,128)}) %all-reduce.41.cloned.1.call-update) | async-done | bytes 393232
  469.3 5.5 convert_reduce_fusion
  501.0 8.1 copy.173
  524.1 8.1 copy.177
  533.4 5.2 fusion.179
  549.3 6.6 fusion.182
  559.5 58.5 %reduce-scatter.65.cloned.1.call-done = f32[96,2304]{1,0:T(8,128)} async-done(((f32[768,2304]{1,0:T(8,128)}), f32[96,2304]{1,0:T(8,128)}) %reduce-scatter.65.cloned.1.call-update) | async-done | bytes 884752
  620.6 66.5 %reduce-scatter.69.cloned.1.call-done = f32[96,2304]{1,0:T(8,128)} async-done(((f32[768,2304]{1,0:T(8,128)}), f32[96,2304]{1,0:T(8,128)}) %reduce-scatter.69.cloned.1.call-update) | async-done | bytes 884752
  689.8 6.6 fusion.168
  696.6 70.7 %reduce-scatter.49.cloned.1.call-done = f32[96,3072]{1,0:T(8,128)} async-done(((f32[768,3072]{1,0:T(8,128)}), f32[96,3072]{1,0:T(8,128)}) %reduce-scatter.49.cloned.1.call-update) | async-done | bytes 1179664 | tf_op jit(solution)/shard_map/reduce_scatter | solution.py:231
  775.9 39.6 %psum.7 = f32[]{:T(128)} all-reduce(f32[]{:T(128)} %subtract_reduce_fusion), channel_id=1, replica_groups=mesh['rep'=4,'shard'=8] {'rep','shard'}, use_global_device_ids=true, to_apply=%region_17.18 | all-reduce | flops 1 | bytes 8 | tf_op jit(solution)/shard_map/psum | solution.py:385
  822.3 19.7 %reduce-scatter.77.cloned.1.call-done = f32[96,2]{1,0:T(8,128)} async-done(((f32[768,2]{1,0:T(8,128)}), f32[96,2]{1,0:T(8,128)}) %reduce-scatter.77.cloned.1.call-update) | async-done | bytes 784
  842.9 79.4 %reduce-scatter.57.cloned.1.call-done = f32[384,768]{1,0:T(8,128)} async-done(((f32[3072,768]{1,0:T(8,128)}), f32[384,768]{1,0:T(8,128)}) %reduce-scatter.57.cloned.1.call-update) | async-done | bytes 1179664 | tf_op jit(solution)/shard_map/reduce_scatter | solution.py:233
  924.7 23.7 %all-reduce.35 = (bf16[1536]{0:T(1024)(128)(2,1)S(1)}, bf16[1536]{0:T(1024)(128)(2,1)S(1)}, bf16[768]{0:T(1024)(128)(2,1)S(1)}, bf16[768]{0:T(1024)(128)(2,1)S(1...) all-reduce(f32[1536]{0:T(1024)S(1)} %pad_maximum_fusion.3, ...), channel_id=26, replica_groups=mesh['rep'=4,'shard'=8] {'shard'}, use_global_device_ids=true, to_apply=%region_37.38.clone | all-reduce | flops 12288 | bytes 73728
  949.1 11.8 all-reduce.38
  968.0 28.6 %reduce-scatter.79.cloned.1.call-done = f32[96,2]{1,0:T(8,128)} async-done(((f32[768,2]{1,0:T(8,128)}), f32[96,2]{1,0:T(8,128)}) %reduce-scatter.79.cloned.1.call-update) | async-done | bytes 784
  997.4 11.8 all-reduce.37
  1010.1 66.8 %reduce-scatter.53.cloned.1.call-done = f32[96,3072]{1,0:T(8,128)} async-done(((f32[768,3072]{1,0:T(8,128)}), f32[96,3072]{1,0:T(8,128)}) %reduce-scatter.53.cloned.1.call-update) | async-done | bytes 1179664 | tf_op jit(solution)/shard_map/reduce_scatter | solution.py:231
  1079.2 10.8 all-gather.22
  1090.1 7.5 all-gather.21
  1097.7 9.5 all-gather.24
  1107.3 7.5 all-gather.23
  1117.8 14.6 %all_gather.158 = bf16[96,768]{1,0:T(8,128)(2,1)S(1)} all-gather(bf16[24,768]{1,0:T(8,128)(2,1)} %reduce-scatter.43.cloned.1.call-done), channel_id=1, replica_groups=mesh['rep'=4,'shard'=8] {'rep'}, dimensions={0}, use_global_device_ids=true | all-gather | bytes 184320 | tf_op jit(solution)/shard_map/all_gather | solution.py:277
  1132.4 13.8 %all_gather.159 = bf16[96,768]{1,0:T(8,128)(2,1)S(1)} all-gather(bf16[24,768]{1,0:T(8,128)(2,1)} %reduce-scatter.47.cloned.1.call-done), channel_id=1, replica_groups=mesh['rep'=4,'shard'=8] {'rep'}, dimensions={0}, use_global_device_ids=true | all-gather | bytes 184320 | tf_op jit(solution)/shard_map/all_gather | solution.py:277
  1147.1 16.9 %all_gather.154 = bf16[96,2304]{1,0:T(8,128)(2,1)S(1)} all-gather(bf16[24,2304]{1,0:T(8,128)(2,1)} %reduce-scatter.67.cloned.1.call-done), channel_id=1, replica_groups=mesh['rep'=4,'shard'=8] {'rep'}, dimensions={0}, use_global_device_ids=true | all-gather | bytes 552960 | tf_op jit(solution)/shard_map/all_gather | solution.py:271
  1164.0 14.6 %all_gather.155 = bf16[96,2304]{1,0:T(8,128)(2,1)S(1)} all-gather(bf16[24,2304]{1,0:T(8,128)(2,1)} %reduce-scatter.71.cloned.1.call-done), channel_id=1, replica_groups=mesh['rep'=4,'shard'=8] {'rep'}, dimensions={0}, use_global_device_ids=true | all-gather | bytes 552960 | tf_op jit(solution)/shard_map/all_gather | solution.py:271
  1178.7 64.3 %reduce-scatter.61.cloned.1.call-done = f32[384,768]{1,0:T(8,128)} async-done(((f32[3072,768]{1,0:T(8,128)}), f32[384,768]{1,0:T(8,128)}) %reduce-scatter.61.cloned.1.call-update) | async-done | bytes 1179664 | tf_op jit(solution)/shard_map/reduce_scatter | solution.py:233
  1246.4 21.4 %reduce-scatter.51.cloned.1.call-done = bf16[24,3072]{1,0:T(8,128)(2,1)} async-done(((bf16[96,3072]{1,0:T(8,128)(2,1)}), bf16[24,3072]{1,0:T(8,128)(2,1)}) %reduce-scatter.51.cloned.1.call-update) | async-done | bytes 147472 | tf_op jit(solution)/shard_map/reduce_scatter | solution.py:251
  1267.8 19.9 %all_gather.162 = bf16[96,3072]{1,0:T(8,128)(2,1)S(1)} all-gather(bf16[24,3072]{1,0:T(8,128)(2,1)} %reduce-scatter.51.cloned.1.call-done), channel_id=1, replica_groups=mesh['rep'=4,'shard'=8] {'rep'}, dimensions={0}, use_global_device_ids=true | all-gather | bytes 737280 | tf_op jit(solution)/shard_map/all_gather | solution.py:283
  1292.5 18.9 %all_gather.166 = bf16[384,768]{1,0:T(8,128)(2,1)S(1)} all-gather(bf16[96,768]{1,0:T(8,128)(2,1)} %reduce-scatter.59.cloned.1.call-done), channel_id=1, replica_groups=mesh['rep'=4,'shard'=8] {'rep'}, dimensions={0}, use_global_device_ids=true | all-gather | bytes 737280 | tf_op jit(solution)/shard_map/all_gather | solution.py:289
  1311.4 7.1 reduce-scatter.55.cloned.1.call-done
  1318.5 20.0 %all_gather.163 = bf16[96,3072]{1,0:T(8,128)(2,1)S(1)} all-gather(bf16[24,3072]{1,0:T(8,128)(2,1)} %reduce-scatter.55.cloned.1.call-done), channel_id=1, replica_groups=mesh['rep'=4,'shard'=8] {'rep'}, dimensions={0}, use_global_device_ids=true | all-gather | bytes 737280 | tf_op jit(solution)/shard_map/all_gather | solution.py:283
  1344.4 16.2 %all_gather.167 = bf16[384,768]{1,0:T(8,128)(2,1)S(1)} all-gather(bf16[96,768]{1,0:T(8,128)(2,1)} %reduce-scatter.63.cloned.1.call-done), channel_id=1, replica_groups=mesh['rep'=4,'shard'=8] {'rep'}, dimensions={0}, use_global_device_ids=true | all-gather | bytes 737280 | tf_op jit(solution)/shard_map/all_gather | solution.py:289
  (548 shorter events, 192.8 us)
Async XLA Ops:
  7.2 97.5 %all-gather.42.cloned.1.call-start = ((), (), s32[]{:S(2)}) async-start(), calls=%async_computation.36 | async-start | bytes 3981312 | tf_op jit(solution)/shard_map/all_gather | solution.py:39
  9.5 100.0 %all-gather.34.cloned.1.call-start = ((), (), s32[]{:S(2)}) async-start(), calls=%async_computation.32 | async-start | bytes 3981312 | tf_op jit(solution)/shard_map/all_gather | solution.py:39
  10.3 105.5 %all-gather.36.cloned.1.call-start = ((), (), s32[]{:S(2)}) async-start(), calls=%async_computation.33 | async-start | bytes 1327104 | tf_op jit(solution)/shard_map/all_gather | solution.py:39
  11.1 124.1 %all-gather.44.cloned.1.call-start = ((), (), s32[]{:S(2)}) async-start(), calls=%async_computation.37 | async-start | bytes 1327104 | tf_op jit(solution)/shard_map/all_gather | solution.py:39
  11.7 164.8 %all-gather.46.cloned.1.call-start = ((), (), s32[]{:S(2)}) async-start(), calls=%async_computation.38 | async-start | bytes 5308416 | tf_op jit(solution)/shard_map/all_gather | solution.py:39
  12.9 204.8 %all-gather.48.cloned.1.call-start = ((), (), s32[]{:S(2)}) async-start(), calls=%async_computation.39 | async-start | bytes 5308416 | tf_op jit(solution)/shard_map/all_gather | solution.py:39
  14.1 254.6 %all-gather.38.cloned.1.call-start = ((), (), s32[]{:S(2)}) async-start(), calls=%async_computation.34 | async-start | bytes 5308416 | tf_op jit(solution)/shard_map/all_gather | solution.py:39
  14.9 287.6 %all-gather.40.cloned.1.call-start = ((), (), s32[]{:S(2)}) async-start(), calls=%async_computation.35 | async-start | bytes 5308416 | tf_op jit(solution)/shard_map/all_gather | solution.py:39
  15.6 440.9 %all-reduce.41.cloned.1.call-start = ((), (), s32[]{:S(2)}) async-start(), calls=%async_computation.48 | async-start | bytes 786432
  90.1 212.3 %copy-start.50 = (f32[768]{0:T(1024)}, f32[768]{0:T(1024)S(1)}, u32[]{:S(2)}) copy-start(f32[768]{0:T(1024)S(1)} %get-tuple-element.88) | copy-start | bytes 9220
  99.6 229.5 %copy-start.42 = (f32[768]{0:T(1024)}, f32[768]{0:T(1024)S(1)}, u32[]{:S(2)}) copy-start(f32[768]{0:T(1024)S(1)} %get-tuple-element.86) | copy-start | bytes 9220
  103.9 362.8 %copy-start.46 = (f32[768]{0:T(1024)}, f32[768]{0:T(1024)S(1)}, u32[]{:S(2)}) copy-start(f32[768]{0:T(1024)S(1)} %get-tuple-element.211) | copy-start | bytes 9220
  103.9 373.2 %copy-start.48 = (f32[768]{0:T(1024)}, f32[768]{0:T(1024)S(1)}, u32[]{:S(2)}) copy-start(f32[768]{0:T(1024)S(1)} %get-tuple-element.210) | copy-start | bytes 9220
  329.0 227.0 %reduce-scatter.41.cloned.1.call-start = ((), (), s32[]{:S(2)}) async-start(), calls=%async_computation.20 | async-start | bytes 2654208 | tf_op jit(solution)/shard_map/reduce_scatter | solution.py:229
  334.4 129.7 %copy-start.62 = (f32[256]{0:T(256)S(1)}, f32[256]{0:T(256)}, u32[]{:S(2)}) copy-start(f32[256]{0:T(256)} %copy-done.61) | copy-start | bytes 3076
  334.5 129.7 %copy-start.65 = (f32[256]{0:T(256)S(1)}, f32[256]{0:T(256)}, u32[]{:S(2)}) copy-start(f32[256]{0:T(256)} %copy-done.64) | copy-start | bytes 3076
  334.5 223.3 %reduce-scatter.45.cloned.1.call-start = ((), (), s32[]{:S(2)}) async-start(), calls=%async_computation.22 | async-start | bytes 2654208 | tf_op jit(solution)/shard_map/reduce_scatter | solution.py:229
  480.8 137.2 %reduce-scatter.65.cloned.1.call-start = ((), (), s32[]{:S(2)}) async-start(), calls=%async_computation.40 | async-start | bytes 7962624
  509.1 178.0 %reduce-scatter.69.cloned.1.call-start = ((), (), s32[]{:S(2)}) async-start(), calls=%async_computation.42 | async-start | bytes 7962624
  532.3 235.0 %reduce-scatter.49.cloned.1.call-start = ((), (), s32[]{:S(2)}) async-start(), calls=%async_computation.24 | async-start | bytes 10616832 | tf_op jit(solution)/shard_map/reduce_scatter | solution.py:231
  538.6 282.7 %reduce-scatter.73.cloned.1.call-start = ((), (), s32[]{:S(2)}) async-start(), calls=%async_computation.44 | async-start | bytes 442368
  540.3 301.8 %reduce-scatter.77.cloned.1.call-start = ((), (), s32[]{:S(2)}) async-start(), calls=%async_computation.46 | async-start | bytes 442368
  541.3 381.0 %reduce-scatter.57.cloned.1.call-start = ((), (), s32[]{:S(2)}) async-start(), calls=%async_computation.28 | async-start | bytes 10616832 | tf_op jit(solution)/shard_map/reduce_scatter | solution.py:233
  546.5 420.6 %reduce-scatter.75.cloned.1.call-start = ((), (), s32[]{:S(2)}) async-start(), calls=%async_computation.45 | async-start | bytes 442368
  548.2 448.4 %reduce-scatter.79.cloned.1.call-start = ((), (), s32[]{:S(2)}) async-start(), calls=%async_computation.47 | async-start | bytes 442368
  549.2 527.7 %reduce-scatter.53.cloned.1.call-start = ((), (), s32[]{:S(2)}) async-start(), calls=%async_computation.26 | async-start | bytes 10616832 | tf_op jit(solution)/shard_map/reduce_scatter | solution.py:231
  556.0 561.9 %reduce-scatter.43.cloned.1.call-start = ((), (), s32[]{:S(2)}) async-start(), calls=%async_computation.21 | async-start | bytes 184320 | tf_op jit(solution)/shard_map/reduce_scatter | solution.py:245
  557.7 574.7 %reduce-scatter.47.cloned.1.call-start = ((), (), s32[]{:S(2)}) async-start(), calls=%async_computation.23 | async-start | bytes 184320 | tf_op jit(solution)/shard_map/reduce_scatter | solution.py:245
  559.5 587.6 %reduce-scatter.67.cloned.1.call-start = ((), (), s32[]{:S(2)}) async-start(), calls=%async_computation.41 | async-start | bytes 552960 | tf_op jit(solution)/shard_map/reduce_scatter | solution.py:239
  620.5 543.5 %reduce-scatter.71.cloned.1.call-start = ((), (), s32[]{:S(2)}) async-start(), calls=%async_computation.43 | async-start | bytes 552960 | tf_op jit(solution)/shard_map/reduce_scatter | solution.py:239
  689.5 553.4 %reduce-scatter.61.cloned.1.call-start = ((), (), s32[]{:S(2)}) async-start(), calls=%async_computation.30 | async-start | bytes 10616832 | tf_op jit(solution)/shard_map/reduce_scatter | solution.py:233
  696.5 119.0 %copy-start.56 = (f32[3,12,64]{2,1,0:T(8,128)S(1)}, f32[3,12,64]{2,1,0:T(8,128)}, u32[]{:S(2)}) copy-start(f32[3,12,64]{2,1,0:T(8,128)} %get-tuple-element.143) | copy-start | bytes 27652
  696.5 119.8 %copy-start.1 = (f32[256,768]{1,0:T(8,128)S(1)}, f32[256,768]{1,0:T(8,128)}, u32[]{:S(2)}) copy-start(f32[256,768]{1,0:T(8,128)} %copy-done) | copy-start | bytes 2359300
  696.5 119.8 %copy-start.47 = (f32[768]{0:T(1024)S(1)}, f32[768]{0:T(1024)}, u32[]{:S(2)}) copy-start(f32[768]{0:T(1024)} %copy-done.46) | copy-start | bytes 9220
  696.5 119.8 %copy-start.60 = (f32[768]{0:T(1024)S(1)}, f32[768]{0:T(1024)}, u32[]{:S(2)}) copy-start(f32[768]{0:T(1024)} %get-tuple-element.93) | copy-start | bytes 9220
  696.5 119.8 %copy-start.63 = (f32[256]{0:T(256)S(1)}, f32[256]{0:T(256)}, u32[]{:S(2)}) copy-start(f32[256]{0:T(256)} %copy-done.61) | copy-start | bytes 3076
  696.5 119.8 %copy-start.66 = (f32[256]{0:T(256)S(1)}, f32[256]{0:T(256)}, u32[]{:S(2)}) copy-start(f32[256]{0:T(256)} %copy-done.64) | copy-start | bytes 3076
  696.5 120.7 %copy-start.8 = (bf16[128,2304]{1,0:T(8,128)(2,1)S(1)}, bf16[128,2304]{1,0:T(8,128)(2,1)}, u32[]{:S(2)}) copy-start(bf16[128,2304]{1,0:T(8,128)(2,1)} %convert_element_type.394) | copy-start | bytes 1769476
  696.6 120.7 %copy-start.12 = (f32[128,768]{1,0:T(8,128)S(1)}, f32[128,768]{1,0:T(8,128)}, u32[]{:S(2)}) copy-start(f32[128,768]{1,0:T(8,128)} %copy-done.11) | copy-start | bytes 1179652
  696.6 571.2 %reduce-scatter.51.cloned.1.call-start = ((), (), s32[]{:S(2)}) async-start(), calls=%async_computation.25 | async-start | bytes 737280 | tf_op jit(solution)/shard_map/reduce_scatter | solution.py:251
  769.5 523.0 %reduce-scatter.59.cloned.1.call-start = ((), (), s32[]{:S(2)}) async-start(), calls=%async_computation.29 | async-start | bytes 737280 | tf_op jit(solution)/shard_map/reduce_scatter | solution.py:257
  821.3 103.4 %copy-start.75 = (f32[768]{0:T(1024)S(1)}, f32[768]{0:T(1024)}, u32[]{:S(2)}) copy-start(f32[768]{0:T(1024)} %get-tuple-element.137) | copy-start | bytes 9220
  821.3 103.4 %copy-start.76 = (f32[768]{0:T(1024)S(1)}, f32[768]{0:T(1024)}, u32[]{:S(2)}) copy-start(f32[768]{0:T(1024)} %get-tuple-element.141) | copy-start | bytes 9220
  821.3 103.4 %copy-start.88 = (f32[3072]{0:T(1024)S(1)}, f32[3072]{0:T(1024)}, u32[]{:S(2)}) copy-start(f32[3072]{0:T(1024)} %get-tuple-element.204) | copy-start | bytes 36868
  821.3 103.4 %copy-start.89 = (f32[3072]{0:T(1024)S(1)}, f32[3072]{0:T(1024)}, u32[]{:S(2)}) copy-start(f32[3072]{0:T(1024)} %get-tuple-element.202) | copy-start | bytes 36868
  821.3 141.9 %copy-start.10 = (f32[256,768]{1,0:T(8,128)S(1)}, f32[256,768]{1,0:T(8,128)}, u32[]{:S(2)}) copy-start(f32[256,768]{1,0:T(8,128)} %copy-done.9) | copy-start | bytes 2359300
  924.4 394.0 %reduce-scatter.55.cloned.1.call-start = ((), (), s32[]{:S(2)}) async-start(), calls=%async_computation.27 | async-start | bytes 737280 | tf_op jit(solution)/shard_map/reduce_scatter | solution.py:251
  1079.0 265.4 %reduce-scatter.63.cloned.1.call-start = ((), (), s32[]{:S(2)}) async-start(), calls=%async_computation.31 | async-start | bytes 737280 | tf_op jit(solution)/shard_map/reduce_scatter | solution.py:257
  (97 other events, 1217.5 us)
Sparse Core Ops, SparseCore 0:
  9.9 36.8 all-gather.41
  48.7 34.0 all-gather.33
  85.2 24.0 all-gather.35
  111.1 24.0 all-gather.43
  137.5 38.9 all-gather.45
  178.8 38.9 all-gather.47
  220.2 40.8 all-gather.37
  263.5 38.9 all-gather.39
  329.1 127.3 all-reduce.40
  460.7 41.5 reduce-scatter.40
  506.2 42.4 reduce-scatter.44
  552.5 65.4 reduce-scatter.64
  621.5 65.4 reduce-scatter.68
  690.8 76.4 reduce-scatter.48
  771.1 33.8 reduce-scatter.72
  808.1 33.8 reduce-scatter.76
  845.8 76.4 reduce-scatter.56
  925.5 33.8 reduce-scatter.74
  962.7 33.8 reduce-scatter.78
  1000.3 76.5 reduce-scatter.52
  1079.2 19.2 reduce-scatter.42
  1100.8 17.4 reduce-scatter.46
  1120.7 19.4 reduce-scatter.66
  1142.3 20.1 reduce-scatter.70
  1166.4 76.4 reduce-scatter.60
  1245.7 21.9 reduce-scatter.50
  1270.0 22.4 reduce-scatter.58
  1295.5 22.9 reduce-scatter.54
  1320.9 23.4 reduce-scatter.62
where the time goes:
time: 1380 us; the launch traced here: 1370 us
  waiting for transfers between devices  721 us (52%)
  blocking collectives  378 us (27%)
  matrix products  117 us (8%)
  local copies, waits for them, and re-layouts  70.2 us (5%)
  other arithmetic  56.7 us (4%)
  between operations  25.7 us (2%)
    unnamed x36, waiting for transfers between devices  298 us
    reduce_scatter x2, waiting for transfers between devices, reduce_layer(): lax.psum_scatter(layer_grads[6], 'shard', scatter_dimension=0, tiled=True)  144 us
    reduce_scatter x2, waiting for transfers between devices, reduce_layer(): lax.psum_scatter(layer_grads[4], 'shard', scatter_dimension=0, tiled=True)  137 us
    all_gather x8, waiting for transfers between devices, fetch_layer(): lax.all_gather(for_sending(pick_tower(stacks, tower_index)), 'shard', axi...  104 us
    unnamed x4, blocking collectives  73.4 us
    all_gather x6, blocking collectives, fetch_layer(): lax.all_gather(for_sending(pick_tower(stacks, tower_index)), 'shard', axi...  49.8 us
    all_gather x1, blocking collectives, local(): lax.all_gather(passage_cls, ('rep', 'shard'), axis=0, tiled=True)  45.2 us
    unnamed x301, local copies, waits for them, and re-layouts  44.6 us
  transfers between devices with their start and end apart: 29, of which 17 were waited for; matrix products, arithmetic and copies ran while one was open for 15% of the time, Pallas kernels for 0%

commit v1 on v0

--- a/solution.py
+++ b/solution.py
@@ -1,8 +1,11 @@
+import functools
 import math
 
 import jax
 import jax.numpy as jnp
 from jax import lax
+from jax.experimental import pallas as pl
+from jax.experimental.pallas import tpu as pltpu
 from jax.sharding import PartitionSpec as P
 
 HD = 64
@@ -13,6 +16,7 @@
 NEG_FILL = -1e30
 INV_ROOT_TWO = 0.7071067811865476
 INV_ROOT_TWO_PI = 0.3989422804014327
+VMEM_LIMIT = 66 * 1000 * 1000
 
 
 def for_sending(array):
@@ -429,6 +433,907 @@
     )
 
 
+BF = jnp.bfloat16
+F32 = jnp.float32
+MESH = pl.DeviceIdType.MESH
+ROWS = (128, 256)
+D = 768
+HALF = 384
+FFN = 768
+NEIGH = tuple((dy, dx, dc) for dy in (0, 1) for dx in (0, 1) for dc in (0, 1) if dy + dx + dc)
+
+(S_X, S_QKV, S_OUT, S_UP, S_DN, S_OP, S_MY, S_MC,
+ S_MF, S_F1A, S_F1B, S_F2, S_DY, S_DC, S_DF, S_D1A,
+ S_D1B, S_D2, S_DA, S_DX, S_GD, S_GU, S_GO, S_GQ,
+ S_ZAD, S_ZAU, S_ZAO, S_ZAQ, S_ZBD, S_ZBU, S_ZBO, S_ZBQ,
+ S_ZOD, S_ZOU, S_ZOO, S_ZOQ) = range(36)
+(S_SMALL, S_CZ, S_CP, S_BG, S_ZAS, S_ZBS, S_ZOS, S_COT, S_FIN, S_FIN2) = range(36, 46)
+N_SEMS = 184
+
+
+def nn(a, b):
+    return jnp.dot(a, b, preferred_element_type=F32)
+
+
+def nt(a, b):
+    return lax.dot_general(a, b, (((1,), (1,)), ((), ())), preferred_element_type=F32)
+
+
+def tn(a, b):
+    return lax.dot_general(a, b, (((0,), (0,)), ((), ())), preferred_element_type=F32)
+
+
+def flip(v, d):
+    return 1 - v if d else v
+
+
+def mo(v, m):
+    return pl.multiple_of(v, m)
+
+
+(B_X, B_COT, B_WQ, B_WO, B_WU, B_WD, B_QB, B_UB, B_QKV, B_P,
+ B_ATT, B_OS, B_OR, B_N1, B_N2, B_R1, B_R2, B_MID, B_ACT, B_SL,
+ B_S1, B_V1, B_S2, B_V2, B_KP, B_Y, B_DF, B_DA, B_GD, B_GU,
+ B_GO, B_GQ, B_ZSD, B_ZSU, B_ZSO, B_ZSQ, B_ZAD, B_ZAU, B_ZAO, B_ZAQ,
+ B_ZBD, B_ZBU, B_ZBO, B_ZBQ, B_SP, B_PV, B_BG, B_BGS, B_BGR, B_BGA,
+ B_BGB, B_CM, B_GA, B_CG) = range(54)
+
+
+def scratch_list():
+    s = []
+
+    def add(name, t, shape, dtype):
+        s.append(((name, t), pltpu.VMEM(shape, dtype)))
+
+    for t, T in enumerate(ROWS):
+        add(B_X, t, (2 * T, D), BF)
+        add(B_COT, t, (T, D), BF)
+        add(B_WQ, t, (D, 3 * HALF), BF)
+        add(B_WO, t, (HALF, D), BF)
+        add(B_WU, t, (D, FFN), BF)
+        add(B_WD, t, (FFN, D), BF)
+        add(B_QB, t, (8, 3 * HALF), F32)
+        add(B_UB, t, (8, FFN), F32)
+        add(B_QKV, t, (2 * T, 3 * HALF), BF)
+        add(B_P, t, (12, T, T), F32)
+        add(B_ATT, t, (2 * T, HALF), BF)
+        add(B_OS, t, (T, D), BF)
+        add(B_OR, t, (T, D), BF)
+        add(B_N1, t, (T, D), F32)
+        add(B_N2, t, (T, D), F32)
+        add(B_R1, t, (T, 128), F32)
+        add(B_R2, t, (T, 128), F32)
+        add(B_MID, t, (4 * T, D), BF)
+        add(B_ACT, t, (4 * T, FFN), BF)
+        add(B_SL, t, (4 * T, FFN), BF)
+        add(B_S1, t, (2, T, D), BF)
+        add(B_V1, t, (2, T, D), BF)
+        add(B_S2, t, (T, D), BF)
+        add(B_V2, t, (T, D), BF)
+        add(B_KP, t, (2, T, D), F32)
+        add(B_Y, t, (T, D), BF)
+        add(B_DF, t, (4 * T, D), BF)
+        add(B_DA, t, (2 * T, D), BF)
+        add(B_GD, t, (HALF, D), BF)
+        add(B_GU, t, (8, 96, FFN), BF)
+        add(B_GO, t, (4, 96, D), BF)
+        add(B_GQ, t, (8, 96, 3 * HALF), BF)
+        for first in (B_ZSD, B_ZAD, B_ZBD):
+            add(first, t, (HALF, D), BF)
+            add(first + 1, t, (96, 4 * D), BF)
+            add(first + 2, t, (96, D), BF)
+            add(first + 3, t, (96, 3 * D), BF)
+    add(B_SP, 0, (8, 32, D), BF)
+    add(B_PV, 0, (32, D), F32)
+    add(B_BG, 0, (32, D), F32)
+    add(B_BGS, 0, (32, D), F32)
+    add(B_BGR, 0, (8, 32, D), F32)
+    add(B_BGA, 0, (32, D), F32)
+    add(B_BGB, 0, (32, D), F32)
+    add(B_CM, 0, (16, 512), BF)
+    add(B_GA, 0, (32, 16, 512), BF)
+    add(B_CG, 0, (2, 16, D), F32)
+    return s
+
+
+def fused_kernel(stop, *refs):
+    (i_x0, i_x1, i_cot0, i_cot1, i_qkvw, i_outw, i_upw, i_dnw, i_small, i_pos, i_flags, i_valid,
+     o_loss, o_y0, o_y1, o_gx0, o_gx1, o_oq, o_oo, o_ou, o_od, o_obg) = refs[:22]
+    held = {key: ref for (key, _), ref in zip(scratch_list(), refs[22:])}
+    sems = refs[-1]
+
+    def g(name, t):
+        return held[(name, t)]
+
+    rep = lax.axis_index("rep")
+    s = lax.axis_index("shard")
+    y = s // 4
+    x = (s // 2) % 2
+    c = s % 2
+    x_in = (i_x0, i_x1)
+    cot_in = (i_cot0, i_cot1)
+
+    def sem(name, t, side):
+        return sems.at[4 * name + 2 * t + side]
+
+    def sh(yy, xx, cc):
+        return yy * 4 + xx * 2 + cc
+
+    def send(src, dst, name, t, dev):
+        pltpu.make_async_remote_copy(src, dst, send_sem=sem(name, t, 1), recv_sem=sem(name, t, 0),
+                                     device_id=dev, device_id_type=MESH).start()
+
+    def local(src, dst, name, t, side=0):
+        pltpu.make_async_copy(src, dst, sem(name, t, side)).start()
+
+    def wait(ref, name, t, side=0):
+        pltpu.make_async_copy(ref, ref, sem(name, t, side)).wait()
+
+    def peer(d):
+        return flip(y, d[0]), flip(x, d[1]), flip(c, d[2])
+
+    sib = (rep, sh(y, x, 1 - c))
+    ypeer = (rep, sh(1 - y, x, c))
+    xpeer = (rep, sh(y, 1 - x, c))
+
+    bar = pltpu.get_barrier_semaphore()
+    for d in NEIGH:
+        pl.semaphore_signal(bar, 1, device_id=(rep, sh(*peer(d))), device_id_type=MESH)
+    for k in (1, 2, 3):
+        pl.semaphore_signal(bar, 1, device_id=((rep + k) % 4, s), device_id_type=MESH)
+    pl.semaphore_wait(bar, 10)
+
+    for t, T in enumerate(ROWS):
+        own = g(B_X, t).at[pl.ds(mo(c * T, 128), T)]
+        send(x_in[t], own, S_X, t, sib)
+        local(x_in[t], own, S_X, t)
+    for d in NEIGH:
+        send(i_small, g(B_SP, 0).at[s], S_SMALL, 0, (rep, sh(*peer(d))))
+    local(i_small, g(B_SP, 0).at[s], S_SMALL, 0)
+    rows96 = pl.ds(mo(s * 96, 32), 96)
+
+    def send_qkv(t):
+        for part in range(3):
+            for d in NEIGH:
+                p = peer(d)
+                send(i_qkvw.at[t, :, pl.ds(mo(part * D + p[2] * HALF, 128), HALF)],
+                     g(B_WQ, t).at[rows96, pl.ds(part * HALF, HALF)], S_QKV, t, (rep, sh(*p)))
+            local(i_qkvw.at[t, :, pl.ds(mo(part * D + c * HALF, 128), HALF)],
+                  g(B_WQ, t).at[rows96, pl.ds(part * HALF, HALF)], S_QKV, t)
+
+    def send_out(t):
+        dst = g(B_WO, t).at[pl.ds(mo((x * 2 + c) * 96, 32), 96)]
+        for dy in (0, 1):
+            for dx in (0, 1):
+                dev = (rep, sh(flip(y, dy), flip(x, dx), y))
+                if dy + dx:
+                    send(i_outw.at[t], dst, S_OUT, t, dev)
+                else:
+                    @pl.when(c == y)
+                    def _():
+                        local(i_outw.at[t], dst, S_OUT, t)
+
+                    @pl.when(c != y)
+                    def _():
+                        send(i_outw.at[t], dst, S_OUT, t, dev)
+
+    def send_up(t):
+        for d in NEIGH + ((0, 0, 0),):
+            p = peer(d)
+            for xx in (0, 1):
+                src = i_upw.at[t, :, pl.ds(mo(HALF * (4 * p[0] + 2 * xx + p[2]), 128), HALF)]
+                dst = g(B_WU, t).at[rows96, pl.ds(xx * HALF, HALF)]
+                if sum(d):
+                    send(src, dst, S_UP, t, (rep, sh(*p)))
+                else:
+                    local(src, dst, S_UP, t)
+
+    def send_dn(t):
+        dst = g(B_WD, t).at[pl.ds(mo(x * HALF, 128), HALF)]
+        send(i_dnw.at[t], dst, S_DN, t, xpeer)
+        local(i_dnw.at[t], dst, S_DN, t)
+
+    for t in (1, 0):
+        send_qkv(t)
+        send_out(t)
+    for t in (1, 0):
+        send_up(t)
+        send_dn(t)
+    for t in (0, 1):
+        local(cot_in[t], g(B_COT, t), S_COT, 0, t)
+
+    wait(g(B_SP, 0), S_SMALL, 0)
+    tot = g(B_SP, 0)[0].astype(F32)
+    for k in range(1, 8):
+        tot = tot + g(B_SP, 0)[k].astype(F32)
+    g(B_PV, 0)[...] = tot
+
+    def prow(t, k):
+        return g(B_PV, 0)[t * 16 + k:t * 16 + k + 1, :]
+
+    lane_half = pl.ds(mo(c * HALF, 128), HALF)
+    for t in (0, 1):
+        g(B_QB, t)[...] = jnp.zeros((8, 3 * HALF), F32)
+        g(B_QB, t)[0:1, 0:HALF] = g(B_PV, 0)[t * 16:t * 16 + 1, lane_half]
+        g(B_QB, t)[0:1, 2 * HALF:] = g(B_PV, 0)[t * 16 + 1:t * 16 + 2, lane_half]
+        for xx in (0, 1):
+            lo = g(B_PV, 0)[t * 16 + 8 + xx:t * 16 + 9 + xx, lane_half]
+            hi = g(B_PV, 0)[t * 16 + 10 + xx:t * 16 + 11 + xx, lane_half]
+            g(B_UB, t)[0:1, xx * HALF:(xx + 1) * HALF] = jnp.where(jnp.full((1, HALF), y) == 0, lo, hi)
+
+    def same_part(t, grp):
+        T = ROWS[t]
+        shift = 5 if t == 0 else 6
+        ri = lax.broadcasted_iota(jnp.int32, (T, T), 0) >> shift
+        ci = lax.broadcasted_iota(jnp.int32, (T, T), 1) >> shift
+        m = ri == ci
+        if t == 1:
+            flag = i_flags[pl.ds(grp * 8, 1), 0:1]
+            m = m | (flag > 0.0)
+        return m
+
+    lane_lo = lax.broadcasted_iota(jnp.int32, (1, 128), 1) < 64
+    mask_a = lane_lo.astype(F32).astype(BF)
+    mask_b = (1.0 - lane_lo.astype(F32)).astype(BF)
+
+    def lnfwd(first, gain, shift):
+        mean = jnp.mean(first, axis=-1, keepdims=True)
+        cen = first - mean
+        inv = lax.rsqrt(jnp.mean(cen * cen, axis=-1, keepdims=True) + LN_EPS)
+        n = cen * inv
+        return n, inv, n * gain + shift
+
+    CH = 64
+
+    def attention(t):
+        T = ROWS[t]
+        X, WQ, QKV, P, ATT = g(B_X, t), g(B_WQ, t), g(B_QKV, t), g(B_P, t), g(B_ATT, t)
+        wait(X, S_X, t)
+        wait(WQ, S_QKV, t)
+
+        @pl.loop(0, 3)
+        def _(j):
+            cols = pl.ds(mo(j * HALF, 128), HALF)
+            QKV[:, cols] = (nn(X[...], WQ[:, cols]) + g(B_QB, t)[0:1, cols]).astype(BF)
+
+        @pl.loop(0, 2)
+        def _(grp):
+            rows = pl.ds(mo(grp * T, 128), T)
+            m = same_part(t, grp)
+
+            @pl.loop(0, 3)
+            def _(hp):
+                q = QKV[rows, pl.ds(mo(hp * 128, 128), 128)]
+                k = QKV[rows, pl.ds(mo(HALF + hp * 128, 128), 128)]
+                val = QKV[rows, pl.ds(mo(2 * HALF + hp * 128, 128), 128)]
+                outs = []
+                for h, msk in ((0, mask_a), (1, mask_b)):
+                    sc = jnp.where(m, nt(q * msk, k) * (1.0 / math.sqrt(HD)), NEG_FILL)
+                    mx = jnp.max(sc, axis=-1, keepdims=True)
+                    e = jnp.exp(sc - mx)
+                    p = e * (1.0 / jnp.sum(e, axis=-1, keepdims=True))
+                    P[grp * 6 + hp * 2 + h] = p
+                    outs.append(nn(p.astype(BF), val))
+                ATT[rows, pl.ds(mo(hp * 128, 128), 128)] = jnp.where(lane_lo, outs[0], outs[1]).astype(BF)
+
+        wait(g(B_WO, t), S_OUT, t)
+        g(B_OS, t)[...] = nn(ATT[pl.ds(mo((1 - c) * T, 128), T), :], g(B_WO, t)[...]).astype(BF)
+        send(g(B_OS, t), g(B_OR, t), S_OP, t, sib)
+        g(B_KP, t)[0] = nn(ATT[pl.ds(mo(c * T, 128), T), :], g(B_WO, t)[...])
+        wait(g(B_OR, t), S_OP, t)
+        me4 = (2 * y + c) * T
+        ob, gain, shift = prow(t, 2), prow(t, 4), prow(t, 6)
+
+        @pl.loop(0, T // CH)
+        def _(i):
+            r = pl.ds(mo(i * CH, CH), CH)
+            first = (X[pl.ds(mo(c * T + i * CH, CH), CH), :].astype(F32) + g(B_KP, t)[0, r, :]
+                     + g(B_OR, t)[r, :].astype(F32) + ob)
+            n, inv, mid = lnfwd(first, gain, shift)
+            g(B_N1, t)[r, :] = n
+            g(B_R1, t)[r, :] = jnp.broadcast_to(inv, (CH, 128))
+            g(B_MID, t)[pl.ds(mo(me4 + i * CH, CH), CH), :] = mid.astype(BF)
+
+        gather_rows(t, B_MID, S_MY, S_MC, S_MF)
+
+    def slot_rows(t, yy, cc):
+        T = ROWS[t]
+        return pl.ds(mo((2 * yy + cc) * T, 128), T)
+
+    def gather_rows(t, buf, ny, nc, nf):
+        own = g(buf, t).at[slot_rows(t, y, c)]
+        send(own, own, ny, t, ypeer)
+        send(own, own, nc, t, sib)
+
+    def gather_near(t, buf, nc):
+        wait(g(buf, t).at[slot_rows(t, y, 1 - c)], nc, t)
+
+    def gather_forward(t, buf, ny, nf):
+        got = g(buf, t).at[slot_rows(t, 1 - y, c)]
+        wait(got, ny, t)
+        send(got, got, nf, t, sib)
+
+    def gather_far(t, buf, nf):
+        wait(g(buf, t).at[slot_rows(t, 1 - y, 1 - c)], nf, t)
+
+    def gather_sent(t, buf, ny, nc, nf):
+        own = g(buf, t).at[slot_rows(t, y, c)]
+        wait(own, ny, t, 1)
+        wait(own, nc, t, 1)
+        wait(own, nf, t, 1)
+
+    def up_pair(t, yy):
+        T = ROWS[t]
+        rows = pl.ds(mo(2 * yy * T, 128), 2 * T)
+
+        @pl.loop(0, 3)
+        def _(j):
+            cols = pl.ds(mo(j * 256, 128), 256)
+            pre = nn(g(B_MID, t)[rows, :], g(B_WU, t)[:, cols]) + g(B_UB, t)[0:1, cols]
+            cdf = 0.5 * (1.0 + lax.erf(pre * INV_ROOT_TWO))
+            g(B_ACT, t)[rows, cols] = (pre * cdf).astype(BF)
+            g(B_SL, t)[rows, cols] = (cdf + pre * jnp.exp(-0.5 * pre * pre) * INV_ROOT_TWO_PI).astype(BF)
+
+    def scatter_partial(t, part, n1a, n1b, n2):
+        S1, V1, S2, V2, KP = g(B_S1, t), g(B_V1, t), g(B_S2, t), g(B_V2, t), g(B_KP, t)
+        S1[0] = part(slot_rows(t, 1 - y, 1 - c)).astype(BF)
+        send(S1.at[0], V1.at[0], n1a, t, sib)
+        KP[0] = part(slot_rows(t, 1 - y, c))
+        S1[1] = part(slot_rows(t, y, 1 - c)).astype(BF)
+        send(S1.at[1], V1.at[1], n1b, t, sib)
+        wait(V1.at[0], n1a, t)
+        S2[...] = (KP[0] + V1[0].astype(F32)).astype(BF)
+        send(S2, V2, n2, t, ypeer)
+        KP[1] = part(slot_rows(t, y, c))
+
+    def scatter_finish(t, n1b, n2):
+        wait(g(B_V1, t).at[1], n1b, t)
+        wait(g(B_V2, t), n2, t)
+
+    def scatter_sent(t, n1a, n1b, n2):
+        wait(g(B_S1, t).at[0], n1a, t, 1)
+        wait(g(B_S1, t).at[1], n1b, t, 1)
+        wait(g(B_S2, t), n2, t, 1)
+
+    def summed(t, r):
+        return g(B_KP, t)[1, r, :] + g(B_V1, t)[1, r, :].astype(F32) + g(B_V2, t)[r, :].astype(F32)
+
+    def ffn(t):
+        gather_near(t, B_MID, S_MC)
+        gather_forward(t, B_MID, S_MY, S_MF)
+        wait(g(B_WU, t), S_UP, t)
+        up_pair(t, y)
+        gather_far(t, B_MID, S_MF)
+        up_pair(t, 1 - y)
+        wait(g(B_WD, t), S_DN, t)
+        scatter_partial(t, lambda rows: nn(g(B_ACT, t)[rows, :], g(B_WD, t)[...]), S_F1A, S_F1B, S_F2)
+
+    def ffn_end(t):
+        T = ROWS[t]
+        scatter_finish(t, S_F1B, S_F2)
+        db, g0, s0, g1, s1 = prow(t, 3), prow(t, 4), prow(t, 6), prow(t, 5), prow(t, 7)
+
+        @pl.loop(0, T // CH)
+        def _(i):
+            r = pl.ds(mo(i * CH, CH), CH)
+            second = g(B_N1, t)[r, :] * g0 + s0 + summed(t, r) + db
+            n, inv, res = lnfwd(second, g1, s1)
+            g(B_N2, t)[r, :] = n
+            g(B_R2, t)[r, :] = jnp.broadcast_to(inv, (CH, 128))
+            g(B_Y, t)[r, :] = res.astype(BF)
+
+        local(g(B_Y, t), (o_y0, o_y1)[t], S_FIN, 0, t)
+
+    attention(1)
+    attention(0)
+    ffn(1)
+    ffn(0)
+    ffn_end(1)
+    ffn_end(0)
+
+    def pick(T, lo, step):
+        ri = lax.broadcasted_iota(jnp.int32, (16, T), 0) & 7
+        ci = lax.broadcasted_iota(jnp.int32, (16, T), 1)
+        return (((ri & 4) == lo) & (ci == (ri & 3) * step)).astype(F32).astype(BF)
+
+    both = nn(pick(128, 0, 32), g(B_Y, 0)[...]) + nn(pick(256, 4, 64), g(B_Y, 1)[...])
+    top = lax.broadcasted_iota(jnp.int32, (16, HALF), 0) < 8
+    g(B_CM, 0)[:, :HALF] = jnp.where(top, both[:, :HALF], both[:, HALF:]).astype(BF)
+    g(B_CM, 0)[:, HALF:] = i_pos[...]
+    mine = g(B_GA, 0).at[s * 4 + rep]
+    for k in (1, 2, 3):
+        send(g(B_CM, 0), mine, S_CZ, 0, ((rep + k) % 4, s))
+    g(B_GA, 0)[s * 4 + rep] = g(B_CM, 0)[...]
+    wait(g(B_GA, 0).at[pl.ds(0, 3)], S_CZ, 0)
+    four = g(B_GA, 0).at[pl.ds(s * 4, 4)]
+    for d in NEIGH:
+        send(four, four, S_CP, 0, (rep, sh(*peer(d))))
+
+    for t in (0, 1):
+        own = g(B_X, t).at[pl.ds(mo(c * ROWS[t], 128), ROWS[t])]
+        wait(own, S_X, t, 1)
+        wait(g(B_WQ, t).at[pl.ds(0, 672)], S_QKV, t, 1)
+
+        @pl.when(c == y)
+        def _():
+            wait(g(B_WO, t).at[pl.ds(0, 288)], S_OUT, t, 1)
+
+        @pl.when(c != y)
+        def _():
+            wait(g(B_WO, t), S_OUT, t, 1)
+
+        wait(g(B_WU, t).at[pl.ds(0, 672)], S_UP, t, 1)
+        wait(g(B_WD, t).at[pl.ds(0, HALF)], S_DN, t, 1)
+        wait(g(B_OS, t), S_OP, t, 1)
+        gather_sent(t, B_MID, S_MY, S_MC, S_MF)
+        scatter_sent(t, S_F1A, S_F1B, S_F2)
+        wait(g(B_COT, t), S_COT, 0, t)
+    wait(g(B_SP, 0).at[pl.ds(0, 7)], S_SMALL, 0, 1)
+    wait(g(B_GA, 0).at[pl.ds(0, 3)], S_CZ, 0, 1)
+    g(B_BG, 0)[...] = jnp.zeros((32, D), F32)
+
+    wait(g(B_GA, 0).at[pl.ds(0, 28)], S_CP, 0)
+    wait(g(B_GA, 0).at[pl.ds(0, 28)], S_CP, 0, 1)
+
+    def pick_all(base):
+        ri = lax.broadcasted_iota(jnp.int32, (128, 512), 0)
+        ci = lax.broadcasted_iota(jnp.int32, (128, 512), 1)
+        blk = ci >> 4
+        within = (ci & 15) - base
+        row = ((blk & 3) * 8 + (blk >> 2)) * 4 + within
+        return ((within >= 0) & (within < 4) & (ri == row)).astype(F32).astype(BF)
+
+    ga = g(B_GA, 0)[...].reshape(512, 512)
+    qa_f = nn(pick_all(0), ga)
+    qa = qa_f[:, :HALF].astype(BF)
+    pa = nn(pick_all(4), ga)[:, :HALF].astype(BF)
+    qb = nn(pick_all(8), ga)[:, :HALF].astype(BF)
+    pb = nn(pick_all(12), ga)[:, :HALF].astype(BF)
+    scale = 2.0 / math.sqrt(D)
+    logits = (nt(qa, pa) + nt(qb, pb)) * scale
+    masked = jnp.where(i_valid[0:1, :] > 0.0, logits, NEG_FILL)
+    mx = jnp.max(masked, axis=1, keepdims=True)
+    ex = jnp.exp(masked - mx)
+    sm = jnp.sum(ex, axis=1, keepdims=True)
+    hit = lax.broadcasted_iota(jnp.int32, (128, 128), 1).astype(F32) == qa_f[:, HALF:]
+    ce = mx + jnp.log(sm) - jnp.sum(jnp.where(hit, masked, 0.0), axis=1, keepdims=True)
+    o_loss[...] = jnp.broadcast_to(jnp.sum(ce, axis=0, keepdims=True) * (1.0 / 128.0), (8, 128))
+    dl = (ex / sm - hit.astype(F32)).astype(BF)
+    ri = lax.broadcasted_iota(jnp.int32, (16, 128), 0)
+    ci = lax.broadcasted_iota(jnp.int32, (16, 128), 1)
+    sel = ((ri < 4) & (ci == ri + 4 * (rep * 8 + s))).astype(F32).astype(BF)
+    dlq = nn(sel, dl).astype(BF)
+    dlp = nt(sel, dl.T).astype(BF) if False else lax.dot_general(
+        sel, dl, (((1,), (1,)), ((), ())), preferred_element_type=F32).astype(BF)
+    g(B_CG, 0)[0, :, :HALF] = nn(dlq, pa) * scale
+    g(B_CG, 0)[0, :, HALF:] = nn(dlq, pb) * scale
+    g(B_CG, 0)[1, :, :HALF] = nn(dlp, qa) * scale
+    g(B_CG, 0)[1, :, HALF:] = nn(dlp, qb) * scale
+
+    def fold(a):
+        return jnp.sum(a.reshape(CH // 8, 8, D), axis=0)
+
+    def put_bias(t, k, row):
+        g(B_BG, 0)[t * 16 + k:t * 16 + k + 1, :] = row
+
+    def ln_back(t, din, nrm, inv, gain):
+        gg = din * gain
+        m1 = jnp.mean(gg, axis=-1, keepdims=True)
+        m2 = jnp.mean(gg * nrm, axis=-1, keepdims=True)
+        return inv * (gg - m1 - nrm * m2)
+
+    def out_back(t):
+        T = ROWS[t]
+        step = 32 if t == 0 else 64
+        KP = g(B_KP, t)
+        KP[0] = g(B_COT, t)[...].astype(F32)
+        for i in range(4):
+            KP[0, i * step:i * step + 1, :] = KP[0, i * step:i * step + 1, :] + g(B_CG, 0)[t, i:i + 1, :]
+        gain = prow(t, 5)
+        me4 = (2 * y + c) * T
+        zero = jnp.zeros((8, D), F32)
+
+        def body(i, acc):
+            r = pl.ds(mo(i * CH, CH), CH)
+            dout = KP[0, r, :]
+            nrm = g(B_N2, t)[r, :]
+            dsec = ln_back(t, dout, nrm, g(B_R2, t)[r, 0:1], gain)
+            low = dsec.astype(BF)
+            g(B_N2, t)[r, :] = dsec
+            g(B_DF, t)[pl.ds(mo(me4 + i * CH, CH), CH), :] = low
+            return (acc[0] + fold(dout * nrm), acc[1] + fold(dout), acc[2] + fold(low.astype(F32)))
+
+        acc = lax.fori_loop(0, T // CH, body, (zero, zero, zero))
+        gather_rows(t, B_DF, S_DY, S_DC, S_DF)
+        for k, a in zip((5, 7, 3), acc):
+            put_bias(t, k, jnp.sum(a, axis=0, keepdims=True))
+
+    def down_pair(t, yy):
+        T = ROWS[t]
+        rows = pl.ds(mo(2 * yy * T, 128), 2 * T)
+
+        @pl.loop(0, 3)
+        def _(j):
+            cols = pl.ds(mo(j * 256, 128), 256)
+            da = nt(g(B_DF, t)[rows, :], g(B_WD, t)[cols, :])
+            g(B_SL, t)[rows, cols] = (da * g(B_SL, t)[rows, cols].astype(F32)).astype(BF)
+
+    def ffn_back(t):
+        gather_near(t, B_DF, S_DC)
+        gather_forward(t, B_DF, S_DY, S_DF)
+        down_pair(t, y)
+        gather_far(t, B_DF, S_DF)
+        down_pair(t, 1 - y)
+        scatter_partial(t, lambda rows: nt(g(B_SL, t)[rows, :], g(B_WU, t)[...]), S_D1A, S_D1B, S_D2)
+        ones = jnp.ones((8, 4 * ROWS[t]), F32).astype(BF)
+        sums = nn(ones, g(B_SL, t)[...])[0:1, :]
+        for xx in (0, 1):
+            part = sums[:, xx * HALF:(xx + 1) * HALF]
+
+            @pl.when(y == 0)
+            def _():
+                g(B_BG, 0)[t * 16 + 8 + xx:t * 16 + 9 + xx, lane_half] = part
+
+            @pl.when(y == 1)
+            def _():
+                g(B_BG, 0)[t * 16 + 10 + xx:t * 16 + 11 + xx, lane_half] = part
+
+        @pl.loop(0, 3)
+        def _(j):
+            cols = pl.ds(mo(j * 256, 128), 256)
+            g(B_WD, t)[cols, :] = tn(g(B_ACT, t)[:, cols], g(B_DF, t)[...]).astype(BF)
+
+        send(g(B_WD, t).at[pl.ds(mo((1 - x) * HALF, 128), HALF)], g(B_GD, t), S_GD, t, xpeer)
+
+        @pl.loop(0, 3)
+        def _(j):
+            cols = pl.ds(mo(j * 256, 128), 256)
+            g(B_WU, t)[cols, :] = tn(g(B_MID, t)[:, cols], g(B_SL, t)[...]).astype(BF)
+
+        for d in NEIGH:
+            p = peer(d)
+            send(g(B_WU, t).at[pl.ds(mo(96 * sh(*p), 32), 96)], g(B_GU, t).at[s], S_GU, t, (rep, sh(*p)))
+        local(g(B_WU, t).at[rows96], g(B_GU, t).at[s], S_GU, t)
+
+    def mid_back(t):
+        T = ROWS[t]
+        scatter_finish(t, S_D1B, S_D2)
+        gain = prow(t, 4)
+        zero = jnp.zeros((8, D), F32)
+
+        def body(i, acc):
+            r = pl.ds(mo(i * CH, CH), CH)
+            dmid = g(B_N2, t)[r, :] + summed(t, r)
+            nrm = g(B_N1, t)[r, :]
+            dfirst = ln_back(t, dmid, nrm, g(B_R1, t)[r, 0:1], gain)
+            low = dfirst.astype(BF)
+            g(B_N1, t)[r, :] = dfirst
+            g(B_DA, t)[pl.ds(mo(c * T + i * CH, CH), CH), :] = low
+            return (acc[0] + fold(dmid * nrm), acc[1] + fold(dmid), acc[2] + fold(low.astype(F32)))
+
+        acc = lax.fori_loop(0, T // CH, body, (zero, zero, zero))
+        own = g(B_DA, t).at[pl.ds(mo(c * T, 128), T)]
+        send(own, own, S_DA, t, sib)
+        for k, a in zip((4, 6, 2), acc):
+            put_bias(t, k, jnp.sum(a, axis=0, keepdims=True))
+
+    def attention_back(t):
+        T = ROWS[t]
+        QKV, P, ATT, DA, WO, WQ = g(B_QKV, t), g(B_P, t), g(B_ATT, t), g(B_DA, t), g(B_WO, t), g(B_WQ, t)
+        wait(DA.at[pl.ds(mo((1 - c) * T, 128), T)], S_DA, t)
+
+        @pl.loop(0, 2)
+        def _(grp):
+            rows = pl.ds(mo(grp * T, 128), T)
+
+            @pl.loop(0, 3)
+            def _(hp):
+                lanes = pl.ds(mo(hp * 128, 128), 128)
+                dat = nt(DA[rows, :], WO[lanes, :]).astype(BF)
+                qs, ks = lanes, pl.ds(mo(HALF + hp * 128, 128), 128)
+                vs = pl.ds(mo(2 * HALF + hp * 128, 128), 128)
+                q, k, val = QKV[rows, qs], QKV[rows, ks], QKV[rows, vs]
+                dq, dk, dv = [], [], []
+                for h, msk in ((0, mask_a), (1, mask_b)):
+                    p = P[grp * 6 + hp * 2 + h]
+                    dp = nt(dat * msk, val)
+                    ds = (p * (dp - jnp.sum(dp * p, axis=-1, keepdims=True))).astype(BF)
+                    dv.append(tn(p.astype(BF), dat))
+                    dq.append(nn(ds, k))
+                    dk.append(tn(ds, q))
+                root = 1.0 / math.sqrt(HD)
+                QKV[rows, qs] = (jnp.where(lane_lo, dq[0], dq[1]) * root).astype(BF)
+                QKV[rows, ks] = (jnp.where(lane_lo, dk[0], dk[1]) * root).astype(BF)
+                QKV[rows, vs] = jnp.where(lane_lo, dv[0], dv[1]).astype(BF)
+
+        g(B_OS, t)[...] = nt(QKV[pl.ds(mo((1 - c) * T, 128), T), :], WQ[...]).astype(BF)
+        send(g(B_OS, t), g(B_OR, t), S_DX, t, sib)
+        g(B_KP, t)[0] = nt(QKV[pl.ds(mo(c * T, 128), T), :], WQ[...])
+
+        ones = jnp.ones((8, 2 * T), F32).astype(BF)
+        sums = nn(ones, QKV[...])[0:1, :]
+        g(B_BG, 0)[t * 16:t * 16 + 1, lane_half] = sums[:, :HALF]
+        g(B_BG, 0)[t * 16 + 1:t * 16 + 2, lane_half] = sums[:, 2 * HALF:]
+
+        @pl.loop(0, 3)
+        def _(j):
+            cols = pl.ds(mo(j * 128, 128), 128)
+            WO[cols, :] = tn(ATT[:, cols], DA[...]).astype(BF)
+
+        dst = g(B_GO, t).at[y * 2 + x]
+        for dy in (0, 1):
+            for dx in (0, 1):
+                for dc in (0, 1):
+                    pass
+        for xx in (0, 1):
+            for cc in (0, 1):
+                src = WO.at[pl.ds((2 * xx + cc) * 96, 96)]
+                dev = sh(c, xx, cc)
+
+                @pl.when(dev == s)
+                def _():
+                    local(src, dst, S_GO, t)
+
+                @pl.when(dev != s)
+                def _():
+                    send(src, dst, S_GO, t, (rep, dev))
+
+        @pl.loop(0, 3)
+        def _(j):
+            cols = pl.ds(mo(j * 256, 128), 256)
+            WQ[cols, :] = tn(g(B_X, t)[:, cols], QKV[...]).astype(BF)
+
+        for d in NEIGH:
+            p = peer(d)
+            send(WQ.at[pl.ds(mo(96 * sh(*p), 32), 96)], g(B_GQ, t).at[s], S_GQ, t, (rep, sh(*p)))
+        local(WQ.at[rows96], g(B_GQ, t).at[s], S_GQ, t)
+
+    def input_back(t):
+        T = ROWS[t]
+        wait(g(B_OR, t), S_DX, t)
+
+        @pl.loop(0, T // CH)
+        def _(i):
+            r = pl.ds(mo(i * CH, CH), CH)
+            g(B_Y, t)[r, :] = (g(B_N1, t)[r, :] + g(B_KP, t)[0, r, :] + g(B_OR, t)[r, :].astype(F32)).astype(BF)
+
+        local(g(B_Y, t), (o_gx0, o_gx1)[t], S_FIN2, 0, t)
+
+    out_back(0)
+    out_back(1)
+    for t in (0, 1):
+        wait(g(B_Y, t), S_FIN, 0, t)
+    ffn_back(0)
+    ffn_back(1)
+    mid_back(0)
+    mid_back(1)
+    attention_back(0)
+    attention_back(1)
+    input_back(0)
+    input_back(1)
+
+    for d in NEIGH:
+        send(g(B_BG, 0), g(B_BGR, 0).at[s], S_BG, 0, (rep, sh(*peer(d))))
+    local(g(B_BG, 0), g(B_BGR, 0).at[s], S_BG, 0)
+
+    def sum_dn(t, r0, n):
+        return g(B_WD, t)[pl.ds(mo(x * HALF + r0, 32), n), :].astype(F32) + g(B_GD, t)[pl.ds(r0, n), :].astype(F32)
+
+    def each_dn(t, use):
+        wait(g(B_GD, t), S_GD, t)
+        for r0 in range(0, HALF, 96):
+            use(pl.ds(r0, 96), pl.ds(0, D), sum_dn(t, r0, 96))
+
+    def each_up(t, use):
+        wait(g(B_GU, t), S_GU, t)
+        for yy in (0, 1):
+            for cc in (0, 1):
+                both = g(B_GU, t)[sh(yy, 0, cc)].astype(F32) + g(B_GU, t)[sh(yy, 1, cc)].astype(F32)
+                for xx in (0, 1):
+                    j = 4 * yy + 2 * xx + cc
+                    use(pl.ds(0, 96), pl.ds(j * HALF, HALF), both[:, xx * HALF:(xx + 1) * HALF])
+
+    def each_out(t, use):
+        wait(g(B_GO, t), S_GO, t)
+        tot = g(B_GO, t)[0].astype(F32)
+        for k in range(1, 4):
+            tot = tot + g(B_GO, t)[k].astype(F32)
+        use(pl.ds(0, 96), pl.ds(0, D), tot)
+
+    def each_qkv(t, use):
+        wait(g(B_GQ, t), S_GQ, t)
+        for cc in (0, 1):
+            tot = g(B_GQ, t)[cc].astype(F32)
+            for k in range(1, 4):
+                tot = tot + g(B_GQ, t)[2 * k + cc].astype(F32)
+            for part in range(3):
+                use(pl.ds(0, 96), pl.ds(part * D + cc * HALF, HALF), tot[:, part * HALF:(part + 1) * HALF])
+
+    def each_small(t, use):
+        wait(g(B_BGR, 0), S_BG, 0)
+        tot = g(B_BGR, 0)[0]
+        for k in range(1, 8):
+            tot = tot + g(B_BGR, 0)[k]
+        use(pl.ds(0, 32), pl.ds(0, D), tot)
+
+    is_end = (rep == 0) | (rep == 3)
+    chunks = []
+    for t in (0, 1):
+        chunks.append((0, t, each_dn, o_od.at[t]))
+        chunks.append((1, t, each_up, o_ou.at[t]))
+    for t in (0, 1):
+        chunks.append((2, t, each_out, o_oo.at[t]))
+        chunks.append((3, t, each_qkv, o_oq.at[t]))
+    chunks.append((4, 0, each_small, o_obg))
+
+    def zbuf(kind, which, t):
+        if kind == 4:
+            return g((B_BGS, B_BGA, B_BGB)[which], 0)
+        return g((B_ZSD, B_ZAD, B_ZBD)[which] + kind, t)
+
+    def zsem(hop, kind):
+        return (S_ZAS, S_ZBS, S_ZOS)[hop] if kind == 4 else (S_ZAD, S_ZBD, S_ZOD)[hop] + kind
+
+    def stage_a(k):
+        kind, t, each, out = chunks[k]
+        ZS, ZA, ZB = zbuf(kind, 0, t), zbuf(kind, 1, t), zbuf(kind, 2, t)
+
+        def put(r, cl, val):
+            ZS[r, cl] = val.astype(ZS.dtype)
+
+        def put_add(r, cl, val):
+            ZS[r, cl] = (val + ZA[r, cl].astype(F32)).astype(ZS.dtype)
+
+        for end, mid in ((0, 1), (3, 2)):
+            @pl.when(rep == end)
+            def _():
+                each(t, put)
+                send(ZS, ZA, zsem(0, kind), t, (mid, s))
+
+            @pl.when(rep == mid)
+            def _():
+                wait(ZA, zsem(0, kind), t)
+                each(t, put_add)
+                send(ZS, ZB, zsem(1, kind), t, (3 - mid, s))
+
+    def stage_b(k):
+        kind, t, each, out = chunks[k]
+        ZS, ZB = zbuf(kind, 0, t), zbuf(kind, 2, t)
+        for end, mid in ((0, 1), (3, 2)):
+            @pl.when(rep == mid)
+            def _():
+                wait(ZB, zsem(1, kind), t)
+                wait(ZB, zsem(1, kind), t, 1)
+                n = ZS.shape[0]
+                for r0 in range(0, n, 32):
+                    r = pl.ds(r0, 32)
+                    ZS[r, :] = (ZS[r, :].astype(F32) + ZB[r, :].astype(F32)).astype(ZS.dtype)
+                send(ZS, out, zsem(2, kind), t, (end, s))
+                local(ZS, out, zsem(2, kind), t)
+
+    for k in range(len(chunks)):
+        stage_a(k)
+        if k:
+            stage_b(k - 1)
+    stage_b(len(chunks) - 1)
+
+    for k in range(len(chunks)):
+        kind, t, each, out = chunks[k]
+        ZS = zbuf(kind, 0, t)
+        wait(ZS, zsem(2, kind), t)
+
+        @pl.when(is_end)
+        def _():
+            wait(ZS, zsem(0, kind), t, 1)
+
+        @pl.when(jnp.logical_not(is_end))
+        def _():
+            wait(ZS, zsem(2, kind), t, 1)
+
+    for t in (0, 1):
+        gather_sent(t, B_DF, S_DY, S_DC, S_DF)
+        scatter_sent(t, S_D1A, S_D1B, S_D2)
+        wait(g(B_OS, t), S_DA, t, 1)
+        wait(g(B_OS, t), S_DX, t, 1)
+        wait(g(B_GD, t), S_GD, t, 1)
+        wait(g(B_GU, t).at[pl.ds(0, 7)], S_GU, t, 1)
+
+        @pl.when(c == y)
+        def _():
+            wait(g(B_GO, t).at[pl.ds(0, 3)], S_GO, t, 1)
+
+        @pl.when(c != y)
+        def _():
+            wait(g(B_GO, t), S_GO, t, 1)
+
+        wait(g(B_GQ, t).at[pl.ds(0, 7)], S_GQ, t, 1)
+        wait(g(B_Y, t), S_FIN2, 0, t)
+    wait(g(B_BGR, 0).at[pl.ds(0, 7)], S_BG, 0, 1)
+
+
+def fused_call(x0, x1, cot0, cot1, qkvw, outw, upw, dnw, small, pos, flags, valid):
+    hbm = pl.BlockSpec(memory_space=pl.ANY)
+    vm = pl.BlockSpec(memory_space=pltpu.VMEM)
+    out_shape = [
+        jax.ShapeDtypeStruct((8, 128), F32),
+        jax.ShapeDtypeStruct((128, D), BF),
+        jax.ShapeDtypeStruct((256, D), BF),
+        jax.ShapeDtypeStruct((128, D), BF),
+        jax.ShapeDtypeStruct((256, D), BF),
+        jax.ShapeDtypeStruct((2, 96, 3 * D), BF),
+        jax.ShapeDtypeStruct((2, 96, D), BF),
+        jax.ShapeDtypeStruct((2, 96, 4 * D), BF),
+        jax.ShapeDtypeStruct((2, HALF, D), BF),
+        jax.ShapeDtypeStruct((32, D), F32),
+    ]
+    return pl.pallas_call(
+        functools.partial(fused_kernel, None),
+        out_shape=out_shape,
+        in_specs=[hbm] * 8 + [hbm] + [vm] * 3,
+        out_specs=[vm] + [hbm] * 9,
+        scratch_shapes=[shape for _, shape in scratch_list()] + [pltpu.SemaphoreType.DMA((N_SEMS,))],
+        compiler_params=pltpu.CompilerParams(collective_id=0, has_side_effects=True, vmem_limit_bytes=VMEM_LIMIT),
+        cost_estimate=pl.CostEstimate(flops=18 * 10**9, bytes_accessed=40 * 10**6, transcendentals=4 * 10**6),
+    )(x0, x1, cot0, cot1, qkvw, outw, upw, dnw, small, pos, flags, valid)
+
+
+def spread(shard, s, n):
+    w = shard.shape[1]
+    place = lax.broadcasted_iota(jnp.int32, (1, n * w), 1) // w == s
+    return jnp.where(place, jnp.tile(shard, (1, n)), jnp.zeros((), BF))
+
+
+def local_fast(query_tokens, passage_tokens, query_cot, passage_cot, bucket_counts, positives, qkv_weight, qv_bias,
+               out_weight, out_bias, up_weight, up_bias, down_weight, down_bias, norm_gains, norm_shifts):
+    rep = lax.axis_index("rep")
+    s = lax.axis_index("shard")
+    rows = [
+        spread(qv_bias, s, 8).reshape(2, 2, D),
+        spread(out_bias, s, 8)[:, None],
+        spread(down_bias, s, 8)[:, None],
+        spread(norm_gains[:, 0], s, 8)[:, None],
+        spread(norm_gains[:, 1], s, 8)[:, None],
+        spread(norm_shifts[:, 0], s, 8)[:, None],
+        spread(norm_shifts[:, 1], s, 8)[:, None],
+        spread(up_bias, s, 8).reshape(2, 4, D),
+        jnp.zeros((2, 4, D), BF),
+    ]
+    small = jnp.concatenate(rows, axis=1).reshape(32, D)
+    pos = jnp.concatenate([jnp.broadcast_to(positives.astype(BF)[:, None], (4, 128)), jnp.zeros((12, 128), BF)], axis=0)
+    chip = lax.dynamic_slice(bucket_counts, ((rep * 8 + s) // 2 * 2,), (2,))
+    flags = jnp.broadcast_to((chip > 0).astype(F32)[:, None, None], (2, 8, 128)).reshape(16, 128)
+    slot = lax.iota(jnp.int32, 128)
+    counts = jnp.broadcast_to(bucket_counts[:, None], (32, 4)).reshape(128)
+    valid = jnp.broadcast_to(((counts <= 0) | (slot % 4 == 0)).astype(F32)[None], (8, 128))
+    loss, y0, y1, gx0, gx1, oq, oo, ou, od, bg = fused_call(
+        query_tokens.reshape(128, D), passage_tokens.reshape(256, D),
+        query_cot.reshape(128, D), passage_cot.reshape(256, D),
+        qkv_weight, out_weight, up_weight, down_weight, small, pos, flags, valid)
+    bg = bg.reshape(2, 16, D)
+
+    def own(a, w):
+        return lax.dynamic_slice(a, (0, s * w), (2, w))
+
+    def own_pair(a):
+        return lax.dynamic_slice(a, (0, 0, s * 96), (2, 2, 96))
+
+    return (
+        loss[0, 0],
+        y0.reshape(query_tokens.shape), y1.reshape(passage_tokens.shape),
+        gx0.reshape(query_tokens.shape), gx1.reshape(passage_tokens.shape),
+        oq.astype(F32),
+        own(bg[:, 0:2].reshape(2, 2 * D), 192),
+        oo.astype(F32),
+        own(bg[:, 2], 96),
+        ou.astype(F32),
+        own(bg[:, 8:12].reshape(2, 4 * D), HALF),
+        od.astype(F32),
+        own(bg[:, 3], 96),
+        own_pair(bg[:, 4:6]),
+        own_pair(bg[:, 6:8]),
+    )
+
+
 def solution(mesh):
     in_specs = (
         P(("rep", "shard"), None, None),
@@ -465,4 +1370,6 @@
         P(None, None, "shard"),
         P(None, None, "shard"),
     )
-    return jax.shard_map(local, mesh=mesh, in_specs=in_specs, out_specs=out_specs, check_vma=False)
+    small_mesh = (mesh.shape["rep"], mesh.shape["shard"]) == (4, 8)
+    step = local_fast if small_mesh else local
+    return jax.shard_map(step, mesh=mesh, in_specs=in_specs, out_specs=out_specs, check_vma=False)

time: 1380 us -> 331 us (0.24)
  waiting for transfers between devices: 721 us -> 0 us
  blocking collectives: 378 us -> 0 us
  Pallas kernels: 0 us -> 301 us
  matrix products: 117 us -> 0 us
  local copies, waits for them, and re-layouts: 70.2 us -> 16.5 us
  other arithmetic: 56.7 us -> 8.97 us
  between operations: 25.7 us -> 0.86 us
    reduce_scatter x14 -> x0, waiting for transfers between devices: 319 us -> none  [the longest x2 144 us: reduce_layer(): lax.psum_scatter(layer_grads[6], 'shard', scatter_dimension=0, tiled=True)]
    pallas_call x0 -> x1, Pallas kernels: none -> 301 us  [fused_call(): pl.pallas_call(functools.partial(fused_kernel, None), out_shape=out_shape...]
    unnamed x36 -> x0, waiting for transfers between devices: 298 us -> none
    all_gather x19 -> x0, blocking collectives: 265 us -> none  [the longest x6 49.8 us: fetch_layer(): lax.all_gather(for_sending(pick_tower(stacks, tower_index)), 'shard', axi...]
    dot_general x39 -> x0, matrix products: 117 us -> none  [the longest x2 19.4 us: layer_forward(): jnp.dot(middle_low, up_w, preferred_element_type=jnp.float32)]
    all_gather x8 -> x0, waiting for transfers between devices: 104 us -> none  [fetch_layer(): lax.all_gather(for_sending(pick_tower(stacks, tower_index)), 'shard', axi...]
    unnamed x4 -> x0, blocking collectives: 73.4 us -> none
    unnamed x301 -> x25, local copies, waits for them, and re-layouts: 44.6 us -> 2.91 us
  transfers between devices with their start and end apart: 29 -> 0, of which waited for: 17 -> 0; matrix products, arithmetic and copies ran while one was open for 15% -> 0% of each run, Pallas kernels for 0% -> 0%
where the time goes in v1:
time: 331 us; the launch traced here: 327 us
  Pallas kernels  301 us (91%)
  local copies, waits for them, and re-layouts  16.5 us (5%)
  other arithmetic  8.97 us (3%)
    pallas_call x1, Pallas kernels, fused_call(): pl.pallas_call(functools.partial(fused_kernel, None), out_shape=out_shape...  301 us

profile of v1, /device:TPU:0, one launch (start us, length us, event | category | flops | bytes accessed | tf_op | source)
XLA Modules:
  0.0 327.2 jit_solution(9766926711554063629)
XLA Ops:
  0.7 0.7 compare_convert_fusion
  1.4 0.1 broadcast_in_dim.96
  1.5 0.1 broadcast_in_dim.97
  1.6 0.7 broadcast_in_dim.98.refs_10_
  2.2 0.8 fusion.10
  3.0 0.1 tile.84
  3.1 0.1 tile.87
  3.2 0.8 fusion.9
  4.0 0.1 tile.90
  4.1 0.1 tile.93
  4.2 0.7 tile.78
  4.8 0.1 tile.79
  4.9 0.7 tile.80
  5.6 0.1 tile.81
  5.8 0.7 tile.94
  6.6 0.7 tile.76
  7.3 0.1 tile.77
  7.4 1.3 concatenate.8
  8.7 0.7 broadcast_compare_fusion
  9.4 0.1 broadcast_in_dim.99
  9.4 0.1 le.12
  9.6 0.6 broadcast_in_dim.100.refs_11_
  10.2 0.7 convert_element_type.25
  10.8 0.7 concatenate.10.refs_9_
  11.5 301.0 %shard_map.271 = (f32[8,128]{1,0:T(8,128)}, bf16[128,768]{1,0:T(8,128)(2,1)}, bf16[256,768]{1,0:T(8,128)(2,1)}, bf16[128,768]{1,0:T(8,128)(2,1)}, bf16[256,768]{...) custom-call(bf16[128,768]{1,0:T(8,128)(2,1)} %bitcast.41, ...), custom_call_target="tpu_custom_call" | custom-call | flops 17999998976 | bytes 40000000 | tf_op jit(solution)/shard_map/pallas_call | solution.py:1269
  312.5 0.0 copy-start
  312.5 3.0 convert_element_type.30
  315.5 0.0 copy-done
  315.5 1.6 convert_element_type.31
  317.1 0.0 copy-done.1
  317.1 1.3 convert_element_type.28
  318.4 0.0 copy-done.4
  318.4 0.0 copy-start.2
  318.5 0.9 convert_element_type.29
  319.3 0.0 copy-done.7
  319.3 0.6 constant_dynamic-slice_fusion.3
  320.0 0.7 constant_dynamic-slice_fusion.5
  320.6 0.7 constant_dynamic-slice_fusion
  321.3 0.7 constant_dynamic-slice_fusion.1
  321.9 0.6 constant_dynamic-slice_fusion.4
  322.6 0.6 constant_dynamic-slice_fusion.2
  323.2 1.2 slice.37
  324.4 0.0 copy-done.6
  324.4 0.7 copy.51
  325.1 0.0 copy-done.3
  325.1 0.7 copy.52
  325.8 0.7 copy.53
  326.5 0.7 copy.54
  (35 shorter events, 0.3 us)
Async XLA Ops:
  312.5 3.0 copy-start
  315.5 1.6 copy-start.1
  317.1 1.3 copy-start.4
  317.1 2.2 copy-start.7
  318.4 6.0 %copy-start.6 = (bf16[128,768]{1,0:T(8,128)(2,1)S(1)}, bf16[128,768]{1,0:T(8,128)(2,1)}, u32[]{:S(2)}) copy-start(bf16[128,768]{1,0:T(8,128)(2,1)} %get-tuple-element.26) | copy-start | bytes 589828
  318.4 6.6 %copy-start.3 = (bf16[256,768]{1,0:T(8,128)(2,1)S(1)}, bf16[256,768]{1,0:T(8,128)(2,1)}, u32[]{:S(2)}) copy-start(bf16[256,768]{1,0:T(8,128)(2,1)} %get-tuple-element.27) | copy-start | bytes 1179652
  318.4 7.4 %copy-start.5 = (bf16[128,768]{1,0:T(8,128)(2,1)S(1)}, bf16[128,768]{1,0:T(8,128)(2,1)}, u32[]{:S(2)}) copy-start(bf16[128,768]{1,0:T(8,128)(2,1)} %get-tuple-element.28) | copy-start | bytes 589828
  318.4 8.1 %copy-start.2 = (bf16[256,768]{1,0:T(8,128)(2,1)S(1)}, bf16[256,768]{1,0:T(8,128)(2,1)}, u32[]{:S(2)}) copy-start(bf16[256,768]{1,0:T(8,128)(2,1)} %get-tuple-element.29) | copy-start | bytes 1179652

commit v2 on v1

--- a/solution.py
+++ b/solution.py
@@ -442,13 +442,11 @@
 FFN = 768
 NEIGH = tuple((dy, dx, dc) for dy in (0, 1) for dx in (0, 1) for dc in (0, 1) if dy + dx + dc)
 
-(S_X, S_QKV, S_OUT, S_UP, S_DN, S_OP, S_MY, S_MC,
- S_MF, S_F1A, S_F1B, S_F2, S_DY, S_DC, S_DF, S_D1A,
- S_D1B, S_D2, S_DA, S_DX, S_GD, S_GU, S_GO, S_GQ,
- S_ZAD, S_ZAU, S_ZAO, S_ZAQ, S_ZBD, S_ZBU, S_ZBO, S_ZBQ,
- S_ZOD, S_ZOU, S_ZOO, S_ZOQ) = range(36)
-(S_SMALL, S_CZ, S_CP, S_BG, S_ZAS, S_ZBS, S_ZOS, S_COT, S_FIN, S_FIN2) = range(36, 46)
-N_SEMS = 184
+(S_X, S_QKV, S_QKVC, S_QKVZ, S_OUT, S_OUTC, S_OUTZ, S_UP, S_UPC, S_UPZ,
+ S_DN, S_OP, S_MY, S_MC, S_MF, S_F1A, S_F1B, S_F2, S_DY, S_DC, S_DF, S_D1A, S_D1B, S_D2,
+ S_DA, S_DX, S_GD, S_GU, S_GO, S_GQ, S_SMALL, S_CZ, S_CP, S_BG, S_COT, S_FIN, S_FIN2, S_Z) = range(38)
+N_UNITS = 17
+N_SEMS = 4 * S_Z + 6 * N_UNITS + 2
 
 
 def nn(a, b):
@@ -475,8 +473,8 @@
  B_ATT, B_OS, B_OR, B_N1, B_N2, B_R1, B_R2, B_MID, B_ACT, B_SL,
  B_S1, B_V1, B_S2, B_V2, B_KP, B_Y, B_DF, B_DA, B_GD, B_GU,
  B_GO, B_GQ, B_ZSD, B_ZSU, B_ZSO, B_ZSQ, B_ZAD, B_ZAU, B_ZAO, B_ZAQ,
- B_ZBD, B_ZBU, B_ZBO, B_ZBQ, B_SP, B_PV, B_BG, B_BGS, B_BGR, B_BGA,
- B_BGB, B_CM, B_GA, B_CG) = range(54)
+ B_ZBD, B_ZBU, B_ZBO, B_ZBQ, B_T96, B_T192, B_LP, B_SP, B_PV, B_BG, B_BGS, B_BGR, B_BGA,
+ B_BGB, B_CM, B_GA, B_CG) = range(57)
 
 
 def scratch_list():
@@ -523,6 +521,9 @@
             add(first + 1, t, (96, 4 * D), BF)
             add(first + 2, t, (96, D), BF)
             add(first + 3, t, (96, 3 * D), BF)
+    add(B_T96, 0, (16, 128), F32)
+    add(B_T192, 0, (8, 256), F32)
+    add(B_LP, 0, (32, D), F32)
     add(B_SP, 0, (8, 32, D), BF)
     add(B_PV, 0, (32, D), F32)
     add(B_BG, 0, (32, D), F32)
@@ -536,10 +537,10 @@
     return s
 
 
-def fused_kernel(stop, *refs):
-    (i_x0, i_x1, i_cot0, i_cot1, i_qkvw, i_outw, i_upw, i_dnw, i_small, i_pos, i_flags, i_valid,
-     o_loss, o_y0, o_y1, o_gx0, o_gx1, o_oq, o_oo, o_ou, o_od, o_obg) = refs[:22]
-    held = {key: ref for (key, _), ref in zip(scratch_list(), refs[22:])}
+def fused_kernel(*refs):
+    (i_x0, i_x1, i_cot0, i_cot1, i_qkvw, i_outw, i_upw, i_dnw, i_qvb, i_ob, i_ub, i_db, i_gn, i_sf, i_cnt, i_pos,
+     o_loss, o_y0, o_y1, o_gx0, o_gx1, o_oq, o_oo, o_ou, o_od, o_obg) = refs[:26]
+    held = {key: ref for (key, _), ref in zip(scratch_list(), refs[26:])}
     sems = refs[-1]
 
     def g(name, t):
@@ -581,52 +582,128 @@
         pl.semaphore_signal(bar, 1, device_id=(rep, sh(*peer(d))), device_id_type=MESH)
     for k in (1, 2, 3):
         pl.semaphore_signal(bar, 1, device_id=((rep + k) % 4, s), device_id_type=MESH)
+
+    T96, T192, LP, SP, PV = (g(b, 0) for b in (B_T96, B_T192, B_LP, B_SP, B_PV))
+    T96[...] = jnp.zeros((16, 128), F32)
+    T192[...] = jnp.zeros((8, 256), F32)
+    LP[...] = jnp.zeros((32, D), F32)
+    T96[0:2, 0:96] = i_ob[...].astype(F32)
+    T96[2:4, 0:96] = i_db[...].astype(F32)
+    for t in (0, 1):
+        for k in (0, 1):
+            T96[4 + 2 * t + k:5 + 2 * t + k, 0:96] = i_gn[t, k:k + 1, :].astype(F32)
+            T96[8 + 2 * t + k:9 + 2 * t + k, 0:96] = i_sf[t, k:k + 1, :].astype(F32)
+    T192[0:2, 0:192] = i_qvb[...].astype(F32)
+
+    def place(n, w, at):
+        i = lax.broadcasted_iota(jnp.int32, (n, D), 0)
+        j = lax.broadcasted_iota(jnp.int32, (n, D), 1)
+        return ((j == i + at) & (i < w)).astype(F32).astype(BF)
+
+    LP[0:16, :] = nn(T96[...].astype(BF), place(128, 96, s * 96))
+    qv = nn(T192[...].astype(BF), place(256, 192, (s % 4) * 192))[0:2, :]
+    in_q = jnp.full((2, D), y) == 0
+    LP[12:14, :] = jnp.where(in_q, qv, 0.0)
+    LP[14:16, :] = jnp.where(in_q, 0.0, qv)
+    for t in (0, 1):
+        LP[pl.ds(16 + 4 * t + s // 2, 1), pl.ds(mo((s % 2) * HALF, 128), HALF)] = i_ub[t:t + 1, :].astype(F32)
+    SP[s] = LP[...].astype(BF)
+
     pl.semaphore_wait(bar, 10)
 
-    for t, T in enumerate(ROWS):
+    half = rep % 2
+    zpair = (rep + 1 - 2 * half, s)
+    for d in NEIGH:
+        send(SP.at[s], SP.at[s], S_SMALL, 0, (rep, sh(*peer(d))))
+    rows96 = pl.ds(mo(s * 96, 32), 96)
+    half48 = pl.ds(mo(half * 48, 16), 48)
+
+    def send_x(t):
+        T = ROWS[t]
         own = g(B_X, t).at[pl.ds(mo(c * T, 128), T)]
         send(x_in[t], own, S_X, t, sib)
         local(x_in[t], own, S_X, t)
-    for d in NEIGH:
-        send(i_small, g(B_SP, 0).at[s], S_SMALL, 0, (rep, sh(*peer(d))))
-    local(i_small, g(B_SP, 0).at[s], S_SMALL, 0)
-    rows96 = pl.ds(mo(s * 96, 32), 96)
+
+    def rows48(owner):
+        return pl.ds(mo(owner * 96 + half * 48, 16), 48)
+
+    def send_cols(t, src, dst, pieces, far, near):
+        for d in NEIGH + ((0, 0, 0),):
+            p = peer(d)
+            for k, at in enumerate(pieces(p)):
+                cols, to = pl.ds(mo(at, 128), HALF), pl.ds(k * HALF, HALF)
+                if d[0] + d[1]:
+                    send(src.at[t, half48, cols], dst.at[rows48(s), to], far, t, (rep, sh(*p)))
+                elif d[2]:
+                    send(src.at[t, :, cols], dst.at[rows96, to], near, t, sib)
+                else:
+                    local(src.at[t, :, cols], dst.at[rows96, to], near, t)
 
     def send_qkv(t):
-        for part in range(3):
-            for d in NEIGH:
-                p = peer(d)
-                send(i_qkvw.at[t, :, pl.ds(mo(part * D + p[2] * HALF, 128), HALF)],
-                     g(B_WQ, t).at[rows96, pl.ds(part * HALF, HALF)], S_QKV, t, (rep, sh(*p)))
-            local(i_qkvw.at[t, :, pl.ds(mo(part * D + c * HALF, 128), HALF)],
-                  g(B_WQ, t).at[rows96, pl.ds(part * HALF, HALF)], S_QKV, t)
+        send_cols(t, i_qkvw, g(B_WQ, t), lambda p: [part * D + p[2] * HALF for part in range(3)], S_QKV, S_QKVC)
+
+    def send_up(t):
+        send_cols(t, i_upw, g(B_WU, t), lambda p: [HALF * (4 * p[0] + 2 * xx + p[2]) for xx in (0, 1)], S_UP, S_UPC)
+
+    def forward_cols(t, buf, far, pair):
+        wait(buf.at[pl.ds(0, 288)], far, t)
+        for d in NEIGH:
+            if d[0] + d[1]:
+                piece = buf.at[rows48(sh(*peer(d)))]
+                send(piece, piece, pair, t, zpair)
+
+    def whole_cols(t, buf, near, pair):
+        wait(buf.at[pl.ds(0, 192)], near, t)
+        wait(buf.at[pl.ds(0, 288)], pair, t)
 
     def send_out(t):
-        dst = g(B_WO, t).at[pl.ds(mo((x * 2 + c) * 96, 32), 96)]
+        WO = g(B_WO, t)
         for dy in (0, 1):
             for dx in (0, 1):
                 dev = (rep, sh(flip(y, dy), flip(x, dx), y))
                 if dy + dx:
-                    send(i_outw.at[t], dst, S_OUT, t, dev)
+                    send(i_outw.at[t, half48], WO.at[rows48(x * 2 + c)], S_OUT, t, dev)
                 else:
+                    dst = WO.at[pl.ds(mo((x * 2 + c) * 96, 32), 96)]
+
                     @pl.when(c == y)
                     def _():
-                        local(i_outw.at[t], dst, S_OUT, t)
+                        local(i_outw.at[t], dst, S_OUTC, t)
 
                     @pl.when(c != y)
                     def _():
-                        send(i_outw.at[t], dst, S_OUT, t, dev)
-
-    def send_up(t):
-        for d in NEIGH + ((0, 0, 0),):
-            p = peer(d)
-            for xx in (0, 1):
-                src = i_upw.at[t, :, pl.ds(mo(HALF * (4 * p[0] + 2 * xx + p[2]), 128), HALF)]
-                dst = g(B_WU, t).at[rows96, pl.ds(xx * HALF, HALF)]
-                if sum(d):
-                    send(src, dst, S_UP, t, (rep, sh(*p)))
-                else:
-                    local(src, dst, S_UP, t)
+                        send(i_outw.at[t], dst, S_OUTC, t, dev)
+
+    def forward_out(t):
+        WO = g(B_WO, t)
+
+        def go(xs):
+            for xx in xs:
+                for cc in (0, 1):
+                    piece = WO.at[rows48(xx * 2 + cc)]
+                    send(piece, piece, S_OUTZ, t, zpair)
+
+        @pl.when(c == y)
+        def _():
+            wait(WO.at[pl.ds(0, 96)], S_OUT, t)
+            go((1 - x,))
+
+        @pl.when(c != y)
+        def _():
+            wait(WO.at[pl.ds(0, 192)], S_OUT, t)
+            go((0, 1))
+
+    def whole_out(t):
+        WO = g(B_WO, t)
+
+        @pl.when(c == y)
+        def _():
+            wait(WO.at[pl.ds(0, 192)], S_OUTC, t)
+            wait(WO.at[pl.ds(0, 96)], S_OUTZ, t)
+
+        @pl.when(c != y)
+        def _():
+            wait(WO.at[pl.ds(0, 192)], S_OUTZ, t)
 
     def send_dn(t):
         dst = g(B_WD, t).at[pl.ds(mo(x * HALF, 128), HALF)]
@@ -634,31 +711,32 @@
         local(i_dnw.at[t], dst, S_DN, t)
 
     for t in (1, 0):
+        send_x(t)
         send_qkv(t)
         send_out(t)
-    for t in (1, 0):
-        send_up(t)
-        send_dn(t)
+    send_up(1)
+    send_dn(1)
     for t in (0, 1):
         local(cot_in[t], g(B_COT, t), S_COT, 0, t)
 
-    wait(g(B_SP, 0), S_SMALL, 0)
-    tot = g(B_SP, 0)[0].astype(F32)
+    wait(SP.at[pl.ds(0, 7)], S_SMALL, 0)
+    tot = SP[0].astype(F32)
     for k in range(1, 8):
-        tot = tot + g(B_SP, 0)[k].astype(F32)
-    g(B_PV, 0)[...] = tot
-
-    def prow(t, k):
-        return g(B_PV, 0)[t * 16 + k:t * 16 + k + 1, :]
+        tot = tot + SP[k].astype(F32)
+    PV[...] = tot
+    R_OB, R_DB, R_GN, R_SF, R_QB, R_VB, R_UB = 0, 2, 4, 8, 12, 14, 16
+
+    def prow(k):
+        return PV[k:k + 1, :]
 
     lane_half = pl.ds(mo(c * HALF, 128), HALF)
     for t in (0, 1):
         g(B_QB, t)[...] = jnp.zeros((8, 3 * HALF), F32)
-        g(B_QB, t)[0:1, 0:HALF] = g(B_PV, 0)[t * 16:t * 16 + 1, lane_half]
-        g(B_QB, t)[0:1, 2 * HALF:] = g(B_PV, 0)[t * 16 + 1:t * 16 + 2, lane_half]
+        g(B_QB, t)[0:1, 0:HALF] = PV[R_QB + t:R_QB + t + 1, lane_half]
+        g(B_QB, t)[0:1, 2 * HALF:] = PV[R_VB + t:R_VB + t + 1, lane_half]
         for xx in (0, 1):
-            lo = g(B_PV, 0)[t * 16 + 8 + xx:t * 16 + 9 + xx, lane_half]
-            hi = g(B_PV, 0)[t * 16 + 10 + xx:t * 16 + 11 + xx, lane_half]
+            at = R_UB + 4 * t + xx
+            lo, hi = PV[at:at + 1, lane_half], PV[at + 2:at + 3, lane_half]
             g(B_UB, t)[0:1, xx * HALF:(xx + 1) * HALF] = jnp.where(jnp.full((1, HALF), y) == 0, lo, hi)
 
     def same_part(t, grp):
@@ -668,8 +746,7 @@
         ci = lax.broadcasted_iota(jnp.int32, (T, T), 1) >> shift
         m = ri == ci
         if t == 1:
-            flag = i_flags[pl.ds(grp * 8, 1), 0:1]
-            m = m | (flag > 0.0)
+            m = m | (jnp.full((T, T), i_cnt[rep * 8 + (s // 2) * 2 + grp]) > 0)
         return m
 
     lane_lo = lax.broadcasted_iota(jnp.int32, (1, 128), 1) < 64
@@ -689,7 +766,7 @@
         T = ROWS[t]
         X, WQ, QKV, P, ATT = g(B_X, t), g(B_WQ, t), g(B_QKV, t), g(B_P, t), g(B_ATT, t)
         wait(X, S_X, t)
-        wait(WQ, S_QKV, t)
+        whole_cols(t, WQ, S_QKVC, S_QKVZ)
 
         @pl.loop(0, 3)
         def _(j):
@@ -716,13 +793,13 @@
                     outs.append(nn(p.astype(BF), val))
                 ATT[rows, pl.ds(mo(hp * 128, 128), 128)] = jnp.where(lane_lo, outs[0], outs[1]).astype(BF)
 
-        wait(g(B_WO, t), S_OUT, t)
+        whole_out(t)
         g(B_OS, t)[...] = nn(ATT[pl.ds(mo((1 - c) * T, 128), T), :], g(B_WO, t)[...]).astype(BF)
         send(g(B_OS, t), g(B_OR, t), S_OP, t, sib)
         g(B_KP, t)[0] = nn(ATT[pl.ds(mo(c * T, 128), T), :], g(B_WO, t)[...])
         wait(g(B_OR, t), S_OP, t)
         me4 = (2 * y + c) * T
-        ob, gain, shift = prow(t, 2), prow(t, 4), prow(t, 6)
+        ob, gain, shift = prow(R_OB + t), prow(R_GN + 2 * t), prow(R_SF + 2 * t)
 
         @pl.loop(0, T // CH)
         def _(i):
@@ -801,7 +878,7 @@
     def ffn(t):
         gather_near(t, B_MID, S_MC)
         gather_forward(t, B_MID, S_MY, S_MF)
-        wait(g(B_WU, t), S_UP, t)
+        whole_cols(t, g(B_WU, t), S_UPC, S_UPZ)
         up_pair(t, y)
         gather_far(t, B_MID, S_MF)
         up_pair(t, 1 - y)
@@ -811,7 +888,8 @@
     def ffn_end(t):
         T = ROWS[t]
         scatter_finish(t, S_F1B, S_F2)
-        db, g0, s0, g1, s1 = prow(t, 3), prow(t, 4), prow(t, 6), prow(t, 5), prow(t, 7)
+        db = prow(R_DB + t)
+        g0, g1, s0, s1 = (prow(base + 2 * t + k) for base in (R_GN, R_SF) for k in (0, 1))
 
         @pl.loop(0, T // CH)
         def _(i):
@@ -824,8 +902,16 @@
 
         local(g(B_Y, t), (o_y0, o_y1)[t], S_FIN, 0, t)
 
+    forward_cols(1, g(B_WQ, 1), S_QKV, S_QKVZ)
+    forward_out(1)
+    forward_cols(0, g(B_WQ, 0), S_QKV, S_QKVZ)
     attention(1)
+    send_up(0)
+    send_dn(0)
+    forward_out(0)
+    forward_cols(1, g(B_WU, 1), S_UP, S_UPZ)
     attention(0)
+    forward_cols(0, g(B_WU, 0), S_UP, S_UPZ)
     ffn(1)
     ffn(0)
     ffn_end(1)
@@ -839,7 +925,11 @@
     both = nn(pick(128, 0, 32), g(B_Y, 0)[...]) + nn(pick(256, 4, 64), g(B_Y, 1)[...])
     top = lax.broadcasted_iota(jnp.int32, (16, HALF), 0) < 8
     g(B_CM, 0)[:, :HALF] = jnp.where(top, both[:, :HALF], both[:, HALF:]).astype(BF)
-    g(B_CM, 0)[:, HALF:] = i_pos[...]
+    ri = lax.broadcasted_iota(jnp.int32, (16, 128), 0)
+    pos = jnp.zeros((16, 128), jnp.int32)
+    for i in range(4):
+        pos = jnp.where(ri == i, i_pos[i], pos)
+    g(B_CM, 0)[:, HALF:] = pos.astype(F32).astype(BF)
     mine = g(B_GA, 0).at[s * 4 + rep]
     for k in (1, 2, 3):
         send(g(B_CM, 0), mine, S_CZ, 0, ((rep + k) % 4, s))
@@ -852,17 +942,21 @@
     for t in (0, 1):
         own = g(B_X, t).at[pl.ds(mo(c * ROWS[t], 128), ROWS[t])]
         wait(own, S_X, t, 1)
-        wait(g(B_WQ, t).at[pl.ds(0, 672)], S_QKV, t, 1)
+        for buf, far, near, pair in ((g(B_WQ, t), S_QKV, S_QKVC, S_QKVZ), (g(B_WU, t), S_UP, S_UPC, S_UPZ)):
+            wait(buf.at[pl.ds(0, 288)], far, t, 1)
+            wait(buf.at[pl.ds(0, 96)], near, t, 1)
+            wait(buf.at[pl.ds(0, 288)], pair, t, 1)
+        wait(g(B_WO, t).at[pl.ds(0, 144)], S_OUT, t, 1)
 
         @pl.when(c == y)
         def _():
-            wait(g(B_WO, t).at[pl.ds(0, 288)], S_OUT, t, 1)
+            wait(g(B_WO, t).at[pl.ds(0, 96)], S_OUTZ, t, 1)
 
         @pl.when(c != y)
         def _():
-            wait(g(B_WO, t), S_OUT, t, 1)
-
-        wait(g(B_WU, t).at[pl.ds(0, 672)], S_UP, t, 1)
+            wait(g(B_WO, t).at[pl.ds(0, 96)], S_OUTC, t, 1)
+            wait(g(B_WO, t).at[pl.ds(0, 192)], S_OUTZ, t, 1)
+
         wait(g(B_WD, t).at[pl.ds(0, HALF)], S_DN, t, 1)
         wait(g(B_OS, t), S_OP, t, 1)
         gather_sent(t, B_MID, S_MY, S_MC, S_MF)
@@ -891,7 +985,11 @@
     pb = nn(pick_all(12), ga)[:, :HALF].astype(BF)
     scale = 2.0 / math.sqrt(D)
     logits = (nt(qa, pa) + nt(qb, pb)) * scale
-    masked = jnp.where(i_valid[0:1, :] > 0.0, logits, NEG_FILL)
+    lane = lax.broadcasted_iota(jnp.int32, (1, 128), 1)
+    cnt = jnp.zeros((1, 128), jnp.int32)
+    for k in range(32):
+        cnt = jnp.where(lane >> 2 == k, i_cnt[k], cnt)
+    masked = jnp.where((cnt <= 0) | (lane & 3 == 0), logits, NEG_FILL)
     mx = jnp.max(masked, axis=1, keepdims=True)
     ex = jnp.exp(masked - mx)
     sm = jnp.sum(ex, axis=1, keepdims=True)
@@ -913,8 +1011,8 @@
     def fold(a):
         return jnp.sum(a.reshape(CH // 8, 8, D), axis=0)
 
-    def put_bias(t, k, row):
-        g(B_BG, 0)[t * 16 + k:t * 16 + k + 1, :] = row
+    def put_bias(k, row):
+        g(B_BG, 0)[k:k + 1, :] = row
 
     def ln_back(t, din, nrm, inv, gain):
         gg = din * gain
@@ -929,7 +1027,7 @@
         KP[0] = g(B_COT, t)[...].astype(F32)
         for i in range(4):
             KP[0, i * step:i * step + 1, :] = KP[0, i * step:i * step + 1, :] + g(B_CG, 0)[t, i:i + 1, :]
-        gain = prow(t, 5)
+        gain = prow(R_GN + 2 * t + 1)
         me4 = (2 * y + c) * T
         zero = jnp.zeros((8, D), F32)
 
@@ -945,8 +1043,8 @@
 
         acc = lax.fori_loop(0, T // CH, body, (zero, zero, zero))
         gather_rows(t, B_DF, S_DY, S_DC, S_DF)
-        for k, a in zip((5, 7, 3), acc):
-            put_bias(t, k, jnp.sum(a, axis=0, keepdims=True))
+        for k, a in zip((R_GN + 2 * t + 1, R_SF + 2 * t + 1, R_DB + t), acc):
+            put_bias(k, jnp.sum(a, axis=0, keepdims=True))
 
     def down_pair(t, yy):
         T = ROWS[t]
@@ -969,14 +1067,15 @@
         sums = nn(ones, g(B_SL, t)[...])[0:1, :]
         for xx in (0, 1):
             part = sums[:, xx * HALF:(xx + 1) * HALF]
+            at = R_UB + 4 * t + xx
 
             @pl.when(y == 0)
             def _():
-                g(B_BG, 0)[t * 16 + 8 + xx:t * 16 + 9 + xx, lane_half] = part
+                g(B_BG, 0)[at:at + 1, lane_half] = part
 
             @pl.when(y == 1)
             def _():
-                g(B_BG, 0)[t * 16 + 10 + xx:t * 16 + 11 + xx, lane_half] = part
+                g(B_BG, 0)[at + 2:at + 3, lane_half] = part
 
         @pl.loop(0, 3)
         def _(j):
@@ -998,7 +1097,7 @@
     def mid_back(t):
         T = ROWS[t]
         scatter_finish(t, S_D1B, S_D2)
-        gain = prow(t, 4)
+        gain = prow(R_GN + 2 * t)
         zero = jnp.zeros((8, D), F32)
 
         def body(i, acc):
@@ -1014,8 +1113,8 @@
         acc = lax.fori_loop(0, T // CH, body, (zero, zero, zero))
         own = g(B_DA, t).at[pl.ds(mo(c * T, 128), T)]
         send(own, own, S_DA, t, sib)
-        for k, a in zip((4, 6, 2), acc):
-            put_bias(t, k, jnp.sum(a, axis=0, keepdims=True))
+        for k, a in zip((R_GN + 2 * t, R_SF + 2 * t, R_OB + t), acc):
+            put_bias(k, jnp.sum(a, axis=0, keepdims=True))
 
     def attention_back(t):
         T = ROWS[t]
@@ -1052,8 +1151,8 @@
 
         ones = jnp.ones((8, 2 * T), F32).astype(BF)
         sums = nn(ones, QKV[...])[0:1, :]
-        g(B_BG, 0)[t * 16:t * 16 + 1, lane_half] = sums[:, :HALF]
-        g(B_BG, 0)[t * 16 + 1:t * 16 + 2, lane_half] = sums[:, 2 * HALF:]
+        g(B_BG, 0)[R_QB + t:R_QB + t + 1, lane_half] = sums[:, :HALF]
+        g(B_BG, 0)[R_VB + t:R_VB + t + 1, lane_half] = sums[:, 2 * HALF:]
 
         @pl.loop(0, 3)
         def _(j):
@@ -1061,10 +1160,6 @@
             WO[cols, :] = tn(ATT[:, cols], DA[...]).astype(BF)
 
         dst = g(B_GO, t).at[y * 2 + x]
-        for dy in (0, 1):
-            for dx in (0, 1):
-                for dc in (0, 1):
-                    pass
         for xx in (0, 1):
             for cc in (0, 1):
                 src = WO.at[pl.ds((2 * xx + cc) * 96, 96)]
@@ -1077,6 +1172,11 @@
                 @pl.when(dev != s)
                 def _():
                     send(src, dst, S_GO, t, (rep, dev))
+
+        if t == 1:
+            for d in NEIGH:
+                send(g(B_BG, 0), g(B_BGR, 0).at[s], S_BG, 0, (rep, sh(*peer(d))))
+            local(g(B_BG, 0), g(B_BGR, 0).at[s], S_BG, 0)
 
         @pl.loop(0, 3)
         def _(j):
@@ -1112,71 +1212,99 @@
     input_back(0)
     input_back(1)
 
-    for d in NEIGH:
-        send(g(B_BG, 0), g(B_BGR, 0).at[s], S_BG, 0, (rep, sh(*peer(d))))
-    local(g(B_BG, 0), g(B_BGR, 0).at[s], S_BG, 0)
-
-    def sum_dn(t, r0, n):
-        return g(B_WD, t)[pl.ds(mo(x * HALF + r0, 32), n), :].astype(F32) + g(B_GD, t)[pl.ds(r0, n), :].astype(F32)
-
-    def each_dn(t, use):
-        wait(g(B_GD, t), S_GD, t)
-        for r0 in range(0, HALF, 96):
-            use(pl.ds(r0, 96), pl.ds(0, D), sum_dn(t, r0, 96))
-
-    def each_up(t, use):
-        wait(g(B_GU, t), S_GU, t)
-        for yy in (0, 1):
+    def make_dn(t, k):
+        def each(use):
+            if k == 0:
+                wait(g(B_GD, t), S_GD, t)
+            for r0 in (k * 192, k * 192 + 96):
+                own = g(B_WD, t)[pl.ds(mo(x * HALF + r0, 32), 96), :].astype(F32)
+                use(pl.ds(r0, 96), pl.ds(0, D), own + g(B_GD, t)[pl.ds(r0, 96), :].astype(F32))
+        return each
+
+    def make_up(t, yy):
+        GU = g(B_GU, t)
+
+        def each(use):
+            if yy == 0:
+                wait(GU, S_GU, t)
             for cc in (0, 1):
-                both = g(B_GU, t)[sh(yy, 0, cc)].astype(F32) + g(B_GU, t)[sh(yy, 1, cc)].astype(F32)
+                both = GU[sh(yy, 0, cc)].astype(F32) + GU[sh(yy, 1, cc)].astype(F32)
                 for xx in (0, 1):
                     j = 4 * yy + 2 * xx + cc
                     use(pl.ds(0, 96), pl.ds(j * HALF, HALF), both[:, xx * HALF:(xx + 1) * HALF])
-
-    def each_out(t, use):
-        wait(g(B_GO, t), S_GO, t)
-        tot = g(B_GO, t)[0].astype(F32)
-        for k in range(1, 4):
-            tot = tot + g(B_GO, t)[k].astype(F32)
-        use(pl.ds(0, 96), pl.ds(0, D), tot)
-
-    def each_qkv(t, use):
-        wait(g(B_GQ, t), S_GQ, t)
-        for cc in (0, 1):
-            tot = g(B_GQ, t)[cc].astype(F32)
+        return each
+
+    def make_out(t):
+        GO = g(B_GO, t)
+
+        def each(use):
+            wait(GO, S_GO, t)
+            tot = GO[0].astype(F32)
             for k in range(1, 4):
-                tot = tot + g(B_GQ, t)[2 * k + cc].astype(F32)
-            for part in range(3):
-                use(pl.ds(0, 96), pl.ds(part * D + cc * HALF, HALF), tot[:, part * HALF:(part + 1) * HALF])
-
-    def each_small(t, use):
-        wait(g(B_BGR, 0), S_BG, 0)
-        tot = g(B_BGR, 0)[0]
+                tot = tot + GO[k].astype(F32)
+            use(pl.ds(0, 96), pl.ds(0, D), tot)
+        return each
+
+    def make_qkv(t, part):
+        GQ = g(B_GQ, t)
+
+        def each(use):
+            if part == 0:
+                wait(GQ, S_GQ, t)
+            cols = slice(part * HALF, (part + 1) * HALF)
+            for cc in (0, 1):
+                tot = GQ[cc, :, cols].astype(F32)
+                for k in range(1, 4):
+                    tot = tot + GQ[2 * k + cc, :, cols].astype(F32)
+                use(pl.ds(0, 96), pl.ds(part * D + cc * HALF, HALF), tot)
+        return each
+
+    def each_small(use):
+        BGR = g(B_BGR, 0)
+        wait(BGR, S_BG, 0)
+        tot = BGR[0]
         for k in range(1, 8):
-            tot = tot + g(B_BGR, 0)[k]
+            tot = tot + BGR[k]
         use(pl.ds(0, 32), pl.ds(0, D), tot)
 
     is_end = (rep == 0) | (rep == 3)
-    chunks = []
+    units = []
+
+    def unit(kind, t, each, out, rows, cols):
+        if kind == 4:
+            bufs = (B_BGS, B_BGA, B_BGB)
+        else:
+            bufs = (B_ZSD + kind, B_ZAD + kind, B_ZBD + kind)
+        units.append((len(units), tuple(g(b, t) for b in bufs), each, out, rows, cols))
+
+    def add_ffn(t):
+        for k in (0, 1):
+            unit(0, t, make_dn(t, k), o_od.at[t], (192 * k, 192), (0, D))
+        for yy in (0, 1):
+            unit(1, t, make_up(t, yy), o_ou.at[t], (0, 96), (2 * D * yy, 2 * D))
+
+    def add_qkv(t):
+        for part in range(3):
+            unit(3, t, make_qkv(t, part), o_oq.at[t], (0, 96), (part * D, D))
+
+    add_ffn(0)
+    add_ffn(1)
     for t in (0, 1):
-        chunks.append((0, t, each_dn, o_od.at[t]))
-        chunks.append((1, t, each_up, o_ou.at[t]))
-    for t in (0, 1):
-        chunks.append((2, t, each_out, o_oo.at[t]))
-        chunks.append((3, t, each_qkv, o_oq.at[t]))
-    chunks.append((4, 0, each_small, o_obg))
-
-    def zbuf(kind, which, t):
-        if kind == 4:
-            return g((B_BGS, B_BGA, B_BGB)[which], 0)
-        return g((B_ZSD, B_ZAD, B_ZBD)[which] + kind, t)
-
-    def zsem(hop, kind):
-        return (S_ZAS, S_ZBS, S_ZOS)[hop] if kind == 4 else (S_ZAD, S_ZBD, S_ZOD)[hop] + kind
-
-    def stage_a(k):
-        kind, t, each, out = chunks[k]
-        ZS, ZA, ZB = zbuf(kind, 0, t), zbuf(kind, 1, t), zbuf(kind, 2, t)
+        unit(2, t, make_out(t), o_oo.at[t], (0, 96), (0, D))
+        if t == 1:
+            unit(4, 0, each_small, o_obg, (0, 32), (0, D))
+        add_qkv(t)
+    assert len(units) == N_UNITS
+
+    def hop(which, u):
+        at = which * N_UNITS + u[0]
+        return S_Z + at // 2, at % 2
+
+    def view(ref, u):
+        return ref.at[pl.ds(*u[4]), pl.ds(*u[5])]
+
+    def stage_a(u):
+        ZS, ZA, ZB = u[1]
 
         def put(r, cl, val):
             ZS[r, cl] = val.astype(ZS.dtype)
@@ -1187,48 +1315,45 @@
         for end, mid in ((0, 1), (3, 2)):
             @pl.when(rep == end)
             def _():
-                each(t, put)
-                send(ZS, ZA, zsem(0, kind), t, (mid, s))
+                u[2](put)
+                send(view(ZS, u), view(ZA, u), *hop(0, u), (mid, s))
 
             @pl.when(rep == mid)
             def _():
-                wait(ZA, zsem(0, kind), t)
-                each(t, put_add)
-                send(ZS, ZB, zsem(1, kind), t, (3 - mid, s))
-
-    def stage_b(k):
-        kind, t, each, out = chunks[k]
-        ZS, ZB = zbuf(kind, 0, t), zbuf(kind, 2, t)
+                wait(view(ZA, u), *hop(0, u))
+                u[2](put_add)
+                send(view(ZS, u), view(ZB, u), *hop(1, u), (3 - mid, s))
+
+    def stage_b(u):
+        ZS, ZA, ZB = u[1]
         for end, mid in ((0, 1), (3, 2)):
             @pl.when(rep == mid)
             def _():
-                wait(ZB, zsem(1, kind), t)
-                wait(ZB, zsem(1, kind), t, 1)
-                n = ZS.shape[0]
-                for r0 in range(0, n, 32):
-                    r = pl.ds(r0, 32)
-                    ZS[r, :] = (ZS[r, :].astype(F32) + ZB[r, :].astype(F32)).astype(ZS.dtype)
-                send(ZS, out, zsem(2, kind), t, (end, s))
-                local(ZS, out, zsem(2, kind), t)
-
-    for k in range(len(chunks)):
-        stage_a(k)
+                wait(view(ZB, u), *hop(1, u))
+                wait(view(ZB, u), *hop(1, u), 1)
+                for r0 in range(u[4][0], u[4][0] + u[4][1], 32):
+                    r, cl = pl.ds(r0, 32), pl.ds(*u[5])
+                    ZS[r, cl] = (ZS[r, cl].astype(F32) + ZB[r, cl].astype(F32)).astype(ZS.dtype)
+                send(view(ZS, u), view(u[3], u), *hop(2, u), (end, s))
+                local(view(ZS, u), view(u[3], u), *hop(2, u))
+
+    for k, u in enumerate(units):
+        stage_a(u)
         if k:
-            stage_b(k - 1)
-    stage_b(len(chunks) - 1)
-
-    for k in range(len(chunks)):
-        kind, t, each, out = chunks[k]
-        ZS = zbuf(kind, 0, t)
-        wait(ZS, zsem(2, kind), t)
+            stage_b(units[k - 1])
+    stage_b(units[-1])
+
+    for u in units:
+        ZS = view(u[1][0], u)
+        wait(ZS, *hop(2, u))
 
         @pl.when(is_end)
         def _():
-            wait(ZS, zsem(0, kind), t, 1)
+            wait(ZS, *hop(0, u), 1)
 
         @pl.when(jnp.logical_not(is_end))
         def _():
-            wait(ZS, zsem(2, kind), t, 1)
+            wait(ZS, *hop(2, u), 1)
 
     for t in (0, 1):
         gather_sent(t, B_DF, S_DY, S_DC, S_DF)
@@ -1251,9 +1376,10 @@
     wait(g(B_BGR, 0).at[pl.ds(0, 7)], S_BG, 0, 1)
 
 
-def fused_call(x0, x1, cot0, cot1, qkvw, outw, upw, dnw, small, pos, flags, valid):
+def fused_call(*args):
     hbm = pl.BlockSpec(memory_space=pl.ANY)
     vm = pl.BlockSpec(memory_space=pltpu.VMEM)
+    sm = pl.BlockSpec(memory_space=pltpu.SMEM)
     out_shape = [
         jax.ShapeDtypeStruct((8, 128), F32),
         jax.ShapeDtypeStruct((128, D), BF),
@@ -1267,71 +1393,92 @@
         jax.ShapeDtypeStruct((32, D), F32),
     ]
     return pl.pallas_call(
-        functools.partial(fused_kernel, None),
+        fused_kernel,
         out_shape=out_shape,
-        in_specs=[hbm] * 8 + [hbm] + [vm] * 3,
+        in_specs=[hbm] * 8 + [vm] * 6 + [sm] * 2,
         out_specs=[vm] + [hbm] * 9,
         scratch_shapes=[shape for _, shape in scratch_list()] + [pltpu.SemaphoreType.DMA((N_SEMS,))],
         compiler_params=pltpu.CompilerParams(collective_id=0, has_side_effects=True, vmem_limit_bytes=VMEM_LIMIT),
         cost_estimate=pl.CostEstimate(flops=18 * 10**9, bytes_accessed=40 * 10**6, transcendentals=4 * 10**6),
-    )(x0, x1, cot0, cot1, qkvw, outw, upw, dnw, small, pos, flags, valid)
-
-
-def spread(shard, s, n):
-    w = shard.shape[1]
-    place = lax.broadcasted_iota(jnp.int32, (1, n * w), 1) // w == s
-    return jnp.where(place, jnp.tile(shard, (1, n)), jnp.zeros((), BF))
+    )(*args)
+
+
+def widen_kernel(*refs):
+    loss, y0, y1, gx0, gx1, oq, oo, ou, od, bg = refs[:10]
+    r_loss, r_y0, r_y1, r_gx0, r_gx1, r_q, r_qb, r_o, r_ob, r_u, r_ub, r_d, r_db, r_gn, r_sf = refs[10:25]
+    low = refs[25:29]
+    wide = refs[29:33]
+    through = refs[33:37]
+    sem_in, sem_out, sem_move, sem_move_out = refs[37:]
+    s = lax.axis_index("shard")
+    groups = list(zip((oq, ou, od, oo), low, wide, (r_q, r_u, r_d, r_o)))
+    reads, writes, moves = [], [], []
+    for k, (src, lo, hi, dst) in enumerate(groups):
+        for t in (0, 1):
+            reads.append(pltpu.make_async_copy(src.at[t], lo.at[t], sem_in.at[2 * k + t]))
+            reads[-1].start()
+    for k, (src, dst) in enumerate(((y0, r_y0), (y1, r_y1), (gx0, r_gx0), (gx1, r_gx1))):
+        moves.append((pltpu.make_async_copy(src, through[k], sem_move.at[k]),
+                      pltpu.make_async_copy(through[k], dst, sem_move_out.at[k])))
+        moves[-1][0].start()
+    r_loss[...] = loss[0:1, 0:1]
+    first = pltpu.roll(bg[0:16, :], lax.rem(D - 96 * s, D), 1)[:, :96]
+    r_ob[...] = first[0:2, :]
+    r_db[...] = first[2:4, :]
+    for t in (0, 1):
+        r_gn[t] = first[4 + 2 * t:6 + 2 * t, :]
+        r_sf[t] = first[8 + 2 * t:10 + 2 * t, :]
+    second = pltpu.roll(bg[8:16, :], lax.rem(D - 192 * (s % 4), D), 1)[:, :192]
+    r_qb[...] = jnp.where(jnp.full((2, 192), s) < 4, second[4:6, :], second[6:8, :])
+    for t in (0, 1):
+        r_ub[t:t + 1, :] = bg[pl.ds(16 + 4 * t + s // 2, 1), pl.ds(mo((s % 2) * HALF, 128), HALF)]
+    for k, (src, lo, hi, dst) in enumerate(groups):
+        for t in (0, 1):
+            reads[2 * k + t].wait()
+            hi[t] = lo[t].astype(F32)
+            writes.append(pltpu.make_async_copy(hi.at[t], dst.at[t], sem_out.at[2 * k + t]))
+            writes[-1].start()
+    for there, onward in moves:
+        there.wait()
+        onward.start()
+    for copy in writes + [onward for there, onward in moves]:
+        copy.wait()
+
+
+def widen_call(*args):
+    hbm = pl.BlockSpec(memory_space=pl.ANY)
+    vm = pl.BlockSpec(memory_space=pltpu.VMEM)
+
+    def out(dtype, *shape):
+        return jax.ShapeDtypeStruct(shape, dtype)
+
+    shapes = [(2, 96, 3 * D), (2, 96, 4 * D), (2, HALF, D), (2, 96, D)]
+    return pl.pallas_call(
+        widen_kernel,
+        out_shape=[out(F32, 1, 1), out(BF, 128, D), out(BF, 256, D), out(BF, 128, D), out(BF, 256, D),
+                   out(F32, *shapes[0]), out(F32, 2, 192), out(F32, *shapes[3]), out(F32, 2, 96),
+                   out(F32, *shapes[1]), out(F32, 2, HALF), out(F32, *shapes[2]), out(F32, 2, 96),
+                   out(F32, 2, 2, 96), out(F32, 2, 2, 96)],
+        in_specs=[vm] + [hbm] * 8 + [vm],
+        out_specs=[vm, hbm, hbm, hbm, hbm, hbm, vm, hbm, vm, hbm, vm, hbm, vm, vm, vm],
+        scratch_shapes=[pltpu.VMEM(shape, BF) for shape in shapes] + [pltpu.VMEM(shape, F32) for shape in shapes]
+        + [pltpu.VMEM((rows, D), BF) for rows in ROWS * 2]
+        + [pltpu.SemaphoreType.DMA((8,)), pltpu.SemaphoreType.DMA((8,)), pltpu.SemaphoreType.DMA((4,)),
+           pltpu.SemaphoreType.DMA((4,))],
+        compiler_params=pltpu.CompilerParams(vmem_limit_bytes=VMEM_LIMIT),
+    )(*args)
 
 
 def local_fast(query_tokens, passage_tokens, query_cot, passage_cot, bucket_counts, positives, qkv_weight, qv_bias,
                out_weight, out_bias, up_weight, up_bias, down_weight, down_bias, norm_gains, norm_shifts):
-    rep = lax.axis_index("rep")
-    s = lax.axis_index("shard")
-    rows = [
-        spread(qv_bias, s, 8).reshape(2, 2, D),
-        spread(out_bias, s, 8)[:, None],
-        spread(down_bias, s, 8)[:, None],
-        spread(norm_gains[:, 0], s, 8)[:, None],
-        spread(norm_gains[:, 1], s, 8)[:, None],
-        spread(norm_shifts[:, 0], s, 8)[:, None],
-        spread(norm_shifts[:, 1], s, 8)[:, None],
-        spread(up_bias, s, 8).reshape(2, 4, D),
-        jnp.zeros((2, 4, D), BF),
-    ]
-    small = jnp.concatenate(rows, axis=1).reshape(32, D)
-    pos = jnp.concatenate([jnp.broadcast_to(positives.astype(BF)[:, None], (4, 128)), jnp.zeros((12, 128), BF)], axis=0)
-    chip = lax.dynamic_slice(bucket_counts, ((rep * 8 + s) // 2 * 2,), (2,))
-    flags = jnp.broadcast_to((chip > 0).astype(F32)[:, None, None], (2, 8, 128)).reshape(16, 128)
-    slot = lax.iota(jnp.int32, 128)
-    counts = jnp.broadcast_to(bucket_counts[:, None], (32, 4)).reshape(128)
-    valid = jnp.broadcast_to(((counts <= 0) | (slot % 4 == 0)).astype(F32)[None], (8, 128))
-    loss, y0, y1, gx0, gx1, oq, oo, ou, od, bg = fused_call(
+    results = widen_call(*fused_call(
         query_tokens.reshape(128, D), passage_tokens.reshape(256, D),
         query_cot.reshape(128, D), passage_cot.reshape(256, D),
-        qkv_weight, out_weight, up_weight, down_weight, small, pos, flags, valid)
-    bg = bg.reshape(2, 16, D)
-
-    def own(a, w):
-        return lax.dynamic_slice(a, (0, s * w), (2, w))
-
-    def own_pair(a):
-        return lax.dynamic_slice(a, (0, 0, s * 96), (2, 2, 96))
-
-    return (
-        loss[0, 0],
-        y0.reshape(query_tokens.shape), y1.reshape(passage_tokens.shape),
-        gx0.reshape(query_tokens.shape), gx1.reshape(passage_tokens.shape),
-        oq.astype(F32),
-        own(bg[:, 0:2].reshape(2, 2 * D), 192),
-        oo.astype(F32),
-        own(bg[:, 2], 96),
-        ou.astype(F32),
-        own(bg[:, 8:12].reshape(2, 4 * D), HALF),
-        od.astype(F32),
-        own(bg[:, 3], 96),
-        own_pair(bg[:, 4:6]),
-        own_pair(bg[:, 6:8]),
-    )
+        qkv_weight, out_weight, up_weight, down_weight,
+        qv_bias, out_bias, up_bias, down_bias, norm_gains, norm_shifts, bucket_counts, positives))
+    loss, y0, y1, gx0, gx1 = results[:5]
+    return (loss.reshape(()), y0.reshape(query_tokens.shape), y1.reshape(passage_tokens.shape),
+            gx0.reshape(query_tokens.shape), gx1.reshape(passage_tokens.shape), *results[5:])
 
 
 def solution(mesh):

time: 331 us -> 272 us (0.82); the launches traced: 327 us -> 272 us
  Pallas kernels: 301 us -> 271 us
  local copies, waits for them, and re-layouts: 16.5 us -> 0 us
  other arithmetic: 8.97 us -> 0 us
    pallas_call x1 -> x2, Pallas kernels: 301 us -> 271 us  [the longest x1 265 us: fused_call(): pl.pallas_call(fused_kernel, out_shape=out_shape, in_specs=[hbm] * 8 + [v...]
    convert_element_type x7 -> x0, other arithmetic: 8.18 us -> none  [the longest x1 3.03 us: local_fast(): ou.astype(F32)]
    dynamic_slice x6 -> x0, local copies, waits for them, and re-layouts: 3.82 us -> none  [the longest x4 2.52 us: own(): return lax.dynamic_slice(a, (0, s * w), (2, w))]
    another operation x16 -> x0, local copies, waits for them, and re-layouts: 3.33 us -> none  [spread(): return jnp.where(place, jnp.tile(shard, (1, n)), jnp.zeros((), BF))]
where the time goes in v2:
time: 272 us
  Pallas kernels  271 us (100%)
    pallas_call x1, Pallas kernels, fused_call(): pl.pallas_call(fused_kernel, out_shape=out_shape, in_specs=[hbm] * 8 + [v...  265 us
    pallas_call x1, Pallas kernels, widen_call(): pl.pallas_call(widen_kernel, out_shape=[out(F32, 1, 1), out(BF, 128, D),...  6.06 us

profile of v2, /device:TPU:0, one launch (start us, length us, event | category | flops | bytes accessed | tf_op | source)
XLA Modules:
  0.0 271.9 jit_solution(7305014475875669947)
XLA Ops:
  0.7 265.0 %shard_map.271 = (f32[8,128]{1,0:T(8,128)}, bf16[128,768]{1,0:T(8,128)(2,1)}, bf16[256,768]{1,0:T(8,128)(2,1)}, bf16[128,768]{1,0:T(8,128)(2,1)}, bf16[256,768]{...) custom-call(bf16[128,768]{1,0:T(8,128)(2,1)} %bitcast.13, ...), custom_call_target="tpu_custom_call" | custom-call | flops 17999998976 | bytes 40000000 | tf_op jit(solution)/shard_map/pallas_call | solution.py:1395
  265.7 6.1 %shard_map.272 = (f32[1,1]{1,0:T(1,128)}, bf16[128,768]{1,0:T(8,128)(2,1)}, bf16[256,768]{1,0:T(8,128)(2,1)}, bf16[128,768]{1,0:T(8,128)(2,1)}, bf16[256,768]{1,...) custom-call(f32[8,128]{1,0:T(8,128)} %get-tuple-element.40.refs_0_, ...), custom_call_target="tpu_custom_call" | custom-call | tf_op jit(solution)/shard_map/pallas_call | solution.py:1456

commit v3 on v2

--- a/solution.py
+++ b/solution.py
@@ -440,12 +440,17 @@
 D = 768
 HALF = 384
 FFN = 768
+PLAN = [(2, 0, 0),
+        (3, 1, 0), (4, 2, 1), (5, 3, 2), (6, 4, 3), (7, 5, 4), (7, 6, 5),
+        (8, 7, 6), (9, 8, 7), (10, 9, 8), (11, 10, 9), (12, 11, 10), (13, 12, 11),
+        (14, 13, 12),
+        (14, 14, 13), (15, 14, 14), (16, 15, 14), (17, 16, 15), (18, 17, 16), (19, 18, 17)]
 NEIGH = tuple((dy, dx, dc) for dy in (0, 1) for dx in (0, 1) for dc in (0, 1) if dy + dx + dc)
 
-(S_X, S_QKV, S_QKVC, S_QKVZ, S_OUT, S_OUTC, S_OUTZ, S_UP, S_UPC, S_UPZ,
+(S_X, S_QKV, S_QKV1, S_QKV2, S_QKVC, S_QKVZ, S_QKVZ1, S_QKVZ2, S_OUT, S_OUTC, S_OUTZ, S_UP, S_UP1, S_UPC, S_UPZ, S_UPZ1,
  S_DN, S_OP, S_MY, S_MC, S_MF, S_F1A, S_F1B, S_F2, S_DY, S_DC, S_DF, S_D1A, S_D1B, S_D2,
- S_DA, S_DX, S_GD, S_GU, S_GO, S_GQ, S_SMALL, S_CZ, S_CP, S_BG, S_COT, S_FIN, S_FIN2, S_Z) = range(38)
-N_UNITS = 17
+ S_DA, S_DX, S_GD, S_GD1, S_GD2, S_GU, S_GU1, S_GO, S_GQ, S_GQ1, S_GQ2, S_YQ, S_YQ1, S_YQ2, S_SMALL, S_CZ, S_CP, S_BG, S_COT, S_FIN, S_FIN2, S_CF, S_Z) = range(53)
+N_UNITS = 23
 N_SEMS = 4 * S_Z + 6 * N_UNITS + 2
 
 
@@ -469,12 +474,12 @@
     return pl.multiple_of(v, m)
 
 
-(B_X, B_COT, B_WQ, B_WO, B_WU, B_WD, B_QB, B_UB, B_QKV, B_P,
- B_ATT, B_OS, B_OR, B_N1, B_N2, B_R1, B_R2, B_MID, B_ACT, B_SL,
- B_S1, B_V1, B_S2, B_V2, B_KP, B_Y, B_DF, B_DA, B_GD, B_GU,
- B_GO, B_GQ, B_ZSD, B_ZSU, B_ZSO, B_ZSQ, B_ZAD, B_ZAU, B_ZAO, B_ZAQ,
- B_ZBD, B_ZBU, B_ZBO, B_ZBQ, B_T96, B_T192, B_LP, B_SP, B_PV, B_BG, B_BGS, B_BGR, B_BGA,
- B_BGB, B_CM, B_GA, B_CG) = range(57)
+(B_X, B_COT, B_WQ, B_WO, B_WU, B_WD, B_QB, B_UB, B_QKV, B_P, B_ATT, B_OS,
+ B_OR, B_N1, B_N2, B_R1, B_R2, B_MID, B_ACT, B_SL, B_S1, B_V1, B_S2, B_V2,
+ B_KP, B_Y, B_DF, B_DA, B_GD, B_GU, B_GO, B_GQ, B_ZSD, B_ZSU, B_ZSO, B_ZSQ,
+ B_ZAD, B_ZAU, B_ZAO, B_ZAQ, B_ZBD, B_ZBU, B_ZBO, B_ZBQ, B_CLN, B_CLR, B_CLC, B_CLS,
+ B_CLD, B_CLP, B_CFW, B_CF, B_YQ, B_T96, B_SP, B_BGC, B_PV, B_BG, B_BGS, B_BGR,
+ B_BGA, B_BGB, B_CM, B_GA, B_CG, B_DAT) = range(66)
 
 
 def scratch_list():
@@ -512,25 +517,35 @@
         add(B_Y, t, (T, D), BF)
         add(B_DF, t, (4 * T, D), BF)
         add(B_DA, t, (2 * T, D), BF)
+        add(B_DAT, t, (2 * T, HALF), BF)
         add(B_GD, t, (HALF, D), BF)
         add(B_GU, t, (8, 96, FFN), BF)
         add(B_GO, t, (4, 96, D), BF)
-        add(B_GQ, t, (8, 96, 3 * HALF), BF)
+        add(B_GQ, t, (4, 96, 3 * HALF), BF)
+        add(B_YQ, t, (HALF, 3 * HALF), BF)
         for first in (B_ZSD, B_ZAD, B_ZBD):
             add(first, t, (HALF, D), BF)
             add(first + 1, t, (96, 4 * D), BF)
             add(first + 2, t, (96, D), BF)
             add(first + 3, t, (96, 3 * D), BF)
-    add(B_T96, 0, (16, 128), F32)
-    add(B_T192, 0, (8, 256), F32)
-    add(B_LP, 0, (32, D), F32)
-    add(B_SP, 0, (8, 32, D), BF)
+    for t in (0, 1):
+        add(B_CLN, t, (8, D), F32)
+        add(B_CLR, t, (8, 128), F32)
+        add(B_CLC, t, (8, D), F32)
+        add(B_CLS, t, (16, FFN), BF)
+        add(B_CLD, t, (16, D), F32)
+        add(B_CLP, t, (16, FFN), F32)
+    add(B_CFW, 0, (16, D), F32)
+    add(B_CF, 0, (4, 16, D), BF)
+    add(B_T96, 0, (16, HALF), F32)
+    add(B_SP, 0, (8, 16, HALF), BF)
     add(B_PV, 0, (32, D), F32)
     add(B_BG, 0, (32, D), F32)
-    add(B_BGS, 0, (32, D), F32)
-    add(B_BGR, 0, (8, 32, D), F32)
-    add(B_BGA, 0, (32, D), F32)
-    add(B_BGB, 0, (32, D), F32)
+    add(B_BGC, 0, (8, 16, HALF), BF)
+    add(B_BGR, 0, (8, 16, HALF), BF)
+    add(B_BGS, 0, (16, HALF), F32)
+    add(B_BGA, 0, (16, HALF), F32)
+    add(B_BGB, 0, (16, HALF), F32)
     add(B_CM, 0, (16, 512), BF)
     add(B_GA, 0, (32, 16, 512), BF)
     add(B_CG, 0, (2, 16, D), F32)
@@ -583,31 +598,22 @@
     for k in (1, 2, 3):
         pl.semaphore_signal(bar, 1, device_id=((rep + k) % 4, s), device_id_type=MESH)
 
-    T96, T192, LP, SP, PV = (g(b, 0) for b in (B_T96, B_T192, B_LP, B_SP, B_PV))
-    T96[...] = jnp.zeros((16, 128), F32)
-    T192[...] = jnp.zeros((8, 256), F32)
-    LP[...] = jnp.zeros((32, D), F32)
+    T96, SP, PV = (g(b, 0) for b in (B_T96, B_SP, B_PV))
+    T96[...] = jnp.zeros((16, HALF), F32)
     T96[0:2, 0:96] = i_ob[...].astype(F32)
     T96[2:4, 0:96] = i_db[...].astype(F32)
     for t in (0, 1):
         for k in (0, 1):
             T96[4 + 2 * t + k:5 + 2 * t + k, 0:96] = i_gn[t, k:k + 1, :].astype(F32)
             T96[8 + 2 * t + k:9 + 2 * t + k, 0:96] = i_sf[t, k:k + 1, :].astype(F32)
-    T192[0:2, 0:192] = i_qvb[...].astype(F32)
+    T96[0:2, 128:320] = i_qvb[...].astype(F32)
+    T96[12:14, :] = i_ub[...].astype(F32)
+    SP[s] = T96[...].astype(BF)
 
     def place(n, w, at):
         i = lax.broadcasted_iota(jnp.int32, (n, D), 0)
         j = lax.broadcasted_iota(jnp.int32, (n, D), 1)
         return ((j == i + at) & (i < w)).astype(F32).astype(BF)
-
-    LP[0:16, :] = nn(T96[...].astype(BF), place(128, 96, s * 96))
-    qv = nn(T192[...].astype(BF), place(256, 192, (s % 4) * 192))[0:2, :]
-    in_q = jnp.full((2, D), y) == 0
-    LP[12:14, :] = jnp.where(in_q, qv, 0.0)
-    LP[14:16, :] = jnp.where(in_q, 0.0, qv)
-    for t in (0, 1):
-        LP[pl.ds(16 + 4 * t + s // 2, 1), pl.ds(mo((s % 2) * HALF, 128), HALF)] = i_ub[t:t + 1, :].astype(F32)
-    SP[s] = LP[...].astype(BF)
 
     pl.semaphore_wait(bar, 10)
 
@@ -628,12 +634,12 @@
         return pl.ds(mo(owner * 96 + half * 48, 16), 48)
 
     def send_cols(t, src, dst, pieces, far, near):
-        for d in NEIGH + ((0, 0, 0),):
-            p = peer(d)
-            for k, at in enumerate(pieces(p)):
-                cols, to = pl.ds(mo(at, 128), HALF), pl.ds(k * HALF, HALF)
+        for k in range(len(pieces((y, x, c)))):
+            for d in NEIGH + ((0, 0, 0),):
+                p = peer(d)
+                cols, to = pl.ds(mo(pieces(p)[k], 128), HALF), pl.ds(k * HALF, HALF)
                 if d[0] + d[1]:
-                    send(src.at[t, half48, cols], dst.at[rows48(s), to], far, t, (rep, sh(*p)))
+                    send(src.at[t, half48, cols], dst.at[rows48(s), to], far + k, t, (rep, sh(*p)))
                 elif d[2]:
                     send(src.at[t, :, cols], dst.at[rows96, to], near, t, sib)
                 else:
@@ -645,16 +651,15 @@
     def send_up(t):
         send_cols(t, i_upw, g(B_WU, t), lambda p: [HALF * (4 * p[0] + 2 * xx + p[2]) for xx in (0, 1)], S_UP, S_UPC)
 
-    def forward_cols(t, buf, far, pair):
-        wait(buf.at[pl.ds(0, 288)], far, t)
+    def part_of(buf, rows, k):
+        return buf.at[pl.ds(0, rows), pl.ds(k * HALF, HALF)]
+
+    def forward_cols(t, buf, k, far, pair):
+        wait(part_of(buf, 288, k), far + k, t)
         for d in NEIGH:
             if d[0] + d[1]:
-                piece = buf.at[rows48(sh(*peer(d)))]
-                send(piece, piece, pair, t, zpair)
-
-    def whole_cols(t, buf, near, pair):
-        wait(buf.at[pl.ds(0, 192)], near, t)
-        wait(buf.at[pl.ds(0, 288)], pair, t)
+                piece = buf.at[rows48(sh(*peer(d))), pl.ds(k * HALF, HALF)]
+                send(piece, piece, pair + k, t, zpair)
 
     def send_out(t):
         WO = g(B_WO, t)
@@ -720,10 +725,18 @@
         local(cot_in[t], g(B_COT, t), S_COT, 0, t)
 
     wait(SP.at[pl.ds(0, 7)], S_SMALL, 0)
-    tot = SP[0].astype(F32)
-    for k in range(1, 8):
-        tot = tot + SP[k].astype(F32)
-    PV[...] = tot
+    low96 = jnp.zeros((16, D), F32)
+    low192 = [jnp.zeros((16, D), F32) for _ in (0, 1)]
+    for k in range(8):
+        low96 = low96 + nn(SP[k, :, 0:128], place(128, 96, 96 * k))
+        low192[k // 4] = low192[k // 4] + nn(SP[k, :, 128:384], place(256, 192, 192 * (k % 4)))
+    PV[0:16, :] = low96
+    PV[12:14, :] = low192[0][0:2, :]
+    PV[14:16, :] = low192[1][0:2, :]
+    for k in range(8):
+        for t in (0, 1):
+            at, lanes = 16 + 4 * t + k // 2, slice(k % 2 * HALF, (k % 2 + 1) * HALF)
+            PV[at:at + 1, lanes] = SP[k].astype(F32)[12 + t:13 + t, :]
     R_OB, R_DB, R_GN, R_SF, R_QB, R_VB, R_UB = 0, 2, 4, 8, 12, 14, 16
 
     def prow(k):
@@ -762,17 +775,18 @@
 
     CH = 64
 
+    def project(t, k):
+        X, WQ = g(B_X, t), g(B_WQ, t)
+        if k == 0:
+            wait(X, S_X, t)
+            wait(WQ.at[pl.ds(0, 192)], S_QKVC, t)
+        wait(part_of(WQ, 288, k), S_QKVZ + k, t)
+        cols = slice(k * HALF, (k + 1) * HALF)
+        g(B_QKV, t)[:, cols] = (nn(X[...], WQ[:, cols]) + g(B_QB, t)[0:1, cols]).astype(BF)
+
     def attention(t):
         T = ROWS[t]
         X, WQ, QKV, P, ATT = g(B_X, t), g(B_WQ, t), g(B_QKV, t), g(B_P, t), g(B_ATT, t)
-        wait(X, S_X, t)
-        whole_cols(t, WQ, S_QKVC, S_QKVZ)
-
-        @pl.loop(0, 3)
-        def _(j):
-            cols = pl.ds(mo(j * HALF, 128), HALF)
-            QKV[:, cols] = (nn(X[...], WQ[:, cols]) + g(B_QB, t)[0:1, cols]).astype(BF)
-
         @pl.loop(0, 2)
         def _(grp):
             rows = pl.ds(mo(grp * T, 128), T)
@@ -878,10 +892,17 @@
     def ffn(t):
         gather_near(t, B_MID, S_MC)
         gather_forward(t, B_MID, S_MY, S_MF)
-        whole_cols(t, g(B_WU, t), S_UPC, S_UPZ)
+        wait(g(B_WU, t).at[pl.ds(0, 192)], S_UPC, t)
+        for k in (0, 1):
+            wait(part_of(g(B_WU, t), 288, k), S_UPZ + k, t)
         up_pair(t, y)
         gather_far(t, B_MID, S_MF)
         up_pair(t, 1 - y)
+        T = ROWS[t]
+        r = lax.broadcasted_iota(jnp.int32, (16, 4 * T), 0)
+        j = lax.broadcasted_iota(jnp.int32, (16, 4 * T), 1)
+        at_cls = (j == (r >> 2) * T + (r & 3) * (32, 64)[t]).astype(F32).astype(BF)
+        g(B_CLS, t)[...] = nn(at_cls, g(B_SL, t)[...]).astype(BF)
         wait(g(B_WD, t), S_DN, t)
         scatter_partial(t, lambda rows: nn(g(B_ACT, t)[rows, :], g(B_WD, t)[...]), S_F1A, S_F1B, S_F2)
 
@@ -902,19 +923,158 @@
 
         local(g(B_Y, t), (o_y0, o_y1)[t], S_FIN, 0, t)
 
-    forward_cols(1, g(B_WQ, 1), S_QKV, S_QKVZ)
+    def forward_qkv(t, k):
+        forward_cols(t, g(B_WQ, t), k, S_QKV, S_QKVZ)
+
+    def forward_up(t):
+        for k in (0, 1):
+            forward_cols(t, g(B_WU, t), k, S_UP, S_UPZ)
+
+    for k in range(3):
+        forward_qkv(1, k)
     forward_out(1)
-    forward_cols(0, g(B_WQ, 0), S_QKV, S_QKVZ)
+    for k in range(3):
+        project(1, k)
+        forward_qkv(0, k)
     attention(1)
     send_up(0)
     send_dn(0)
     forward_out(0)
-    forward_cols(1, g(B_WU, 1), S_UP, S_UPZ)
+    forward_up(1)
+    for k in range(3):
+        project(0, k)
     attention(0)
-    forward_cols(0, g(B_WU, 0), S_UP, S_UPZ)
+    forward_up(0)
+    def fold(a):
+        return jnp.sum(a.reshape(CH // 8, 8, D), axis=0)
+
+    def put_bias(k, row):
+        g(B_BG, 0)[k:k + 1, :] = row
+
+    def ln_back(t, din, nrm, inv, gain):
+        gg = din * gain
+        m1 = jnp.mean(gg, axis=-1, keepdims=True)
+        m2 = jnp.mean(gg * nrm, axis=-1, keepdims=True)
+        return inv * (gg - m1 - nrm * m2)
+
+    steps = (32, 64)
+
+    def out_back(t):
+        T = ROWS[t]
+        wait(g(B_COT, t), S_COT, 0, t)
+        for i in range(4):
+            row = slice(i * steps[t], i * steps[t] + 1)
+            g(B_CLN, t)[i:i + 1, :] = g(B_N2, t)[row, :]
+            g(B_CLR, t)[i:i + 1, :] = g(B_R2, t)[row, :]
+            g(B_CLC, t)[i:i + 1, :] = g(B_COT, t)[row, :].astype(F32)
+        gain = prow(R_GN + 2 * t + 1)
+        me4 = (2 * y + c) * T
+        zero = jnp.zeros((8, D), F32)
+
+        def body(i, acc):
+            r = pl.ds(mo(i * CH, CH), CH)
+            dout = g(B_COT, t)[r, :].astype(F32)
+            nrm = g(B_N2, t)[r, :]
+            dsec = ln_back(t, dout, nrm, g(B_R2, t)[r, 0:1], gain)
+            g(B_N2, t)[r, :] = dsec
+            g(B_DF, t)[pl.ds(mo(me4 + i * CH, CH), CH), :] = dsec.astype(BF)
+            return (acc[0] + fold(dout * nrm), acc[1] + fold(dout))
+
+        acc = lax.fori_loop(0, T // CH, body, (zero, zero))
+        for k, a in zip((R_GN + 2 * t + 1, R_SF + 2 * t + 1), acc):
+            put_bias(k, jnp.sum(a, axis=0, keepdims=True))
+
+    def cls_back(t):
+        dcls = g(B_CG, 0)[t, 0:4, :]
+        nrm = g(B_CLN, t)[0:4, :]
+        dsec = ln_back(t, g(B_CLC, t)[0:4, :] + dcls, nrm, g(B_CLR, t)[0:4, 0:1], prow(R_GN + 2 * t + 1))
+        for i in range(4):
+            g(B_N2, t)[i * steps[t]:i * steps[t] + 1, :] = dsec[i:i + 1, :]
+        g(B_CFW, 0)[4 * t:4 * t + 4, :] = dsec
+        for k, a in ((R_GN + 2 * t + 1, dcls * nrm), (R_SF + 2 * t + 1, dcls)):
+            put_bias(k, g(B_BG, 0)[k:k + 1, :] + jnp.sum(a, axis=0, keepdims=True))
+
+    def cls_place(t):
+        T = ROWS[t]
+        r = lax.broadcasted_iota(jnp.int32, (16, 64), 0)
+        j = lax.broadcasted_iota(jnp.int32, (16, 64), 1)
+        which = (j == (r >> 2) * 16 + 4 * t + (r & 3)).astype(F32).astype(BF)
+        rows = nn(which, g(B_CF, 0)[...].reshape(64, D))
+        g(B_CLD, t)[...] = rows
+        da = nt(rows.astype(BF), g(B_WD, t)[...])
+        g(B_CLP, t)[...] = da * g(B_CLS, t)[...].astype(F32)
+        top = lax.broadcasted_iota(jnp.int32, (16, 1), 0) == 0
+        for slot in range(4):
+            for i in range(4):
+                tile = pl.ds(slot * T + i * steps[t], 16)
+                k = slot * 4 + i
+                for buf, new in ((g(B_DF, t), g(B_CLD, t)), (g(B_SL, t), g(B_CLP, t))):
+                    buf[tile, :] = jnp.where(top, new[k:k + 1, :], buf[tile, :].astype(F32)).astype(BF)
+
+    def down_pair(t, yy):
+        T = ROWS[t]
+        rows = pl.ds(mo(2 * yy * T, 128), 2 * T)
+
+        @pl.loop(0, 3)
+        def _(j):
+            cols = pl.ds(mo(j * 256, 128), 256)
+            da = nt(g(B_DF, t)[rows, :], g(B_WD, t)[cols, :])
+            g(B_SL, t)[rows, cols] = (da * g(B_SL, t)[rows, cols].astype(F32)).astype(BF)
+
+    def pre_back(t):
+        gather_near(t, B_DF, S_DC)
+        gather_forward(t, B_DF, S_DY, S_DF)
+        down_pair(t, y)
+        gather_far(t, B_DF, S_DF)
+        down_pair(t, 1 - y)
+
+    def ffn_back(t):
+        gather_sent(t, B_DF, S_DY, S_DC, S_DF)
+        cls_place(t)
+        ACT, DF, WD, WU = g(B_ACT, t), g(B_DF, t), g(B_WD, t), g(B_WU, t)
+        for k in range(3):
+            cols = pl.ds(mo((1 - x) * HALF + 128 * k, 128), 128)
+            WD[cols, :] = tn(ACT[:, cols], DF[...]).astype(BF)
+            send(WD.at[cols], g(B_GD, t).at[pl.ds(128 * k, 128)], S_GD + k, t, xpeer)
+
+        scatter_partial(t, lambda rows: nt(g(B_SL, t)[rows, :], g(B_WU, t)[...]), S_D1A, S_D1B, S_D2)
+        own_sum = nn(jnp.ones((8, ROWS[t]), F32).astype(BF), g(B_DF, t)[slot_rows(t, y, c), :])
+        put_bias(R_DB + t, own_sum[0:1, :])
+        ones = jnp.ones((8, 4 * ROWS[t]), F32).astype(BF)
+        sums = nn(ones, g(B_SL, t)[...])[0:1, :]
+        for xx in (0, 1):
+            part = sums[:, xx * HALF:(xx + 1) * HALF]
+            at = R_UB + 4 * t + xx
+
+            @pl.when(y == 0)
+            def _():
+                g(B_BG, 0)[at:at + 1, lane_half] = part
+
+            @pl.when(y == 1)
+            def _():
+                g(B_BG, 0)[at + 2:at + 3, lane_half] = part
+
+        cols = pl.ds(mo(x * HALF, 128), HALF)
+        WD[cols, :] = tn(ACT[:, cols], DF[...]).astype(BF)
+        for dy in (1, 0):
+            @pl.loop(0, 3)
+            def _(j):
+                cols = pl.ds(mo(flip(y, dy) * HALF + j * 128, 128), 128)
+                WU[cols, :] = tn(g(B_MID, t)[:, cols], g(B_SL, t)[...]).astype(BF)
+
+            for d in NEIGH:
+                if d[0] == dy:
+                    dest = sh(*peer(d))
+                    send(WU.at[pl.ds(mo(96 * dest, 32), 96)], g(B_GU, t).at[s], S_GU1 - dy, t, (rep, dest))
+        local(WU.at[rows96], g(B_GU, t).at[s], S_GU1, t)
+
+    g(B_BG, 0)[...] = jnp.zeros((32, D), F32)
+    g(B_CFW, 0)[...] = jnp.zeros((16, D), F32)
     ffn(1)
     ffn(0)
     ffn_end(1)
+    out_back(1)
+    gather_rows(1, B_DF, S_DY, S_DC, S_DF)
     ffn_end(0)
 
     def pick(T, lo, step):
@@ -934,18 +1094,21 @@
     for k in (1, 2, 3):
         send(g(B_CM, 0), mine, S_CZ, 0, ((rep + k) % 4, s))
     g(B_GA, 0)[s * 4 + rep] = g(B_CM, 0)[...]
+    out_back(0)
     wait(g(B_GA, 0).at[pl.ds(0, 3)], S_CZ, 0)
     four = g(B_GA, 0).at[pl.ds(s * 4, 4)]
     for d in NEIGH:
         send(four, four, S_CP, 0, (rep, sh(*peer(d))))
+    gather_rows(0, B_DF, S_DY, S_DC, S_DF)
 
     for t in (0, 1):
         own = g(B_X, t).at[pl.ds(mo(c * ROWS[t], 128), ROWS[t])]
         wait(own, S_X, t, 1)
-        for buf, far, near, pair in ((g(B_WQ, t), S_QKV, S_QKVC, S_QKVZ), (g(B_WU, t), S_UP, S_UPC, S_UPZ)):
-            wait(buf.at[pl.ds(0, 288)], far, t, 1)
+        for buf, n, far, near, pair in ((g(B_WQ, t), 3, S_QKV, S_QKVC, S_QKVZ), (g(B_WU, t), 2, S_UP, S_UPC, S_UPZ)):
             wait(buf.at[pl.ds(0, 96)], near, t, 1)
-            wait(buf.at[pl.ds(0, 288)], pair, t, 1)
+            for k in range(n):
+                wait(part_of(buf, 288, k), far + k, t, 1)
+                wait(part_of(buf, 288, k), pair + k, t, 1)
         wait(g(B_WO, t).at[pl.ds(0, 144)], S_OUT, t, 1)
 
         @pl.when(c == y)
@@ -961,10 +1124,9 @@
         wait(g(B_OS, t), S_OP, t, 1)
         gather_sent(t, B_MID, S_MY, S_MC, S_MF)
         scatter_sent(t, S_F1A, S_F1B, S_F2)
-        wait(g(B_COT, t), S_COT, 0, t)
     wait(g(B_SP, 0).at[pl.ds(0, 7)], S_SMALL, 0, 1)
     wait(g(B_GA, 0).at[pl.ds(0, 3)], S_CZ, 0, 1)
-    g(B_BG, 0)[...] = jnp.zeros((32, D), F32)
+    pre_back(1)
 
     wait(g(B_GA, 0).at[pl.ds(0, 28)], S_CP, 0)
     wait(g(B_GA, 0).at[pl.ds(0, 28)], S_CP, 0, 1)
@@ -1008,92 +1170,6 @@
     g(B_CG, 0)[1, :, :HALF] = nn(dlp, qa) * scale
     g(B_CG, 0)[1, :, HALF:] = nn(dlp, qb) * scale
 
-    def fold(a):
-        return jnp.sum(a.reshape(CH // 8, 8, D), axis=0)
-
-    def put_bias(k, row):
-        g(B_BG, 0)[k:k + 1, :] = row
-
-    def ln_back(t, din, nrm, inv, gain):
-        gg = din * gain
-        m1 = jnp.mean(gg, axis=-1, keepdims=True)
-        m2 = jnp.mean(gg * nrm, axis=-1, keepdims=True)
-        return inv * (gg - m1 - nrm * m2)
-
-    def out_back(t):
-        T = ROWS[t]
-        step = 32 if t == 0 else 64
-        KP = g(B_KP, t)
-        KP[0] = g(B_COT, t)[...].astype(F32)
-        for i in range(4):
-            KP[0, i * step:i * step + 1, :] = KP[0, i * step:i * step + 1, :] + g(B_CG, 0)[t, i:i + 1, :]
-        gain = prow(R_GN + 2 * t + 1)
-        me4 = (2 * y + c) * T
-        zero = jnp.zeros((8, D), F32)
-
-        def body(i, acc):
-            r = pl.ds(mo(i * CH, CH), CH)
-            dout = KP[0, r, :]
-            nrm = g(B_N2, t)[r, :]
-            dsec = ln_back(t, dout, nrm, g(B_R2, t)[r, 0:1], gain)
-            low = dsec.astype(BF)
-            g(B_N2, t)[r, :] = dsec
-            g(B_DF, t)[pl.ds(mo(me4 + i * CH, CH), CH), :] = low
-            return (acc[0] + fold(dout * nrm), acc[1] + fold(dout), acc[2] + fold(low.astype(F32)))
-
-        acc = lax.fori_loop(0, T // CH, body, (zero, zero, zero))
-        gather_rows(t, B_DF, S_DY, S_DC, S_DF)
-        for k, a in zip((R_GN + 2 * t + 1, R_SF + 2 * t + 1, R_DB + t), acc):
-            put_bias(k, jnp.sum(a, axis=0, keepdims=True))
-
-    def down_pair(t, yy):
-        T = ROWS[t]
-        rows = pl.ds(mo(2 * yy * T, 128), 2 * T)
-
-        @pl.loop(0, 3)
-        def _(j):
-            cols = pl.ds(mo(j * 256, 128), 256)
-            da = nt(g(B_DF, t)[rows, :], g(B_WD, t)[cols, :])
-            g(B_SL, t)[rows, cols] = (da * g(B_SL, t)[rows, cols].astype(F32)).astype(BF)
-
-    def ffn_back(t):
-        gather_near(t, B_DF, S_DC)
-        gather_forward(t, B_DF, S_DY, S_DF)
-        down_pair(t, y)
-        gather_far(t, B_DF, S_DF)
-        down_pair(t, 1 - y)
-        scatter_partial(t, lambda rows: nt(g(B_SL, t)[rows, :], g(B_WU, t)[...]), S_D1A, S_D1B, S_D2)
-        ones = jnp.ones((8, 4 * ROWS[t]), F32).astype(BF)
-        sums = nn(ones, g(B_SL, t)[...])[0:1, :]
-        for xx in (0, 1):
-            part = sums[:, xx * HALF:(xx + 1) * HALF]
-            at = R_UB + 4 * t + xx
-
-            @pl.when(y == 0)
-            def _():
-                g(B_BG, 0)[at:at + 1, lane_half] = part
-
-            @pl.when(y == 1)
-            def _():
-                g(B_BG, 0)[at + 2:at + 3, lane_half] = part
-
-        @pl.loop(0, 3)
-        def _(j):
-            cols = pl.ds(mo(j * 256, 128), 256)
-            g(B_WD, t)[cols, :] = tn(g(B_ACT, t)[:, cols], g(B_DF, t)[...]).astype(BF)
-
-        send(g(B_WD, t).at[pl.ds(mo((1 - x) * HALF, 128), HALF)], g(B_GD, t), S_GD, t, xpeer)
-
-        @pl.loop(0, 3)
-        def _(j):
-            cols = pl.ds(mo(j * 256, 128), 256)
-            g(B_WU, t)[cols, :] = tn(g(B_MID, t)[:, cols], g(B_SL, t)[...]).astype(BF)
-
-        for d in NEIGH:
-            p = peer(d)
-            send(g(B_WU, t).at[pl.ds(mo(96 * sh(*p), 32), 96)], g(B_GU, t).at[s], S_GU, t, (rep, sh(*p)))
-        local(g(B_WU, t).at[rows96], g(B_GU, t).at[s], S_GU, t)
-
     def mid_back(t):
         T = ROWS[t]
         scatter_finish(t, S_D1B, S_D2)
@@ -1116,19 +1192,41 @@
         for k, a in zip((R_GN + 2 * t, R_SF + 2 * t, R_OB + t), acc):
             put_bias(k, jnp.sum(a, axis=0, keepdims=True))
 
-    def attention_back(t):
+    def attention_back(t, point):
         T = ROWS[t]
         QKV, P, ATT, DA, WO, WQ = g(B_QKV, t), g(B_P, t), g(B_ATT, t), g(B_DA, t), g(B_WO, t), g(B_WQ, t)
         wait(DA.at[pl.ds(mo((1 - c) * T, 128), T)], S_DA, t)
 
-        @pl.loop(0, 2)
-        def _(grp):
-            rows = pl.ds(mo(grp * T, 128), T)
+        DAT = g(B_DAT, t)
+        DAT[...] = nt(DA[...], WO[...]).astype(BF)
+
+        @pl.loop(0, 3)
+        def _(j):
+            cols = pl.ds(mo(j * 128, 128), 128)
+            WO[cols, :] = tn(ATT[:, cols], DA[...]).astype(BF)
+
+        dst = g(B_GO, t).at[y * 2 + x]
+        for xx in (0, 1):
+            for cc in (0, 1):
+                src = WO.at[pl.ds((2 * xx + cc) * 96, 96)]
+                dev = sh(c, xx, cc)
+
+                @pl.when(dev == s)
+                def _():
+                    local(src, dst, S_GO, t)
+
+                @pl.when(dev != s)
+                def _():
+                    send(src, dst, S_GO, t, (rep, dev))
+
+        point()
+        for grp in (0, 1):
+            rows = pl.ds(grp * T, T)
 
             @pl.loop(0, 3)
             def _(hp):
                 lanes = pl.ds(mo(hp * 128, 128), 128)
-                dat = nt(DA[rows, :], WO[lanes, :]).astype(BF)
+                dat = DAT[rows, lanes]
                 qs, ks = lanes, pl.ds(mo(HALF + hp * 128, 128), 128)
                 vs = pl.ds(mo(2 * HALF + hp * 128, 128), 128)
                 q, k, val = QKV[rows, qs], QKV[rows, ks], QKV[rows, vs]
@@ -1145,6 +1243,8 @@
                 QKV[rows, ks] = (jnp.where(lane_lo, dk[0], dk[1]) * root).astype(BF)
                 QKV[rows, vs] = jnp.where(lane_lo, dv[0], dv[1]).astype(BF)
 
+            point()
+
         g(B_OS, t)[...] = nt(QKV[pl.ds(mo((1 - c) * T, 128), T), :], WQ[...]).astype(BF)
         send(g(B_OS, t), g(B_OR, t), S_DX, t, sib)
         g(B_KP, t)[0] = nt(QKV[pl.ds(mo(c * T, 128), T), :], WQ[...])
@@ -1154,39 +1254,51 @@
         g(B_BG, 0)[R_QB + t:R_QB + t + 1, lane_half] = sums[:, :HALF]
         g(B_BG, 0)[R_VB + t:R_VB + t + 1, lane_half] = sums[:, 2 * HALF:]
 
-        @pl.loop(0, 3)
-        def _(j):
-            cols = pl.ds(mo(j * 128, 128), 128)
-            WO[cols, :] = tn(ATT[:, cols], DA[...]).astype(BF)
-
-        dst = g(B_GO, t).at[y * 2 + x]
-        for xx in (0, 1):
-            for cc in (0, 1):
-                src = WO.at[pl.ds((2 * xx + cc) * 96, 96)]
-                dev = sh(c, xx, cc)
-
-                @pl.when(dev == s)
-                def _():
-                    local(src, dst, S_GO, t)
-
-                @pl.when(dev != s)
-                def _():
-                    send(src, dst, S_GO, t, (rep, dev))
-
-        if t == 1:
-            for d in NEIGH:
-                send(g(B_BG, 0), g(B_BGR, 0).at[s], S_BG, 0, (rep, sh(*peer(d))))
-            local(g(B_BG, 0), g(B_BGR, 0).at[s], S_BG, 0)
-
-        @pl.loop(0, 3)
-        def _(j):
-            cols = pl.ds(mo(j * 256, 128), 256)
-            WQ[cols, :] = tn(g(B_X, t)[:, cols], QKV[...]).astype(BF)
-
+        if t == 0:
+            send_small()
+        far_rows = pl.ds(mo((1 - y) * HALF, 128), HALF)
+        for k in range(3):
+            lanes = slice(k * HALF, (k + 1) * HALF)
+
+            @pl.loop(0, 3)
+            def _(j):
+                cols = pl.ds(mo(j * 256, 128), 256)
+                WQ[cols, lanes] = tn(g(B_X, t)[:, cols], QKV[:, lanes]).astype(BF)
+
+            send(WQ.at[far_rows, pl.ds(k * HALF, HALF)], g(B_YQ, t).at[:, pl.ds(k * HALF, HALF)], S_YQ + k, t, ypeer)
+            point()
+
+    def send_small():
+        BG, BGC, BGR = (g(b, 0) for b in (B_BG, B_BGC, B_BGR))
+        low = BG[...].astype(BF)
+        for k in range(8):
+            T96[...] = jnp.zeros((16, HALF), F32)
+            T96[:, 0:128] = nt(low[0:16, :], place(128, 96, 96 * k))
+            at = 12 + 2 * (k // 4)
+            T96[0:2, 128:384] = nt(low[0:16, :], place(256, 192, 192 * (k % 4)))[at:at + 2, :]
+            for t in (0, 1):
+                row = 16 + 4 * t + k // 2
+                T96[12 + t:13 + t, :] = BG[row:row + 1, k % 2 * HALF:(k % 2 + 1) * HALF]
+            BGC[k] = T96[...].astype(BF)
         for d in NEIGH:
-            p = peer(d)
-            send(WQ.at[pl.ds(mo(96 * sh(*p), 32), 96)], g(B_GQ, t).at[s], S_GQ, t, (rep, sh(*p)))
-        local(WQ.at[rows96], g(B_GQ, t).at[s], S_GQ, t)
+            dest = sh(*peer(d))
+            send(BGC.at[dest], BGR.at[s], S_BG, 0, (rep, dest))
+        local(BGC.at[s], BGR.at[s], S_BG, 0)
+
+    def relay_qkv(t, k):
+        WQ, YQ, lanes = g(B_WQ, t), g(B_YQ, t), pl.ds(k * HALF, HALF)
+        wait(YQ.at[:, lanes], S_YQ + k, t)
+        for r0 in range(0, HALF, 128):
+            r = pl.ds(mo(y * HALF + r0, 128), 128)
+            WQ[r, lanes] = (WQ[r, lanes].astype(F32) + YQ[pl.ds(r0, 128), lanes].astype(F32)).astype(BF)
+        dst = g(B_GQ, t).at[2 * x + c, :, lanes]
+        for dx, dc in ((1, 0), (1, 1), (0, 1), (0, 0)):
+            owner = sh(y, flip(x, dx), flip(c, dc))
+            src = WQ.at[pl.ds(mo(96 * owner, 32), 96), lanes]
+            if dx + dc:
+                send(src, dst, S_GQ + k, t, (rep, owner))
+            else:
+                local(src, dst, S_GQ + k, t)
 
     def input_back(t):
         T = ROWS[t]
@@ -1199,39 +1311,25 @@
 
         local(g(B_Y, t), (o_gx0, o_gx1)[t], S_FIN2, 0, t)
 
-    out_back(0)
-    out_back(1)
-    for t in (0, 1):
-        wait(g(B_Y, t), S_FIN, 0, t)
-    ffn_back(0)
-    ffn_back(1)
-    mid_back(0)
-    mid_back(1)
-    attention_back(0)
-    attention_back(1)
-    input_back(0)
-    input_back(1)
-
     def make_dn(t, k):
         def each(use):
-            if k == 0:
-                wait(g(B_GD, t), S_GD, t)
-            for r0 in (k * 192, k * 192 + 96):
-                own = g(B_WD, t)[pl.ds(mo(x * HALF + r0, 32), 96), :].astype(F32)
-                use(pl.ds(r0, 96), pl.ds(0, D), own + g(B_GD, t)[pl.ds(r0, 96), :].astype(F32))
+            wait(g(B_GD, t).at[pl.ds(128 * k, 128)], S_GD + k, t)
+            for r0 in (128 * k, 128 * k + 64):
+                own = g(B_WD, t)[pl.ds(mo(x * HALF + r0, 64), 64), :].astype(F32)
+                use(pl.ds(r0, 64), pl.ds(0, D), own + g(B_GD, t)[pl.ds(r0, 64), :].astype(F32))
         return each
 
-    def make_up(t, yy):
+    def make_up(t, dy, xx):
         GU = g(B_GU, t)
+        yy = flip(y, dy)
 
         def each(use):
-            if yy == 0:
-                wait(GU, S_GU, t)
+            if xx == 0:
+                wait(GU.at[pl.ds(0, 4)], S_GU1 - dy, t)
+            cols = slice(xx * HALF, (xx + 1) * HALF)
             for cc in (0, 1):
-                both = GU[sh(yy, 0, cc)].astype(F32) + GU[sh(yy, 1, cc)].astype(F32)
-                for xx in (0, 1):
-                    j = 4 * yy + 2 * xx + cc
-                    use(pl.ds(0, 96), pl.ds(j * HALF, HALF), both[:, xx * HALF:(xx + 1) * HALF])
+                both = GU[sh(yy, 0, cc), :, cols].astype(F32) + GU[sh(yy, 1, cc), :, cols].astype(F32)
+                use(pl.ds(0, 96), pl.ds(mo((4 * yy + 2 * xx + cc) * HALF, 128), HALF), both)
         return each
 
     def make_out(t):
@@ -1249,23 +1347,20 @@
         GQ = g(B_GQ, t)
 
         def each(use):
-            if part == 0:
-                wait(GQ, S_GQ, t)
             cols = slice(part * HALF, (part + 1) * HALF)
+            wait(GQ.at[:, :, pl.ds(part * HALF, HALF)], S_GQ + part, t)
             for cc in (0, 1):
-                tot = GQ[cc, :, cols].astype(F32)
-                for k in range(1, 4):
-                    tot = tot + GQ[2 * k + cc, :, cols].astype(F32)
+                tot = GQ[cc, :, cols].astype(F32) + GQ[2 + cc, :, cols].astype(F32)
                 use(pl.ds(0, 96), pl.ds(part * D + cc * HALF, HALF), tot)
         return each
 
     def each_small(use):
         BGR = g(B_BGR, 0)
         wait(BGR, S_BG, 0)
-        tot = BGR[0]
+        tot = BGR[0].astype(F32)
         for k in range(1, 8):
-            tot = tot + BGR[k]
-        use(pl.ds(0, 32), pl.ds(0, D), tot)
+            tot = tot + BGR[k].astype(F32)
+        use(pl.ds(0, 16), pl.ds(0, HALF), tot)
 
     is_end = (rep == 0) | (rep == 3)
     units = []
@@ -1278,22 +1373,24 @@
         units.append((len(units), tuple(g(b, t) for b in bufs), each, out, rows, cols))
 
     def add_ffn(t):
-        for k in (0, 1):
-            unit(0, t, make_dn(t, k), o_od.at[t], (192 * k, 192), (0, D))
-        for yy in (0, 1):
-            unit(1, t, make_up(t, yy), o_ou.at[t], (0, 96), (2 * D * yy, 2 * D))
+        for k in range(3):
+            unit(0, t, make_dn(t, k), o_od.at[t], (128 * k, 128), (0, D))
+        for dy in (1, 0):
+            for xx in (0, 1):
+                at = mo((2 * flip(y, dy) + xx) * D, 128)
+                unit(1, t, make_up(t, dy, xx), o_ou.at[t], (0, 96), (at, D))
 
     def add_qkv(t):
         for part in range(3):
             unit(3, t, make_qkv(t, part), o_oq.at[t], (0, 96), (part * D, D))
 
+    add_ffn(1)
     add_ffn(0)
-    add_ffn(1)
-    for t in (0, 1):
-        unit(2, t, make_out(t), o_oo.at[t], (0, 96), (0, D))
-        if t == 1:
-            unit(4, 0, each_small, o_obg, (0, 32), (0, D))
-        add_qkv(t)
+    unit(2, 1, make_out(1), o_oo.at[1], (0, 96), (0, D))
+    unit(2, 0, make_out(0), o_oo.at[0], (0, 96), (0, D))
+    add_qkv(1)
+    unit(4, 0, each_small, o_obg, (0, 16), (0, HALF))
+    add_qkv(0)
     assert len(units) == N_UNITS
 
     def hop(which, u):
@@ -1303,14 +1400,11 @@
     def view(ref, u):
         return ref.at[pl.ds(*u[4]), pl.ds(*u[5])]
 
-    def stage_a(u):
+    def ends(u):
         ZS, ZA, ZB = u[1]
 
         def put(r, cl, val):
             ZS[r, cl] = val.astype(ZS.dtype)
-
-        def put_add(r, cl, val):
-            ZS[r, cl] = (val + ZA[r, cl].astype(F32)).astype(ZS.dtype)
 
         for end, mid in ((0, 1), (3, 2)):
             @pl.when(rep == end)
@@ -1318,6 +1412,13 @@
                 u[2](put)
                 send(view(ZS, u), view(ZA, u), *hop(0, u), (mid, s))
 
+    def stage_a(u):
+        ZS, ZA, ZB = u[1]
+
+        def put_add(r, cl, val):
+            ZS[r, cl] = (val + ZA[r, cl].astype(F32)).astype(ZS.dtype)
+
+        for end, mid in ((0, 1), (3, 2)):
             @pl.when(rep == mid)
             def _():
                 wait(view(ZA, u), *hop(0, u))
@@ -1331,17 +1432,53 @@
             def _():
                 wait(view(ZB, u), *hop(1, u))
                 wait(view(ZB, u), *hop(1, u), 1)
-                for r0 in range(u[4][0], u[4][0] + u[4][1], 32):
-                    r, cl = pl.ds(r0, 32), pl.ds(*u[5])
+                for r0 in range(u[4][0], u[4][0] + u[4][1], 16):
+                    r, cl = pl.ds(r0, 16), pl.ds(*u[5])
                     ZS[r, cl] = (ZS[r, cl].astype(F32) + ZB[r, cl].astype(F32)).astype(ZS.dtype)
                 send(view(ZS, u), view(u[3], u), *hop(2, u), (end, s))
                 local(view(ZS, u), view(u[3], u), *hop(2, u))
 
-    for k, u in enumerate(units):
-        stage_a(u)
-        if k:
-            stage_b(units[k - 1])
-    stage_b(units[-1])
+    done = [0, 0, 0]
+
+    def advance(n0, n1, n2):
+        while done[0] < n0 or done[1] < n1 or done[2] < n2:
+            for k, (step, n) in enumerate(((ends, n0), (stage_a, n1), (stage_b, n2))):
+                if done[k] < n:
+                    step(units[done[k]])
+                    done[k] += 1
+
+    cls_back(1)
+    cls_back(0)
+    mine = g(B_CF, 0).at[2 * y + c]
+    g(B_CF, 0)[2 * y + c] = g(B_CFW, 0)[...].astype(BF)
+    fixers = (ypeer, sib, (rep, sh(1 - y, x, 1 - c)))
+    for dev in fixers:
+        send(mine, mine, S_CF, 0, dev)
+    pre_back(0)
+    wait(g(B_CF, 0).at[pl.ds(0, 3)], S_CF, 0)
+    for t in (0, 1):
+        wait(g(B_Y, t), S_FIN, 0, t)
+    ffn_back(1)
+    ffn_back(0)
+    def point():
+        advance(*plan.pop(0))
+
+    plan = PLAN[:]
+    point()
+    mid_back(1)
+    attention_back(1, point)
+    mid_back(0)
+    attention_back(0, point)
+    input_back(1)
+    input_back(0)
+    point()
+    for t in (1, 0):
+        for k in range(3):
+            relay_qkv(t, k)
+            point()
+    for k in range(done[0], N_UNITS + 1):
+        advance(min(k + 1, N_UNITS), k, k - 1)
+    advance(N_UNITS, N_UNITS, N_UNITS)
 
     for u in units:
         ZS = view(u[1][0], u)
@@ -1356,12 +1493,13 @@
             wait(ZS, *hop(2, u), 1)
 
     for t in (0, 1):
-        gather_sent(t, B_DF, S_DY, S_DC, S_DF)
         scatter_sent(t, S_D1A, S_D1B, S_D2)
         wait(g(B_OS, t), S_DA, t, 1)
         wait(g(B_OS, t), S_DX, t, 1)
-        wait(g(B_GD, t), S_GD, t, 1)
-        wait(g(B_GU, t).at[pl.ds(0, 7)], S_GU, t, 1)
+        for k in range(3):
+            wait(g(B_GD, t).at[pl.ds(0, 128)], S_GD + k, t, 1)
+        wait(g(B_GU, t).at[pl.ds(0, 4)], S_GU, t, 1)
+        wait(g(B_GU, t).at[pl.ds(0, 3)], S_GU1, t, 1)
 
         @pl.when(c == y)
         def _():
@@ -1371,9 +1509,12 @@
         def _():
             wait(g(B_GO, t), S_GO, t, 1)
 
-        wait(g(B_GQ, t).at[pl.ds(0, 7)], S_GQ, t, 1)
+        for k in range(3):
+            wait(g(B_YQ, t).at[:, pl.ds(k * HALF, HALF)], S_YQ + k, t, 1)
+            wait(g(B_GQ, t).at[pl.ds(0, 3), :, pl.ds(k * HALF, HALF)], S_GQ + k, t, 1)
         wait(g(B_Y, t), S_FIN2, 0, t)
     wait(g(B_BGR, 0).at[pl.ds(0, 7)], S_BG, 0, 1)
+    wait(g(B_CF, 0).at[pl.ds(0, 3)], S_CF, 0, 1)
 
 
 def fused_call(*args):
@@ -1390,7 +1531,7 @@
         jax.ShapeDtypeStruct((2, 96, D), BF),
         jax.ShapeDtypeStruct((2, 96, 4 * D), BF),
         jax.ShapeDtypeStruct((2, HALF, D), BF),
-        jax.ShapeDtypeStruct((32, D), F32),
+        jax.ShapeDtypeStruct((16, HALF), F32),
     ]
     return pl.pallas_call(
         fused_kernel,
@@ -1410,7 +1551,6 @@
     wide = refs[29:33]
     through = refs[33:37]
     sem_in, sem_out, sem_move, sem_move_out = refs[37:]
-    s = lax.axis_index("shard")
     groups = list(zip((oq, ou, od, oo), low, wide, (r_q, r_u, r_d, r_o)))
     reads, writes, moves = [], [], []
     for k, (src, lo, hi, dst) in enumerate(groups):
@@ -1422,16 +1562,13 @@
                       pltpu.make_async_copy(through[k], dst, sem_move_out.at[k])))
         moves[-1][0].start()
     r_loss[...] = loss[0:1, 0:1]
-    first = pltpu.roll(bg[0:16, :], lax.rem(D - 96 * s, D), 1)[:, :96]
-    r_ob[...] = first[0:2, :]
-    r_db[...] = first[2:4, :]
+    r_ob[...] = bg[0:2, 0:96]
+    r_db[...] = bg[2:4, 0:96]
     for t in (0, 1):
-        r_gn[t] = first[4 + 2 * t:6 + 2 * t, :]
-        r_sf[t] = first[8 + 2 * t:10 + 2 * t, :]
-    second = pltpu.roll(bg[8:16, :], lax.rem(D - 192 * (s % 4), D), 1)[:, :192]
-    r_qb[...] = jnp.where(jnp.full((2, 192), s) < 4, second[4:6, :], second[6:8, :])
-    for t in (0, 1):
-        r_ub[t:t + 1, :] = bg[pl.ds(16 + 4 * t + s // 2, 1), pl.ds(mo((s % 2) * HALF, 128), HALF)]
+        r_gn[t] = bg[4 + 2 * t:6 + 2 * t, 0:96]
+        r_sf[t] = bg[8 + 2 * t:10 + 2 * t, 0:96]
+    r_qb[...] = bg[0:2, 128:320]
+    r_ub[...] = bg[12:14, :]
     for k, (src, lo, hi, dst) in enumerate(groups):
         for t in (0, 1):
             reads[2 * k + t].wait()

time: 272 us -> 236 us (0.87)
  Pallas kernels: 271 us -> 235 us
    pallas_call x1, Pallas kernels: 265 us -> 229 us  [fused_call(): pl.pallas_call(fused_kernel, out_shape=out_shape, in_specs=[hbm] * 8 + [v...]
where the time goes in v3:
time: 236 us; the launch traced here: 235 us
  Pallas kernels  235 us (100%)
    pallas_call x1, Pallas kernels, fused_call(): pl.pallas_call(fused_kernel, out_shape=out_shape, in_specs=[hbm] * 8 + [v...  229 us
    pallas_call x1, Pallas kernels, widen_call(): pl.pallas_call(widen_kernel, out_shape=[out(F32, 1, 1), out(BF, 128, D),...  5.9 us

profile of v3, /device:TPU:0, one launch (start us, length us, event | category | flops | bytes accessed | tf_op | source)
XLA Modules:
  0.0 235.4 jit_solution(829749023972461612)
XLA Ops:
  0.7 228.7 %shard_map.271 = (f32[8,128]{1,0:T(8,128)}, bf16[128,768]{1,0:T(8,128)(2,1)}, bf16[256,768]{1,0:T(8,128)(2,1)}, bf16[128,768]{1,0:T(8,128)(2,1)}, bf16[256,768]{...) custom-call(bf16[128,768]{1,0:T(8,128)(2,1)} %bitcast.13, ...), custom_call_target="tpu_custom_call" | custom-call | flops 17999998976 | bytes 40000000 | tf_op jit(solution)/shard_map/pallas_call | solution.py:1536
  229.3 5.9 %shard_map.272 = (f32[1,1]{1,0:T(1,128)}, bf16[128,768]{1,0:T(8,128)(2,1)}, bf16[256,768]{1,0:T(8,128)(2,1)}, bf16[128,768]{1,0:T(8,128)(2,1)}, bf16[256,768]{1,...) custom-call(f32[8,128]{1,0:T(8,128)} %get-tuple-element.40.refs_0_, ...), custom_call_target="tpu_custom_call" | custom-call | tf_op jit(solution)/shard_map/pallas_call | solution.py:1593

commit v4 on v3

--- a/solution.py
+++ b/solution.py
@@ -440,16 +440,12 @@
 D = 768
 HALF = 384
 FFN = 768
-PLAN = [(2, 0, 0),
-        (3, 1, 0), (4, 2, 1), (5, 3, 2), (6, 4, 3), (7, 5, 4), (7, 6, 5),
-        (8, 7, 6), (9, 8, 7), (10, 9, 8), (11, 10, 9), (12, 11, 10), (13, 12, 11),
-        (14, 13, 12),
-        (14, 14, 13), (15, 14, 14), (16, 15, 14), (17, 16, 15), (18, 17, 16), (19, 18, 17)]
+PLAN = [(2, 2, 0, 0), (2, 2, 1, 0), (2, 2, 1, 0), (3, 3, 2, 1), (4, 3, 2, 2), (6, 4, 2, 2), (6, 5, 3, 2), (10, 8, 5, 2), (10, 8, 7, 3), (10, 10, 9, 3), (13, 10, 10, 5), (14, 11, 10, 5), (15, 12, 10, 6), (15, 15, 13, 6), (18, 17, 15, 7), (20, 18, 16, 7), (21, 21, 18, 9), (21, 21, 18, 9), (22, 21, 18, 10), (23, 21, 18, 10), (23, 21, 20, 10)]
 NEIGH = tuple((dy, dx, dc) for dy in (0, 1) for dx in (0, 1) for dc in (0, 1) if dy + dx + dc)
 
 (S_X, S_QKV, S_QKV1, S_QKV2, S_QKVC, S_QKVZ, S_QKVZ1, S_QKVZ2, S_OUT, S_OUTC, S_OUTZ, S_UP, S_UP1, S_UPC, S_UPZ, S_UPZ1,
  S_DN, S_OP, S_MY, S_MC, S_MF, S_F1A, S_F1B, S_F2, S_DY, S_DC, S_DF, S_D1A, S_D1B, S_D2,
- S_DA, S_DX, S_GD, S_GD1, S_GD2, S_GU, S_GU1, S_GO, S_GQ, S_GQ1, S_GQ2, S_YQ, S_YQ1, S_YQ2, S_SMALL, S_CZ, S_CP, S_BG, S_COT, S_FIN, S_FIN2, S_CF, S_Z) = range(53)
+ S_DA, S_DX, S_GD, S_GD1, S_GD2, S_GU, S_GU1, S_XU, S_XU1, S_GO, S_GQ, S_GQ1, S_GQ2, S_YQ, S_YQ1, S_YQ2, S_SMALL, S_CZ, S_CP, S_CPC, S_CPF, S_BG, S_COT, S_FIN, S_FIN2, S_CF, S_Z) = range(57)
 N_UNITS = 23
 N_SEMS = 4 * S_Z + 6 * N_UNITS + 2
 
@@ -479,7 +475,7 @@
  B_KP, B_Y, B_DF, B_DA, B_GD, B_GU, B_GO, B_GQ, B_ZSD, B_ZSU, B_ZSO, B_ZSQ,
  B_ZAD, B_ZAU, B_ZAO, B_ZAQ, B_ZBD, B_ZBU, B_ZBO, B_ZBQ, B_CLN, B_CLR, B_CLC, B_CLS,
  B_CLD, B_CLP, B_CFW, B_CF, B_YQ, B_T96, B_SP, B_BGC, B_PV, B_BG, B_BGS, B_BGR,
- B_BGA, B_BGB, B_CM, B_GA, B_CG, B_DAT) = range(66)
+ B_BGA, B_BGB, B_CM, B_GA, B_CG, B_DAT, B_XU) = range(67)
 
 
 def scratch_list():
@@ -519,7 +515,8 @@
         add(B_DA, t, (2 * T, D), BF)
         add(B_DAT, t, (2 * T, HALF), BF)
         add(B_GD, t, (HALF, D), BF)
-        add(B_GU, t, (8, 96, FFN), BF)
+        add(B_GU, t, (4, 96, FFN), BF)
+        add(B_XU, t, (HALF, FFN), BF)
         add(B_GO, t, (4, 96, D), BF)
         add(B_GQ, t, (4, 96, 3 * HALF), BF)
         add(B_YQ, t, (HALF, 3 * HALF), BF)
@@ -1021,14 +1018,15 @@
             da = nt(g(B_DF, t)[rows, :], g(B_WD, t)[cols, :])
             g(B_SL, t)[rows, cols] = (da * g(B_SL, t)[rows, cols].astype(F32)).astype(BF)
 
-    def pre_back(t):
+    def pre_back(t, between=lambda: None):
         gather_near(t, B_DF, S_DC)
+        down_pair(t, y)
+        between()
         gather_forward(t, B_DF, S_DY, S_DF)
-        down_pair(t, y)
         gather_far(t, B_DF, S_DF)
         down_pair(t, 1 - y)
 
-    def ffn_back(t):
+    def ffn_back(t, point=lambda: None):
         gather_sent(t, B_DF, S_DY, S_DC, S_DF)
         cls_place(t)
         ACT, DF, WD, WU = g(B_ACT, t), g(B_DF, t), g(B_WD, t), g(B_WU, t)
@@ -1036,8 +1034,10 @@
             cols = pl.ds(mo((1 - x) * HALF + 128 * k, 128), 128)
             WD[cols, :] = tn(ACT[:, cols], DF[...]).astype(BF)
             send(WD.at[cols], g(B_GD, t).at[pl.ds(128 * k, 128)], S_GD + k, t, xpeer)
+        point()
 
         scatter_partial(t, lambda rows: nt(g(B_SL, t)[rows, :], g(B_WU, t)[...]), S_D1A, S_D1B, S_D2)
+        point()
         own_sum = nn(jnp.ones((8, ROWS[t]), F32).astype(BF), g(B_DF, t)[slot_rows(t, y, c), :])
         put_bias(R_DB + t, own_sum[0:1, :])
         ones = jnp.ones((8, 4 * ROWS[t]), F32).astype(BF)
@@ -1057,16 +1057,31 @@
         cols = pl.ds(mo(x * HALF, 128), HALF)
         WD[cols, :] = tn(ACT[:, cols], DF[...]).astype(BF)
         for dy in (1, 0):
+            far, near = (pl.ds(mo(flip(y, dy) * HALF + xx * 192, 64), 192) for xx in (1 - x, x))
+
             @pl.loop(0, 3)
             def _(j):
                 cols = pl.ds(mo(flip(y, dy) * HALF + j * 128, 128), 128)
                 WU[cols, :] = tn(g(B_MID, t)[:, cols], g(B_SL, t)[...]).astype(BF)
 
-            for d in NEIGH:
-                if d[0] == dy:
-                    dest = sh(*peer(d))
-                    send(WU.at[pl.ds(mo(96 * dest, 32), 96)], g(B_GU, t).at[s], S_GU1 - dy, t, (rep, dest))
-        local(WU.at[rows96], g(B_GU, t).at[s], S_GU1, t)
+            send(WU.at[far], g(B_XU, t).at[pl.ds((1 - dy) * 192, 192)], S_XU1 - dy, t, xpeer)
+            point()
+
+    def relay_up(t, dy):
+        WU, GU, mine = g(B_WU, t), g(B_GU, t), 2 * y + c
+        got = g(B_XU, t).at[pl.ds((1 - dy) * 192, 192)]
+        wait(got, S_XU1 - dy, t)
+        yy = flip(y, dy)
+        for r0 in (0, 96):
+            r = pl.ds(mo(yy * HALF + x * 192 + r0, 32), 96)
+            WU[r, :] = (WU[r, :].astype(F32) + got[pl.ds(r0, 96), :].astype(F32)).astype(BF)
+        for dc in (1, 0):
+            owner = sh(yy, x, flip(c, dc))
+            rows = WU.at[pl.ds(mo(96 * owner, 32), 96)]
+            if dy + dc:
+                send(rows, GU.at[mine], S_GU1 - dy, t, (rep, owner))
+            else:
+                local(rows, GU.at[mine], S_GU1, t)
 
     g(B_BG, 0)[...] = jnp.zeros((32, D), F32)
     g(B_CFW, 0)[...] = jnp.zeros((16, D), F32)
@@ -1097,8 +1112,10 @@
     out_back(0)
     wait(g(B_GA, 0).at[pl.ds(0, 3)], S_CZ, 0)
     four = g(B_GA, 0).at[pl.ds(s * 4, 4)]
+    send(four, four, S_CPC, 0, sib)
     for d in NEIGH:
-        send(four, four, S_CP, 0, (rep, sh(*peer(d))))
+        if not d[2]:
+            send(four, four, S_CP, 0, (rep, sh(*peer(d))))
     gather_rows(0, B_DF, S_DY, S_DC, S_DF)
 
     for t in (0, 1):
@@ -1126,10 +1143,21 @@
         scatter_sent(t, S_F1A, S_F1B, S_F2)
     wait(g(B_SP, 0).at[pl.ds(0, 7)], S_SMALL, 0, 1)
     wait(g(B_GA, 0).at[pl.ds(0, 3)], S_CZ, 0, 1)
-    pre_back(1)
-
-    wait(g(B_GA, 0).at[pl.ds(0, 28)], S_CP, 0)
-    wait(g(B_GA, 0).at[pl.ds(0, 28)], S_CP, 0, 1)
+    def pass_cls():
+        twelve = g(B_GA, 0).at[pl.ds(0, 12)]
+        wait(twelve, S_CP, 0)
+        for d in NEIGH:
+            if not d[2]:
+                got = g(B_GA, 0).at[pl.ds(sh(*peer(d)) * 4, 4)]
+                send(got, got, S_CPF, 0, sib)
+
+    pre_back(1, pass_cls)
+
+    wait(g(B_GA, 0).at[pl.ds(0, 4)], S_CPC, 0)
+    wait(g(B_GA, 0).at[pl.ds(0, 12)], S_CPF, 0)
+    wait(g(B_GA, 0).at[pl.ds(0, 4)], S_CPC, 0, 1)
+    for name in (S_CP, S_CPF):
+        wait(g(B_GA, 0).at[pl.ds(0, 12)], name, 0, 1)
 
     def pick_all(base):
         ri = lax.broadcasted_iota(jnp.int32, (128, 512), 0)
@@ -1325,11 +1353,10 @@
 
         def each(use):
             if xx == 0:
-                wait(GU.at[pl.ds(0, 4)], S_GU1 - dy, t)
+                wait(GU.at[pl.ds(0, 2)], S_GU1 - dy, t)
             cols = slice(xx * HALF, (xx + 1) * HALF)
             for cc in (0, 1):
-                both = GU[sh(yy, 0, cc), :, cols].astype(F32) + GU[sh(yy, 1, cc), :, cols].astype(F32)
-                use(pl.ds(0, 96), pl.ds(mo((4 * yy + 2 * xx + cc) * HALF, 128), HALF), both)
+                use(pl.ds(0, 96), pl.ds(mo((4 * yy + 2 * xx + cc) * HALF, 128), HALF), GU[2 * yy + cc, :, cols].astype(F32))
         return each
 
     def make_out(t):
@@ -1372,9 +1399,10 @@
             bufs = (B_ZSD + kind, B_ZAD + kind, B_ZBD + kind)
         units.append((len(units), tuple(g(b, t) for b in bufs), each, out, rows, cols))
 
-    def add_ffn(t):
+    def add_dn(t):
         for k in range(3):
             unit(0, t, make_dn(t, k), o_od.at[t], (128 * k, 128), (0, D))
+    def add_up(t):
         for dy in (1, 0):
             for xx in (0, 1):
                 at = mo((2 * flip(y, dy) + xx) * D, 128)
@@ -1384,9 +1412,11 @@
         for part in range(3):
             unit(3, t, make_qkv(t, part), o_oq.at[t], (0, 96), (part * D, D))
 
-    add_ffn(1)
-    add_ffn(0)
+    add_dn(1)
+    add_up(1)
+    add_dn(0)
     unit(2, 1, make_out(1), o_oo.at[1], (0, 96), (0, D))
+    add_up(0)
     unit(2, 0, make_out(0), o_oo.at[0], (0, 96), (0, D))
     add_qkv(1)
     unit(4, 0, each_small, o_obg, (0, 16), (0, HALF))
@@ -1447,6 +1477,16 @@
                     step(units[done[k]])
                     done[k] += 1
 
+    relays = [functools.partial(relay_up, t, dy) for t in (1, 0) for dy in (1, 0)]
+    relays += [functools.partial(relay_qkv, t, k) for t in (1, 0) for k in range(3)]
+
+    def point():
+        *steps, through = plan.pop(0)
+        while len(relays) > 10 - through:
+            relays.pop(0)()
+        advance(*steps)
+
+    plan = PLAN[:]
     cls_back(1)
     cls_back(0)
     mine = g(B_CF, 0).at[2 * y + c]
@@ -1459,25 +1499,17 @@
     for t in (0, 1):
         wait(g(B_Y, t), S_FIN, 0, t)
     ffn_back(1)
-    ffn_back(0)
-    def point():
-        advance(*plan.pop(0))
-
-    plan = PLAN[:]
-    point()
+    ffn_back(0, point)
     mid_back(1)
     attention_back(1, point)
     mid_back(0)
     attention_back(0, point)
     input_back(1)
     input_back(0)
-    point()
-    for t in (1, 0):
-        for k in range(3):
-            relay_qkv(t, k)
-            point()
+    while plan:
+        point()
     for k in range(done[0], N_UNITS + 1):
-        advance(min(k + 1, N_UNITS), k, k - 1)
+        advance(min(k + 1, N_UNITS), k, k - 2)
     advance(N_UNITS, N_UNITS, N_UNITS)
 
     for u in units:
@@ -1498,8 +1530,10 @@
         wait(g(B_OS, t), S_DX, t, 1)
         for k in range(3):
             wait(g(B_GD, t).at[pl.ds(0, 128)], S_GD + k, t, 1)
-        wait(g(B_GU, t).at[pl.ds(0, 4)], S_GU, t, 1)
-        wait(g(B_GU, t).at[pl.ds(0, 3)], S_GU1, t, 1)
+        wait(g(B_GU, t).at[pl.ds(0, 2)], S_GU, t, 1)
+        wait(g(B_GU, t).at[pl.ds(0, 1)], S_GU1, t, 1)
+        for dy in (0, 1):
+            wait(g(B_XU, t).at[pl.ds(0, 192)], S_XU1 - dy, t, 1)
 
         @pl.when(c == y)
         def _():

time: 236 us -> 227 us (0.962)
  Pallas kernels: 235 us -> 226 us
    pallas_call x1, Pallas kernels: 229 us -> 220 us  [fused_call(): pl.pallas_call(fused_kernel, out_shape=out_shape, in_specs=[hbm] * 8 + [v...]
where the time goes in v4:
time: 227 us
  Pallas kernels  226 us (100%)
    pallas_call x1, Pallas kernels, fused_call(): pl.pallas_call(fused_kernel, out_shape=out_shape, in_specs=[hbm] * 8 + [v...  220 us
    pallas_call x1, Pallas kernels, widen_call(): pl.pallas_call(widen_kernel, out_shape=[out(F32, 1, 1), out(BF, 128, D),...  5.9 us

profile of v4, /device:TPU:0, one launch (start us, length us, event | category | flops | bytes accessed | tf_op | source)
XLA Modules:
  0.0 227.2 jit_solution(6709990554783187930)
XLA Ops:
  0.7 220.5 %shard_map.271 = (f32[8,128]{1,0:T(8,128)}, bf16[128,768]{1,0:T(8,128)(2,1)}, bf16[256,768]{1,0:T(8,128)(2,1)}, bf16[128,768]{1,0:T(8,128)(2,1)}, bf16[256,768]{...) custom-call(bf16[128,768]{1,0:T(8,128)(2,1)} %bitcast.13, ...), custom_call_target="tpu_custom_call" | custom-call | flops 17999998976 | bytes 40000000 | tf_op jit(solution)/shard_map/pallas_call | solution.py:1570
  221.1 5.9 %shard_map.272 = (f32[1,1]{1,0:T(1,128)}, bf16[128,768]{1,0:T(8,128)(2,1)}, bf16[256,768]{1,0:T(8,128)(2,1)}, bf16[128,768]{1,0:T(8,128)(2,1)}, bf16[256,768]{1,...) custom-call(f32[8,128]{1,0:T(8,128)} %get-tuple-element.40.refs_0_, ...), custom_call_target="tpu_custom_call" | custom-call | tf_op jit(solution)/shard_map/pallas_call | solution.py:1627

commit v5 on v4

--- a/solution.py
+++ b/solution.py
@@ -895,13 +895,13 @@
         up_pair(t, y)
         gather_far(t, B_MID, S_MF)
         up_pair(t, 1 - y)
+        wait(g(B_WD, t), S_DN, t)
+        scatter_partial(t, lambda rows: nn(g(B_ACT, t)[rows, :], g(B_WD, t)[...]), S_F1A, S_F1B, S_F2)
         T = ROWS[t]
         r = lax.broadcasted_iota(jnp.int32, (16, 4 * T), 0)
         j = lax.broadcasted_iota(jnp.int32, (16, 4 * T), 1)
         at_cls = (j == (r >> 2) * T + (r & 3) * (32, 64)[t]).astype(F32).astype(BF)
         g(B_CLS, t)[...] = nn(at_cls, g(B_SL, t)[...]).astype(BF)
-        wait(g(B_WD, t), S_DN, t)
-        scatter_partial(t, lambda rows: nn(g(B_ACT, t)[rows, :], g(B_WD, t)[...]), S_F1A, S_F1B, S_F2)
 
     def ffn_end(t):
         T = ROWS[t]
@@ -933,9 +933,9 @@
     for k in range(3):
         project(1, k)
         forward_qkv(0, k)
-    attention(1)
     send_up(0)
     send_dn(0)
+    attention(1)
     forward_out(0)
     forward_up(1)
     for k in range(3):
@@ -992,7 +992,6 @@
             put_bias(k, g(B_BG, 0)[k:k + 1, :] + jnp.sum(a, axis=0, keepdims=True))
 
     def cls_place(t):
-        T = ROWS[t]
         r = lax.broadcasted_iota(jnp.int32, (16, 64), 0)
         j = lax.broadcasted_iota(jnp.int32, (16, 64), 1)
         which = (j == (r >> 2) * 16 + 4 * t + (r & 3)).astype(F32).astype(BF)
@@ -1000,13 +999,13 @@
         g(B_CLD, t)[...] = rows
         da = nt(rows.astype(BF), g(B_WD, t)[...])
         g(B_CLP, t)[...] = da * g(B_CLS, t)[...].astype(F32)
+        cls_rows(t, g(B_DF, t), g(B_CLD, t))
+
+    def cls_rows(t, buf, new):
         top = lax.broadcasted_iota(jnp.int32, (16, 1), 0) == 0
-        for slot in range(4):
-            for i in range(4):
-                tile = pl.ds(slot * T + i * steps[t], 16)
-                k = slot * 4 + i
-                for buf, new in ((g(B_DF, t), g(B_CLD, t)), (g(B_SL, t), g(B_CLP, t))):
-                    buf[tile, :] = jnp.where(top, new[k:k + 1, :], buf[tile, :].astype(F32)).astype(BF)
+        for k in range(16):
+            tile = pl.ds(k // 4 * ROWS[t] + k % 4 * steps[t], 16)
+            buf[tile, :] = jnp.where(top, new[k:k + 1, :], buf[tile, :].astype(F32)).astype(BF)
 
     def down_pair(t, yy):
         T = ROWS[t]
@@ -1034,6 +1033,7 @@
             cols = pl.ds(mo((1 - x) * HALF + 128 * k, 128), 128)
             WD[cols, :] = tn(ACT[:, cols], DF[...]).astype(BF)
             send(WD.at[cols], g(B_GD, t).at[pl.ds(128 * k, 128)], S_GD + k, t, xpeer)
+        cls_rows(t, g(B_SL, t), g(B_CLP, t))
         point()
 
         scatter_partial(t, lambda rows: nt(g(B_SL, t)[rows, :], g(B_WU, t)[...]), S_D1A, S_D1B, S_D2)

time: 227 us -> 227 us (level)
  no operation moved by 1% of the time
where the time goes in v5:
time: 227 us
  Pallas kernels  226 us (100%)
    pallas_call x1, Pallas kernels, fused_call(): pl.pallas_call(fused_kernel, out_shape=out_shape, in_specs=[hbm] * 8 + [v...  220 us
    pallas_call x1, Pallas kernels, widen_call(): pl.pallas_call(widen_kernel, out_shape=[out(F32, 1, 1), out(BF, 128, D),...  5.9 us

profile of v5, /device:TPU:0, one launch (start us, length us, event | category | flops | bytes accessed | tf_op | source)
XLA Modules:
  0.0 226.7 jit_solution(4344281394206691638)
XLA Ops:
  0.7 220.0 %shard_map.271 = (f32[8,128]{1,0:T(8,128)}, bf16[128,768]{1,0:T(8,128)(2,1)}, bf16[256,768]{1,0:T(8,128)(2,1)}, bf16[128,768]{1,0:T(8,128)(2,1)}, bf16[256,768]{...) custom-call(bf16[128,768]{1,0:T(8,128)(2,1)} %bitcast.13, ...), custom_call_target="tpu_custom_call" | custom-call | flops 17999998976 | bytes 40000000 | tf_op jit(solution)/shard_map/pallas_call | solution.py:1570
  220.7 5.9 %shard_map.272 = (f32[1,1]{1,0:T(1,128)}, bf16[128,768]{1,0:T(8,128)(2,1)}, bf16[256,768]{1,0:T(8,128)(2,1)}, bf16[128,768]{1,0:T(8,128)(2,1)}, bf16[256,768]{1,...) custom-call(f32[8,128]{1,0:T(8,128)} %get-tuple-element.40.refs_0_, ...), custom_call_target="tpu_custom_call" | custom-call | tf_op jit(solution)/shard_map/pallas_call | solution.py:1627

commit v6 on v5

--- a/solution.py
+++ b/solution.py
@@ -441,7 +441,7 @@
 HALF = 384
 FFN = 768
 PLAN = [(2, 2, 0, 0), (2, 2, 1, 0), (2, 2, 1, 0), (3, 3, 2, 1), (4, 3, 2, 2), (6, 4, 2, 2), (6, 5, 3, 2), (10, 8, 5, 2), (10, 8, 7, 3), (10, 10, 9, 3), (13, 10, 10, 5), (14, 11, 10, 5), (15, 12, 10, 6), (15, 15, 13, 6), (18, 17, 15, 7), (20, 18, 16, 7), (21, 21, 18, 9), (21, 21, 18, 9), (22, 21, 18, 10), (23, 21, 18, 10), (23, 21, 20, 10)]
-NEIGH = tuple((dy, dx, dc) for dy in (0, 1) for dx in (0, 1) for dc in (0, 1) if dy + dx + dc)
+NEIGH = tuple((dy, dx, dc) for dy in (1, 0) for dx in (1, 0) for dc in (1, 0) if dy + dx + dc)
 
 (S_X, S_QKV, S_QKV1, S_QKV2, S_QKVC, S_QKVZ, S_QKVZ1, S_QKVZ2, S_OUT, S_OUTC, S_OUTZ, S_UP, S_UP1, S_UPC, S_UPZ, S_UPZ1,
  S_DN, S_OP, S_MY, S_MC, S_MF, S_F1A, S_F1B, S_F2, S_DY, S_DC, S_DF, S_D1A, S_D1B, S_D2,

time: 227 us -> 226 us (level)
  no operation moved by 1% of the time
where the time goes in v6:
time: 226 us
  Pallas kernels  225 us (100%)
    pallas_call x1, Pallas kernels, fused_call(): pl.pallas_call(fused_kernel, out_shape=out_shape, in_specs=[hbm] * 8 + [v...  219 us
    pallas_call x1, Pallas kernels, widen_call(): pl.pallas_call(widen_kernel, out_shape=[out(F32, 1, 1), out(BF, 128, D),...  5.9 us

profile of v6, /device:TPU:0, one launch (start us, length us, event | category | flops | bytes accessed | tf_op | source)
XLA Modules:
  0.0 226.1 jit_solution(17202828576914245058)
XLA Ops:
  0.7 219.3 %shard_map.271 = (f32[8,128]{1,0:T(8,128)}, bf16[128,768]{1,0:T(8,128)(2,1)}, bf16[256,768]{1,0:T(8,128)(2,1)}, bf16[128,768]{1,0:T(8,128)(2,1)}, bf16[256,768]{...) custom-call(bf16[128,768]{1,0:T(8,128)(2,1)} %bitcast.13, ...), custom_call_target="tpu_custom_call" | custom-call | flops 17999998976 | bytes 40000000 | tf_op jit(solution)/shard_map/pallas_call | solution.py:1570
  220.0 5.9 %shard_map.272 = (f32[1,1]{1,0:T(1,128)}, bf16[128,768]{1,0:T(8,128)(2,1)}, bf16[256,768]{1,0:T(8,128)(2,1)}, bf16[128,768]{1,0:T(8,128)(2,1)}, bf16[256,768]{1,...) custom-call(f32[8,128]{1,0:T(8,128)} %get-tuple-element.40.refs_0_, ...), custom_call_target="tpu_custom_call" | custom-call | tf_op jit(solution)/shard_map/pallas_call | solution.py:1627
